TPU v7x, 768 devices: a whole 4x8x12 slice. The times are simulated.
768 devices in a mesh: gx: 12 (over z_lo, core), gy: 64 (over y, z_hi, x).
Axes of the slice: x: 4, y: 8, z: 12 (z_hi: 2, z_lo: 6; z = z_hi * 6 + z_lo), core: 2. Of those that a mesh axis runs over, the one named last changes fastest.
Arguments:
- fluid_state: float32 [6, 3, 192, 8192], P(None, None, 'gx', 'gy'), may hold values from -1.875 to 10.7, as said below
- switch: int32 [3, 192, 8192], P(None, 'gx', 'gy'), may hold values 0 or 1
- z_edges: float32 [2, 6, 3, 192, 8192], P(None, None, None, 'gx', 'gy'), may hold values from -1.875 to 10.7, as said below
- forcing: float32 [3, 3, 192, 8192], P(None, None, 'gx', 'gy'), may hold values from -3 to 3
Outputs:
- updated: float32 [6, 3, 192, 8192], P(None, None, 'gx', 'gy')
Inputs may be any that keep to these rules, and one draw needn't show every extreme that they name: `fluid_state`: density lies in 0.7 to 1.4; total energy minus kinetic energy lies in 1 to 3 in every cell, and so does the internal-energy field. `z_edges`: the same law as the window state.
All inputs are finite; a program needn't handle non-finite values. No bound on the sum of `switch` on one device may be relied on, other than what follows from the above.
Results may differ from a plain program's by a relative error of at most 0.0003.
Values sent between devices are 32-bit elements; how exact they have to be, the bound alone decides.
No kernel may reach another device: no remote copies, remote signals or barrier semaphores. Data moves between devices by JAX's collectives and lax.ppermute only.
A program may use at most 32 MiB of HBM per device.

v0:
```python
import jax
import jax.numpy as jnp
from jax import lax
from jax.sharding import PartitionSpec as P

ADIABATIC = 5.0 / 3.0
CFL_NUMBER = 0.4
INJECTION = 0.04


def padded_2(block, sides, width):
    for axis, dim in sides:
        count = lax.axis_size(axis)
        forward = [(i, i + 1) for i in range(count - 1)]
        forward.append((count - 1, 0))
        backward = [(target, source) for source, target in forward]
        low = lax.ppermute(
            lax.slice_in_dim(block, block.shape[dim] - width, None, axis=dim), axis, forward
        )
        high = lax.ppermute(lax.slice_in_dim(block, 0, width, axis=dim), axis, backward)
        block = jnp.concatenate([low, block, high], axis=dim)
    return block


def kinetic(conserved):
    return 0.5 * (conserved[1] ** 2 + conserved[2] ** 2 + conserved[3] ** 2) / conserved[0]


def thermal(conserved, switch):
    return jnp.where(switch == 1, conserved[5], conserved[4] - kinetic(conserved))


def primitives(conserved, heat_field):
    density = conserved[0]
    return jnp.stack(
        [
            density,
            conserved[1] / density,
            conserved[2] / density,
            conserved[3] / density,
            (ADIABATIC - 1.0) * heat_field,
            conserved[5] / density,
        ]
    )


def signal_speed(conserved, heat_field):
    density = conserved[0]
    sound_speed = jnp.sqrt(ADIABATIC * (ADIABATIC - 1.0) * heat_field / density)
    return (
        jnp.abs(conserved[1] / density)
        + jnp.abs(conserved[2] / density)
        + jnp.abs(conserved[3] / density)
        + 3.0 * sound_speed
    )


def slab_of(values, begin, length, axis_dim):
    return lax.slice_in_dim(values, begin, begin + length, axis=axis_dim)


def edge_states(values, axis_dim):
    cell_count = values.shape[axis_dim] - 6
    face_value = (
        7.0
        * (
            slab_of(values, 1, cell_count + 3, axis_dim)
            + slab_of(values, 2, cell_count + 3, axis_dim)
        )
        - (
            slab_of(values, 0, cell_count + 3, axis_dim)
            + slab_of(values, 3, cell_count + 3, axis_dim)
        )
    ) / 12.0
    bound_low = jnp.minimum(
        slab_of(values, 1, cell_count + 3, axis_dim), slab_of(values, 2, cell_count + 3, axis_dim)
    )
    bound_high = jnp.maximum(
        slab_of(values, 1, cell_count + 3, axis_dim), slab_of(values, 2, cell_count + 3, axis_dim)
    )
    face_value = jnp.minimum(jnp.maximum(face_value, bound_low), bound_high)
    center = slab_of(values, 2, cell_count + 2, axis_dim)
    below_dev = slab_of(face_value, 0, cell_count + 2, axis_dim) - center
    above_dev = slab_of(face_value, 1, cell_count + 2, axis_dim) - center
    opposite = below_dev * above_dev < 0.0
    left_dev = jnp.where(
        opposite, jnp.clip(below_dev, -2.0 * jnp.abs(above_dev), 2.0 * jnp.abs(above_dev)), 0.0
    )
    right_dev = jnp.where(
        opposite, jnp.clip(above_dev, -2.0 * jnp.abs(below_dev), 2.0 * jnp.abs(below_dev)), 0.0
    )
    left_edge = center + left_dev
    right_edge = center + right_dev
    return (
        slab_of(right_edge, 0, cell_count + 1, axis_dim),
        slab_of(left_edge, 1, cell_count + 1, axis_dim),
    )


def physical(primitive, normal):
    density = primitive[0]
    pressure = primitive[4]
    normal_speed = primitive[1 + normal]
    energy = pressure / (ADIABATIC - 1.0) + 0.5 * density * (
        primitive[1] ** 2 + primitive[2] ** 2 + primitive[3] ** 2
    )
    conserved = jnp.stack(
        [
            density,
            density * primitive[1],
            density * primitive[2],
            density * primitive[3],
            energy,
            density * primitive[5],
        ]
    )
    flux_value = conserved * normal_speed
    flux_value = flux_value.at[1 + normal].add(pressure)
    flux_value = flux_value.at[4].add(pressure * normal_speed)
    sound_speed = jnp.sqrt(ADIABATIC * pressure / density)
    return (conserved, flux_value, normal_speed, sound_speed)


def riemann_flux(left_state, right_state, normal):
    left_cons, left_flux, left_speed, left_sound = physical(left_state, normal)
    right_cons, right_flux, right_speed, right_sound = physical(right_state, normal)
    speed_low = jnp.minimum(jnp.minimum(left_speed - left_sound, right_speed - right_sound), 0.0)
    speed_high = jnp.maximum(jnp.maximum(left_speed + left_sound, right_speed + right_sound), 0.0)
    return (
        speed_high * left_flux
        - speed_low * right_flux
        + speed_low * speed_high * (right_cons - left_cons)
    ) / (speed_high - speed_low)


def directional(primitive, axis_dim, normal):
    left_state, right_state = edge_states(primitive, axis_dim)
    flux_value = riemann_flux(left_state, right_state, normal)
    cell_count = primitive.shape[axis_dim] - 6
    difference = slab_of(flux_value, 1, cell_count, axis_dim) - slab_of(
        flux_value, 0, cell_count, axis_dim
    )
    velocity = primitive[1 + normal]
    spread = 0.5 * (
        slab_of(velocity, 4, cell_count, axis_dim - 1)
        - slab_of(velocity, 2, cell_count, axis_dim - 1)
    )
    return (difference, spread)


def tendency(cons_pad, heat_pad, edge_below, edge_above, forcing, force_scale):
    row_strip = primitives(cons_pad[:, :, :, 3:-3], heat_pad[:, :, 3:-3])
    core_prim = row_strip[:, :, 3:-3, :]
    rim_low = primitives(cons_pad[:, :, 3:-3, :3], heat_pad[:, 3:-3, :3])
    rim_high = primitives(cons_pad[:, :, 3:-3, -3:], heat_pad[:, 3:-3, -3:])
    column_strip = jnp.concatenate([rim_low, core_prim, rim_high], axis=3)
    lower_prim = primitives(edge_below, edge_below[4] - kinetic(edge_below))
    upper_prim = primitives(edge_above, edge_above[4] - kinetic(edge_above))
    z_column = jnp.concatenate([lower_prim, core_prim, upper_prim], axis=1)
    flux_rows, spread_rows = directional(row_strip, 2, 0)
    flux_cols, spread_cols = directional(column_strip, 3, 1)
    flux_planes, spread_planes = directional(z_column, 1, 2)
    conserved = cons_pad[:, :, 3:-3, 3:-3]
    density = conserved[0]
    divergence = spread_rows + spread_cols + spread_planes
    momentum_push = force_scale * density * forcing
    power_term = force_scale * (
        conserved[1] * forcing[0] + conserved[2] * forcing[1] + conserved[3] * forcing[2]
    )
    blank_field = jnp.zeros_like(density)
    source = jnp.stack(
        [
            blank_field,
            momentum_push[0],
            momentum_push[1],
            momentum_push[2],
            power_term,
            -core_prim[4] * divergence,
        ]
    )
    return source - (flux_rows + flux_cols + flux_planes)


def settle(conserved, switch):
    return conserved.at[5].set(
        jnp.where(switch == 0, conserved[4] - kinetic(conserved), conserved[5])
    )


def rimmed_tendency(conserved, heat_field, edge_below, edge_above, forcing, force_scale):
    packed = jnp.concatenate([conserved, heat_field[None]], axis=0)
    padded = padded_2(packed, (("gx", 2), ("gy", 3)), 3)
    return tendency(padded[:6], padded[6], edge_below, edge_above, forcing, force_scale)


def local(fluid_state, switch, z_edges, forcing):
    row_count = fluid_state.shape[2]
    col_count = fluid_state.shape[3]
    devices = lax.axis_size("gx") * lax.axis_size("gy")
    heat_field = thermal(fluid_state, switch)
    local_peak = jnp.max(signal_speed(fluid_state, heat_field))
    local_total = jnp.sum(fluid_state[0] * (forcing[0] ** 2 + forcing[1] ** 2 + forcing[2] ** 2))
    peak_speed = lax.pmax(local_peak, ("gx", "gy"))
    power_total = lax.psum(local_total, ("gx", "gy"))
    time_step = CFL_NUMBER / peak_speed
    force_scale = jnp.sqrt(
        INJECTION
        / (0.5 * time_step * (power_total / (3.0 * row_count * col_count * devices) + 1e-06))
    )
    edge_below = z_edges[0]
    edge_above = z_edges[1]
    section_one = settle(
        fluid_state
        + time_step
        * rimmed_tendency(fluid_state, heat_field, edge_below, edge_above, forcing, force_scale),
        switch,
    )
    section_two = rimmed_tendency(
        section_one, thermal(section_one, switch), edge_below, edge_above, forcing, force_scale
    )
    return settle(0.5 * fluid_state + 0.5 * (section_one + time_step * section_two), switch)


def solution(mesh):
    return jax.shard_map(
        local,
        mesh=mesh,
        in_specs=(
            P(None, None, "gx", "gy"),
            P(None, "gx", "gy"),
            P(None, None, None, "gx", "gy"),
            P(None, None, "gx", "gy"),
        ),
        out_specs=P(None, None, "gx", "gy"),
        check_vma=False,
    )
```

profile of v0, /device:TPU:31, one launch (start us, length us, event | category | flops | bytes accessed | tf_op | source)
XLA Modules:
  0.0 322.9 jit_solution(6428958523645822192)
XLA Ops:
  0.0 1.6 fusion.115
  1.6 4.6 %collective-permute-start = (f32[7,3,3,128]{3,0,2,1:T(8,128)S(1)}, f32[7,3,3,128]{3,0,2,1:T(8,128)S(1)}, u32[]{:S(2)}, u32[]{:S(2)}) collective-permute-start(f32[7,3,3,128]{3,0,2,1:T(8,128)S(1)} %copy.216), channel_id=1, source_target_pairs={{0,64},{64,128},{128,192},{192,256},{256,320},{320,384},{384,448},... | collective-permute-start | bytes 96776 | tf_op jit(solution)/shard_map/ppermute | solution.py:17
  6.2 1.9 collective-permute-start.1
  8.3 114.3 %pmax.7 = f32[]{:T(128)} all-reduce(f32[]{:T(128)} %get-tuple-element.318), channel_id=1, replica_groups=mesh['gx'=12,'gy'=64] {'gx','gy'}, use_global_device_ids=true, to_apply=%region_1.2 | all-reduce | flops 1 | bytes 8 | tf_op jit(solution)/shard_map/pmax | solution.py:203
  122.6 107.5 %psum.7 = f32[]{:T(128)} all-reduce(f32[]{:T(128)} %get-tuple-element.317), channel_id=1, replica_groups=mesh['gx'=12,'gy'=64] {'gx','gy'}, use_global_device_ids=true, to_apply=%region_3.4 | all-reduce | flops 1 | bytes 8 | tf_op jit(solution)/shard_map/psum | solution.py:204
  231.8 1.9 collective-permute-start.3
  233.7 11.8 %collective-permute-start.2 = (f32[7,3,22,3]{3,2,1,0:T(8,128)S(1)}, f32[7,3,22,3]{3,2,1,0:T(8,128)S(1)}, u32[]{:S(2)}, u32[]{:S(2)}) collective-permute-start(f32[7,3,22,3]{3,2,1,0:T(8,128)S(1)} %get-tuple-element.377), channel_id=1, source_target_pairs={{0,1},{1,2},{2,3},{3,4},{4,5},{5,6},{6,7},{7,8},{8,9},{9,10},{10,1... | collective-permute-start | bytes 16640 | tf_op jit(solution)/shard_map/ppermute | solution.py:17
  245.6 8.6 %collective-permute-done.3 = f32[7,3,22,3]{3,2,1,0:T(8,128)S(1)} collective-permute-done((f32[7,3,22,3]{3,2,1,0:T(8,128)S(1)}, f32[7,3,22,3]{3,2,1,0:T(8,128)S(1)}, u32[]{:S(2)}, u32[]{:S(2)}) %collective-permute-start.3) | collective-permute-done | bytes 5576 | tf_op jit(solution)/shard_map/ppermute | solution.py:20
  254.2 1.7 collective-permute-done.2
  257.4 0.3 fusion.13
  257.7 0.2 select_add_fusion.3
  260.2 0.6 copy-done.4
  260.9 8.7 %collective-permute-start.4 = (f32[7,3,3,128]{3,0,2,1:T(8,128)S(1)}, f32[7,3,3,128]{3,0,2,1:T(8,128)S(1)}, u32[]{:S(2)}, u32[]{:S(2)}) collective-permute-start(f32[7,3,3,128]{3,0,2,1:T(8,128)S(1)} %copy.218), channel_id=1, source_target_pairs={{0,64},{64,128},{128,192},{192,256},{256,320},{320,384},{384,448},... | collective-permute-start | bytes 96776 | tf_op jit(solution)/shard_map/ppermute | solution.py:17
  269.6 1.9 collective-permute-start.5
  271.5 3.3 %collective-permute-done.5 = f32[7,3,3,128]{3,0,2,1:T(8,128)S(1)} collective-permute-done((f32[7,3,3,128]{3,0,2,1:T(8,128)S(1)}, f32[7,3,3,128]{3,0,2,1:T(8,128)S(1)}, u32[]{:S(2)}, u32[]{:S(2)}) %collective-permute-start.5) | collective-permute-done | bytes 32288 | tf_op jit(solution)/shard_map/ppermute | solution.py:20
  275.1 13.3 %collective-permute-start.6 = (f32[7,3,22,3]{3,2,1,0:T(8,128)S(1)}, f32[7,3,22,3]{3,2,1,0:T(8,128)S(1)}, u32[]{:S(2)}, u32[]{:S(2)}) collective-permute-start(f32[7,3,22,3]{3,2,1,0:T(8,128)S(1)} %get-tuple-element.373), channel_id=1, source_target_pairs={{0,1},{1,2},{2,3},{3,4},{4,5},{5,6},{6,7},{7,8},{8,9},{9,10},{10,1... | collective-permute-start | bytes 16640 | tf_op jit(solution)/shard_map/ppermute | solution.py:17
  288.3 1.9 collective-permute-start.7
  290.3 2.6 collective-permute-done.6
  292.9 23.6 %collective-permute-done.7 = f32[7,3,22,3]{3,2,1,0:T(8,128)S(1)} collective-permute-done((f32[7,3,22,3]{3,2,1,0:T(8,128)S(1)}, f32[7,3,22,3]{3,2,1,0:T(8,128)S(1)}, u32[]{:S(2)}, u32[]{:S(2)}) %collective-permute-start.7) | collective-permute-done | bytes 5576 | tf_op jit(solution)/shard_map/ppermute | solution.py:20
  317.3 0.2 pad_maximum_fusion.9
  318.1 0.3 fusion.17
  318.4 0.2 select_add_fusion.1
  320.9 0.6 copy-done.3
  321.5 1.4 fusion.82
  (210 shorter events, 7.0 us)
Async XLA Ops:
  0.0 1.6 copy-start
  0.0 8.1 %copy-start.2 = (f32[2,6,3,16,128]{4,3,2,1,0:T(8,128)S(1)}, f32[2,6,3,16,128]{4,3,2,1,0:T(8,128)}, u32[]{:S(2)}) copy-start(f32[2,6,3,16,128]{4,3,2,1,0:T(8,128)} %param.58) | copy-start | bytes 884740
  1.6 230.0 %collective-permute-start = (f32[7,3,3,128]{3,0,2,1:T(8,128)S(1)}, f32[7,3,3,128]{3,0,2,1:T(8,128)S(1)}, u32[]{:S(2)}, u32[]{:S(2)}) collective-permute-start(f32[7,3,3,128]{3,0,2,1:T(8,128)S(1)} %copy.216), channel_id=1, source_target_pairs={{0,64},{64,128},{128,192},{192,256},{256,320},{320,384},{384,448},... | collective-permute-start | bytes 96776 | tf_op jit(solution)/shard_map/ppermute | solution.py:17
  6.2 225.4 %collective-permute-start.1 = (f32[7,3,3,128]{3,0,2,1:T(8,128)S(1)}, f32[7,3,3,128]{3,0,2,1:T(8,128)S(1)}, u32[]{:S(2)}, u32[]{:S(2)}) collective-permute-start(f32[7,3,3,128]{3,0,2,1:T(8,128)S(1)} %copy.217), channel_id=1, source_target_pairs={{64,0},{128,64},{192,128},{256,192},{320,256},{384,320},{448,384},... | collective-permute-start | bytes 96776 | tf_op jit(solution)/shard_map/ppermute | solution.py:20
  8.3 223.2 %copy-start.1 = (f32[3,3,16,128]{3,2,1,0:T(8,128)S(1)}, f32[3,3,16,128]{3,2,1,0:T(8,128)}, u32[]{:S(2)}) copy-start(f32[3,3,16,128]{3,2,1,0:T(8,128)} %param.59) | copy-start | bytes 221188
  231.8 22.4 %collective-permute-start.3 = (f32[7,3,22,3]{3,2,1,0:T(8,128)S(1)}, f32[7,3,22,3]{3,2,1,0:T(8,128)S(1)}, u32[]{:S(2)}, u32[]{:S(2)}) collective-permute-start(f32[7,3,22,3]{3,2,1,0:T(8,128)S(1)} %get-tuple-element.378), channel_id=1, source_target_pairs={{1,0},{2,1},{3,2},{4,3},{5,4},{6,5},{7,6},{8,7},{9,8},{10,9},{11,1... | collective-permute-start | bytes 16640 | tf_op jit(solution)/shard_map/ppermute | solution.py:20
  233.7 22.1 %collective-permute-start.2 = (f32[7,3,22,3]{3,2,1,0:T(8,128)S(1)}, f32[7,3,22,3]{3,2,1,0:T(8,128)S(1)}, u32[]{:S(2)}, u32[]{:S(2)}) collective-permute-start(f32[7,3,22,3]{3,2,1,0:T(8,128)S(1)} %get-tuple-element.377), channel_id=1, source_target_pairs={{0,1},{1,2},{2,3},{3,4},{4,5},{5,6},{6,7},{7,8},{8,9},{9,10},{10,1... | collective-permute-start | bytes 16640 | tf_op jit(solution)/shard_map/ppermute | solution.py:17
  260.0 0.7 copy-start.4
  260.9 10.6 %collective-permute-start.4 = (f32[7,3,3,128]{3,0,2,1:T(8,128)S(1)}, f32[7,3,3,128]{3,0,2,1:T(8,128)S(1)}, u32[]{:S(2)}, u32[]{:S(2)}) collective-permute-start(f32[7,3,3,128]{3,0,2,1:T(8,128)S(1)} %copy.218), channel_id=1, source_target_pairs={{0,64},{64,128},{128,192},{192,256},{256,320},{320,384},{384,448},... | collective-permute-start | bytes 96776 | tf_op jit(solution)/shard_map/ppermute | solution.py:17
  269.6 5.3 %collective-permute-start.5 = (f32[7,3,3,128]{3,0,2,1:T(8,128)S(1)}, f32[7,3,3,128]{3,0,2,1:T(8,128)S(1)}, u32[]{:S(2)}, u32[]{:S(2)}) collective-permute-start(f32[7,3,3,128]{3,0,2,1:T(8,128)S(1)} %copy.219), channel_id=1, source_target_pairs={{64,0},{128,64},{192,128},{256,192},{320,256},{384,320},{448,384},... | collective-permute-start | bytes 96776 | tf_op jit(solution)/shard_map/ppermute | solution.py:20
  275.1 17.9 %collective-permute-start.6 = (f32[7,3,22,3]{3,2,1,0:T(8,128)S(1)}, f32[7,3,22,3]{3,2,1,0:T(8,128)S(1)}, u32[]{:S(2)}, u32[]{:S(2)}) collective-permute-start(f32[7,3,22,3]{3,2,1,0:T(8,128)S(1)} %get-tuple-element.373), channel_id=1, source_target_pairs={{0,1},{1,2},{2,3},{3,4},{4,5},{5,6},{6,7},{7,8},{8,9},{9,10},{10,1... | collective-permute-start | bytes 16640 | tf_op jit(solution)/shard_map/ppermute | solution.py:17
  288.3 28.2 %collective-permute-start.7 = (f32[7,3,22,3]{3,2,1,0:T(8,128)S(1)}, f32[7,3,22,3]{3,2,1,0:T(8,128)S(1)}, u32[]{:S(2)}, u32[]{:S(2)}) collective-permute-start(f32[7,3,22,3]{3,2,1,0:T(8,128)S(1)} %get-tuple-element.374), channel_id=1, source_target_pairs={{1,0},{2,1},{3,2},{4,3},{5,4},{6,5},{7,6},{8,7},{9,8},{10,9},{11,1... | collective-permute-start | bytes 16640 | tf_op jit(solution)/shard_map/ppermute | solution.py:20
  320.9 0.7 copy-start.3
where the time goes:
time: 323 us
  blocking collectives  222 us (69%)
  starting transfers between devices  46 us (14%)
  waiting for transfers between devices  39.8 us (12%)
  other arithmetic  10.6 us (3%)
    pmax x1, blocking collectives, local(): peak_speed = lax.pmax(local_peak, ('gx', 'gy'))  114 us
    psum x1, blocking collectives, local(): power_total = lax.psum(local_total, ('gx', 'gy'))  107 us
    ppermute x4, starting transfers between devices, padded_2(): lax.ppermute(lax.slice_in_dim(block, block.shape[dim] - width, None, axis...  38.3 us
    ppermute x4, waiting for transfers between devices, padded_2(): lax.ppermute(lax.slice_in_dim(block, 0, width, axis=dim), axis, backward)  35.5 us
    ppermute x4, starting transfers between devices, padded_2(): lax.ppermute(lax.slice_in_dim(block, 0, width, axis=dim), axis, backward)  7.68 us
  transfers between devices with their start and end apart: 8, of which 5 were waited for; matrix products, arithmetic and copies ran while one was open for 0% of the time, Pallas kernels for 0%

commit v1 on v0

v1 whole, which is shorter than its diff:
```python
import functools

import jax
import jax.numpy as jnp
from jax import lax
from jax.experimental import pallas as pl
from jax.experimental.pallas import tpu as pltpu
from jax.sharding import Mesh
from jax.sharding import PartitionSpec as P

ADIABATIC = 5.0 / 3.0
CFL_NUMBER = 0.4
INJECTION = 0.04
LANES = 128
ROWS = 16
EXT = 32
FIELDS = 21
EDGES = 36
FORCES = 9
X_TILES = FIELDS + EDGES + FORCES
VMEM_LIMIT = 16 * 1024 * 1024
F32 = jnp.float32


def lane_index(shape):
    return lax.broadcasted_iota(jnp.int32, shape, len(shape) - 1)


def roll(values, shift, axis):
    size = values.shape[axis]
    shift = shift % size
    return values if shift == 0 else pltpu.roll(values, shift, axis)


def source_tile(refs, index):
    state, switch, edges, forcing = refs
    if index < 18:
        return lambda rows: state[index // 3, index % 3, rows, :]
    index -= 18
    if index < 3:
        return lambda rows: switch[index, rows, :].astype(F32)
    index -= 3
    if index < EDGES:
        side, rest = divmod(index, 18)
        return lambda rows: edges[side, rest // 3, rest % 3, rows, :]
    index -= EDGES
    return lambda rows: forcing[index // 3, index % 3, rows, :]


def first_kernel(place, state, switch, edges, forcing, pair_out, odd_out):
    odd = place[0]
    near = pl.multiple_of(8 * (1 - odd), 8)
    far = pl.multiple_of(8 * odd, 8)
    refs = (state, switch, edges, forcing)
    peak = None
    total = None
    for plane in range(3):
        density = state[0, plane]
        inverse = 1.0 / density
        momenta = [state[1 + k, plane] for k in range(3)]
        kinetic = 0.5 * inverse * (momenta[0] ** 2 + momenta[1] ** 2 + momenta[2] ** 2)
        heat = jnp.where(switch[plane] == 1, state[5, plane], state[4, plane] - kinetic)
        sound = jnp.sqrt(ADIABATIC * (ADIABATIC - 1.0) * heat * inverse)
        speed = (
            jnp.abs(momenta[0]) + jnp.abs(momenta[1]) + jnp.abs(momenta[2])
        ) * inverse + 3.0 * sound
        power = density * (forcing[0, plane] ** 2 + forcing[1, plane] ** 2 + forcing[2, plane] ** 2)
        peak = speed if peak is None else jnp.maximum(peak, speed)
        total = power if total is None else total + power
    for index in range(X_TILES):
        tile = source_tile(refs, index)
        pair_out[index] = tile(pl.ds(near, 8))
        odd_out[index] = tile(pl.ds(far, 8))
    row = lax.broadcasted_iota(jnp.int32, (8, LANES), 0)
    pair_out[X_TILES] = jnp.where(row == 0, jnp.max(peak), jnp.sum(total))


def second_kernel(place, state, switch, edges, forcing, pair_in, odd_in, even_out, odd_out):
    odd_x = place[0]
    odd_y = place[1]
    refs = (state, switch, edges, forcing)
    lane = lane_index((EXT, LANES))
    high = jnp.zeros((EXT, LANES), F32)
    low = jnp.zeros((EXT, LANES), F32)
    for index in range(FIELDS):
        from_pair = pair_in[1 - odd_x, index]
        from_odd = odd_in[index]
        below = jnp.where(odd_x == 0, from_odd, from_pair)
        above = jnp.where(odd_x == 0, from_pair, from_odd)
        block = source_tile(refs, index)(slice(0, ROWS))
        column = jnp.concatenate([below, block, above], axis=0)
        mine = (lane >= 6 * index) & (lane < 6 * index + 6)
        high = jnp.where(mine, roll(column, 6 * index - 122, 1), high)
        low = jnp.where(mine, roll(column, 6 * index, 1), low)
    even_out[0:EXT] = jnp.where(odd_y == 0, high, low)
    odd_out[0:EXT] = jnp.where(odd_y == 0, low, high)
    lane = lane_index((ROWS, LANES))
    for begin, count, row in ((FIELDS, EDGES, EXT), (FIELDS + EDGES, FORCES, EXT + ROWS)):
        high = jnp.zeros((ROWS, LANES), F32)
        low = jnp.zeros((ROWS, LANES), F32)
        for index in range(count):
            block = source_tile(refs, begin + index)(slice(0, ROWS))
            mine = (lane >= 3 * index) & (lane < 3 * index + 3)
            high = jnp.where(mine, roll(block, 3 * index - 125, 1), high)
            low = jnp.where(mine, roll(block, 3 * index, 1), low)
        even_out[row : row + ROWS] = jnp.where(odd_y == 0, high, low)
        odd_out[row : row + ROWS] = jnp.where(odd_y == 0, low, high)


def face_above(before, here, after, beyond):
    value = (7.0 / 12.0) * (here + after) - (1.0 / 12.0) * (before + beyond)
    return jnp.minimum(
        jnp.maximum(value, jnp.minimum(here, after)), jnp.maximum(here, after)
    )


def limited(here, face_low, face_high):
    low_dev = face_low - here
    high_dev = face_high - here
    opposite = low_dev * high_dev < 0.0
    low_span = 2.0 * jnp.abs(low_dev)
    high_span = 2.0 * jnp.abs(high_dev)
    low_dev = jnp.minimum(jnp.maximum(low_dev, -high_span), high_span)
    high_dev = jnp.minimum(jnp.maximum(high_dev, -low_span), low_span)
    return jnp.where(opposite, here + low_dev, here), jnp.where(opposite, here + high_dev, here)


def face_flux(left, right, normal):
    left_u, right_u = left[1 + normal], right[1 + normal]
    left_sound = jnp.sqrt(ADIABATIC * left[4] / left[0])
    right_sound = jnp.sqrt(ADIABATIC * right[4] / right[0])
    slow = jnp.minimum(jnp.minimum(left_u - left_sound, right_u - right_sound), 0.0)
    fast = jnp.maximum(jnp.maximum(left_u + left_sound, right_u + right_sound), 0.0)
    share = 1.0 / (fast - slow)
    left_part = fast * share
    right_part = -slow * share
    left_rate = left_part * (left_u - slow)
    right_rate = right_part * (right_u - fast)
    left_mass = left_rate * left[0]
    right_mass = right_rate * right[0]
    left_square = left[1] * left[1] + left[2] * left[2] + left[3] * left[3]
    right_square = right[1] * right[1] + right[2] * right[2] + right[3] * right[3]
    flux = [left_mass + right_mass]
    for k in (1, 2, 3):
        flux.append(left_mass * left[k] + right_mass * right[k])
    left_push = left_part * left[4]
    right_push = right_part * right[4]
    flux[1 + normal] = flux[1 + normal] + (left_push + right_push)
    flux.append(
        0.5 * (left_mass * left_square + right_mass * right_square)
        + left[4] * (1.5 * left_rate)
        + right[4] * (1.5 * right_rate)
        + left_push * left_u
        + right_push * right_u
    )
    flux.append(left_mass * left[5] + right_mass * right[5])
    return flux


def z_fluxes(planes):
    lower, upper = [], []
    for k in range(6):
        column = [planes[j][k] for j in range(9)]
        faces = [face_above(*column[j : j + 4]) for j in range(6)]
        cells = [limited(column[j + 2], faces[j], faces[j + 1]) for j in range(5)]
        lower.append([cells[j][1] for j in range(4)])
        upper.append([cells[j + 1][0] for j in range(4)])
    return [
        face_flux([lower[k][j] for k in range(6)], [upper[k][j] for k in range(6)], 2)
        for j in range(4)
    ]


def edge_primitives(fields):
    density = fields[0]
    inverse = 1.0 / density
    kinetic = 0.5 * inverse * (fields[1] ** 2 + fields[2] ** 2 + fields[3] ** 2)
    return [
        density,
        fields[1] * inverse,
        fields[2] * inverse,
        fields[3] * inverse,
        (ADIABATIC - 1.0) * (fields[4] - kinetic),
        fields[5] * inverse,
    ]


def shift_pair(main, rim, step):
    lane = lane_index(main.shape)
    main_rolled = roll(main, -step, 1)
    rim_rolled = roll(rim, -step, 1)
    inside = lane < LANES - step if step > 0 else lane >= -step
    return (
        jnp.where(inside, main_rolled, rim_rolled),
        jnp.where(inside, rim_rolled, main_rolled),
    )


def y_differences(main, rim):
    lows, highs = ([], []), ([], [])
    spread = None
    for k in range(6):
        here = (main[k], rim[k])
        before = shift_pair(*here, -1)
        after = shift_pair(*here, 1)
        beyond = shift_pair(*here, 2)
        faces = [face_above(before[j], here[j], after[j], beyond[j]) for j in range(2)]
        below = shift_pair(*faces, -1)
        cells = [limited(here[j], below[j], faces[j]) for j in range(2)]
        nexts = shift_pair(cells[0][0], cells[1][0], 1)
        for j in range(2):
            lows[j].append(cells[j][1])
            highs[j].append(nexts[j])
        if k == 2:
            spread = [0.5 * (after[j] - before[j]) for j in range(2)]
    fluxes = [face_flux(lows[j], highs[j], 1) for j in range(2)]
    differences = ([], [])
    for k in range(6):
        below = shift_pair(fluxes[0][k], fluxes[1][k], -1)
        for j in range(2):
            differences[j].append(fluxes[j][k] - below[j])
    return differences, spread


CHUNKS = (4, 12, 20)


def x_sweep(prims, plane, chunks, low_ref, high_ref, flux_ref):
    for row in chunks:
        for k in range(6):
            rows = [prims[k, plane, pl.ds(row + s, 8), :] for s in (-2, -1, 0, 1, 2)]
            below = face_above(*rows[0:4])
            above = face_above(*rows[1:5])
            low_ref[k, pl.ds(row, 8), :], high_ref[k, pl.ds(row, 8), :] = limited(
                rows[2], below, above
            )
    for row in chunks:
        left = [high_ref[k, pl.ds(row, 8), :] for k in range(6)]
        right = [low_ref[k, pl.ds(row + 1, 8), :] for k in range(6)]
        flux = face_flux(left, right, 0)
        for k in range(6):
            flux_ref[k, pl.ds(row, 8), :] = flux[k]


def third_kernel(
    place, state, switch, edges, forcing, pair_in, odd_in, even_in, odd_y_in,
    fields, force, tend, prims, planes, low_ref, high_ref, flux_ref,
):
    odd_x = place[0]
    odd_y = place[1]
    refs = (state, switch, edges, forcing)
    lane = lane_index((EXT, LANES))
    above_strip = jnp.where(odd_y == 0, even_in[...], odd_y_in[...])
    below_strip = jnp.where(odd_y == 0, odd_y_in[...], even_in[...])

    def with_rows(index):
        from_pair = pair_in[1 - odd_x, index]
        from_odd = odd_in[index]
        below = jnp.where(odd_x == 0, from_odd, from_pair)
        above = jnp.where(odd_x == 0, from_pair, from_odd)
        block = source_tile(refs, index)(slice(0, ROWS))
        return jnp.concatenate([below, block, above], axis=0)

    for index in range(FIELDS):
        fields[0, index] = with_rows(index)
        fields[1, index] = jnp.where(
            lane < 64,
            roll(above_strip[0:EXT], -6 * index, 1),
            roll(below_strip[0:EXT], 122 - 6 * index, 1),
        )
    lane = lane_index((ROWS, LANES))
    rim_edges = []
    for begin, count, row in ((FIELDS, EDGES, EXT), (FIELDS + EDGES, FORCES, EXT + ROWS)):
        for index in range(count):
            rim = jnp.where(
                lane < 64,
                roll(above_strip[row : row + ROWS], -3 * index, 1),
                roll(below_strip[row : row + ROWS], 125 - 3 * index, 1),
            )
            if begin == FIELDS:
                rim_edges.append(rim)
            else:
                force[0, index] = with_rows(begin + index)
                force[1, index, 0:8] = jnp.zeros((8, LANES), F32)
                force[1, index, 8:24] = rim
                force[1, index, 24:32] = jnp.zeros((8, LANES), F32)

    for plane in range(3):
        for tile in range(2):
            values = [fields[tile, 3 * k + plane] for k in range(7)]
            density = values[0]
            inverse = 1.0 / density
            kinetic = 0.5 * inverse * (values[1] ** 2 + values[2] ** 2 + values[3] ** 2)
            heat = jnp.where(values[6] == 1.0, values[5], values[4] - kinetic)
            prims[tile, 0, plane] = density
            for k in (1, 2, 3):
                prims[tile, k, plane] = values[k] * inverse
            prims[tile, 4, plane] = (ADIABATIC - 1.0) * heat
            prims[tile, 5, plane] = values[5] * inverse
    for side in range(2):
        for plane in range(3):
            index = 18 * side + plane
            values = edge_primitives([with_rows(FIELDS + index + 3 * k) for k in range(6)])
            for k in range(6):
                planes[0, side, k, plane] = values[k]
            values = edge_primitives([rim_edges[index + 3 * k] for k in range(6)])
            for k in range(6):
                planes[1, side, k, plane, 0:8] = jnp.ones((8, LANES), F32)
                planes[1, side, k, plane, 8:24] = values[k]
                planes[1, side, k, plane, 24:32] = jnp.ones((8, LANES), F32)

    for plane in range(3):
        spreads = {}
        for row in CHUNKS:
            both = [
                [prims[tile, k, plane, pl.ds(row, 8), :] for k in range(6)] for tile in range(2)
            ]
            differences, spread = y_differences(*both)
            for tile in range(2):
                spreads[tile, row] = spread[tile]
                for k in range(6):
                    tend[tile, 3 * k + plane, pl.ds(row, 8), :] = -differences[tile][k]
        for tile in range(2):
            for k in range(6):
                low_ref[k, pl.ds(28, 4), :] = jnp.ones((4, LANES), F32)
                flux_ref[k, pl.ds(0, 4), :] = jnp.zeros((4, LANES), F32)
            x_sweep(prims.at[tile], plane, CHUNKS, low_ref, high_ref, flux_ref)
            for row in CHUNKS:
                for k in range(6):
                    difference = (
                        flux_ref[k, pl.ds(row, 8), :] - flux_ref[k, pl.ds(row - 1, 8), :]
                    )
                    tend[tile, 3 * k + plane, pl.ds(row, 8), :] -= difference
                before = prims[tile, 1, plane, pl.ds(row - 1, 8), :]
                after = prims[tile, 1, plane, pl.ds(row + 1, 8), :]
                spread = spreads[tile, row] + 0.5 * (after - before)
                below = prims[tile, 3, plane - 1, pl.ds(row, 8), :] if plane > 0 else (
                    planes[tile, 0, 3, 2, pl.ds(row, 8), :]
                )
                above = prims[tile, 3, plane + 1, pl.ds(row, 8), :] if plane < 2 else (
                    planes[tile, 1, 3, 0, pl.ds(row, 8), :]
                )
                spread = spread + 0.5 * (above - below)
                pressure = prims[tile, 4, plane, pl.ds(row, 8), :]
                tend[tile, 15 + plane, pl.ds(row, 8), :] -= pressure * spread
    for tile in range(2):
        for row in CHUNKS:
            rows = pl.ds(row, 8)
            column = (
                [[planes[tile, 0, k, p, rows, :] for k in range(6)] for p in range(3)]
                + [[prims[tile, k, p, rows, :] for k in range(6)] for p in range(3)]
                + [[planes[tile, 1, k, p, rows, :] for k in range(6)] for p in range(3)]
            )
            flux = z_fluxes(column)
            for plane in range(3):
                for k in range(6):
                    tend[tile, 3 * k + plane, rows, :] -= flux[plane + 1][k] - flux[plane][k]


def settled(values, switch):
    kinetic = 0.5 / values[0] * (values[1] ** 2 + values[2] ** 2 + values[3] ** 2)
    return jnp.where(switch == 0.0, values[4] - kinetic, values[5])


def fourth_kernel(
    cells, totals, fields, force, tend, edges, updated,
    section, prims, low_ref, high_ref, flux_ref,
):
    peak = jnp.max(totals[:, 0, :], axis=0, keepdims=True)
    power = jnp.sum(totals[:, 1, :], axis=0, keepdims=True)
    time_step = CFL_NUMBER / peak
    scale = jnp.sqrt(INJECTION / (0.5 * time_step * (power / cells + 1e-06)))

    def forced(values, force_values, tendency):
        result = list(tendency)
        for k in (1, 2, 3):
            result[k] = result[k] + scale * values[0] * force_values[k - 1]
        result[4] = result[4] + scale * (
            values[1] * force_values[0] + values[2] * force_values[1] + values[3] * force_values[2]
        )
        return result

    for plane in range(3):
        for tile in range(2):
            for row in CHUNKS:
                rows = pl.ds(row, 8)
                values = [fields[tile, 3 * k + plane, rows, :] for k in range(7)]
                drive = [force[tile, 3 * k + plane, rows, :] for k in range(3)]
                rate = forced(values, drive, [tend[tile, 3 * k + plane, rows, :] for k in range(6)])
                stage = [values[k] + time_step * rate[k] for k in range(6)]
                stage[5] = settled(stage, values[6])
                inverse = 1.0 / stage[0]
                if tile == 0:
                    for k in range(6):
                        section[k, plane, rows, :] = stage[k]
                prims[tile, 0, plane, rows, :] = stage[0]
                for k in (1, 2, 3):
                    prims[tile, k, plane, rows, :] = stage[k] * inverse
                prims[tile, 4, plane, rows, :] = (ADIABATIC - 1.0) * stage[5]
                prims[tile, 5, plane, rows, :] = stage[5] * inverse

    z_flux = []
    outer = {}
    for row in (8, 16):
        rows = pl.ds(row, 8)
        for side in range(2):
            for plane in range(3):
                outer[side, plane] = edge_primitives(
                    [edges[side, k, plane, pl.ds(row - 8, 8), :] for k in range(6)]
                )
        column = (
            [outer[0, p] for p in range(3)]
            + [[prims[0, k, p, rows, :] for k in range(6)] for p in range(3)]
            + [outer[1, p] for p in range(3)]
        )
        flux = z_fluxes(column)
        for plane in range(3):
            below = outer[0, 2][3] if plane == 0 else prims[0, 3, plane - 1, rows, :]
            above = outer[1, 0][3] if plane == 2 else prims[0, 3, plane + 1, rows, :]
            spread = 0.5 * (above - below)
            for k in range(6):
                updated[k, plane, pl.ds(row - 8, 8), :] = flux[plane][k] - flux[plane + 1][k]
            pressure = prims[0, 4, plane, rows, :]
            updated[5, plane, pl.ds(row - 8, 8), :] -= pressure * spread
    for plane in range(3):
        for k in range(6):
            low_ref[k, pl.ds(28, 4), :] = jnp.ones((4, LANES), F32)
        x_sweep(prims.at[0], plane, CHUNKS, low_ref, high_ref, flux_ref)
        for row in (8, 16):
            rows = pl.ds(row, 8)
            inner = pl.ds(row - 8, 8)
            both = [
                [prims[tile, k, plane, rows, :] for k in range(6)] for tile in range(2)
            ]
            differences, spread = y_differences(*both)
            before = prims[0, 1, plane, pl.ds(row - 1, 8), :]
            after = prims[0, 1, plane, pl.ds(row + 1, 8), :]
            spread = spread[0] + 0.5 * (after - before)
            rate = []
            for k in range(6):
                across = flux_ref[k, rows, :] - flux_ref[k, pl.ds(row - 1, 8), :]
                rate.append(updated[k, plane, inner, :] - differences[0][k] - across)
            rate[5] = rate[5] - both[0][4] * spread
            stage = [section[k, plane, rows, :] for k in range(6)]
            drive = [force[0, 3 * k + plane, rows, :] for k in range(3)]
            rate = forced(stage, drive, rate)
            values = [fields[0, 3 * k + plane, rows, :] for k in range(7)]
            result = [
                0.5 * values[k] + 0.5 * (stage[k] + time_step * rate[k]) for k in range(6)
            ]
            result[5] = settled(result, values[6])
            for k in range(6):
                updated[k, plane, inner, :] = result[k]


def shape(*sizes):
    return jax.ShapeDtypeStruct(sizes, F32)


def vmem_specs(count):
    return [pl.BlockSpec(memory_space=pltpu.VMEM)] * count


def call(kernel, name, outs, scalars, arrays, scratch=(), flops=0):
    single = not isinstance(outs, tuple)
    return pl.pallas_call(
        kernel,
        out_shape=outs,
        in_specs=[pl.BlockSpec(memory_space=pltpu.SMEM)] * len(scalars) + vmem_specs(len(arrays)),
        out_specs=vmem_specs(1)[0] if single else tuple(vmem_specs(len(outs))),
        scratch_shapes=list(scratch),
        compiler_params=pltpu.CompilerParams(vmem_limit_bytes=VMEM_LIMIT),
        cost_estimate=pl.CostEstimate(flops=flops, bytes_accessed=1000000, transcendentals=0),
        name=name,
    )(*scalars, *arrays)


def pairs(count, begin):
    table = []
    for first in range(begin, begin + count, 2):
        low, high = first % count, (first + 1) % count
        table += [(low, high), (high, low)]
    return table


def join(rows):
    return jnp.stack([jnp.max(rows[:, 0], axis=0), jnp.sum(rows[:, 1], axis=0)])


def exchanged(row, axes):
    count = lax.axis_size(axes)
    spread = jnp.broadcast_to(row[None], (count,) + row.shape)
    return lax.all_to_all(spread, axes, 0, 0, tiled=True)


GX = ("zl", "core")
GY = ("y", "zh", "x")


def local(fluid_state, switch, z_edges, forcing):
    count_x = lax.axis_size(GX)
    count_y = lax.axis_size(GY)
    cells = 3.0 * ROWS * LANES * count_x * count_y
    place = jnp.stack([lax.axis_index(GX) % 2, lax.axis_index(GY) % 2]).astype(jnp.int32)
    arrays = (fluid_state, switch, z_edges, forcing)
    tile = (8, LANES)
    pair_out, odd_out = call(
        first_kernel,
        "first",
        (shape(X_TILES + 1, *tile), shape(X_TILES, *tile)),
        (place,),
        arrays,
    )
    pair_in = lax.all_gather(pair_out, "core")
    odd_in = lax.ppermute(odd_out, GX, pairs(count_x, 1))
    totals = exchanged(join(pair_in[:, X_TILES, 0:2]), ("y", "x"))
    strips = call(
        second_kernel,
        "second",
        (shape(EXT + 2 * ROWS, LANES), shape(EXT + 2 * ROWS, LANES)),
        (place,),
        (*arrays, pair_in, odd_in),
    )
    even_in = lax.ppermute(strips[0], GY, pairs(count_y, 0))
    odd_y_in = lax.ppermute(strips[1], GY, pairs(count_y, 1))
    totals = exchanged(join(totals), ("zh", "zl"))
    extended = (EXT, LANES)
    work = [pltpu.VMEM((6, *extended), F32) for _ in range(3)]
    fields, force, tend = call(
        third_kernel,
        "third",
        (shape(2, FIELDS, *extended), shape(2, FORCES, *extended), shape(2, 18, *extended)),
        (place,),
        (*arrays, pair_in, odd_in, even_in, odd_y_in),
        [pltpu.VMEM((2, 6, 3, *extended), F32), pltpu.VMEM((2, 2, 6, 3, *extended), F32), *work],
        flops=10_000_000,
    )
    return call(
        functools.partial(fourth_kernel, cells),
        "fourth",
        shape(6, 3, ROWS, LANES),
        (),
        (totals, fields, force, tend, z_edges),
        [pltpu.VMEM((6, 3, *extended), F32), pltpu.VMEM((2, 6, 3, *extended), F32), *work],
        flops=10_000_000,
    )


def solution(mesh):
    count_x, count_y = mesh.devices.shape
    count_z = 2 if count_y % 8 == 0 else 1
    parts = (count_x // 2, 2, count_y // (4 * count_z), count_z, 4)
    split = Mesh(mesh.devices.reshape(parts), (*GX, *GY))
    return jax.shard_map(
        local,
        mesh=split,
        in_specs=(
            P(None, None, GX, GY),
            P(None, GX, GY),
            P(None, None, None, GX, GY),
            P(None, None, GX, GY),
        ),
        out_specs=P(None, None, GX, GY),
        check_vma=False,
    )
```

time: 323 us -> 73.7 us (0.23)
  the two profiles are of different devices: /device:TPU:31 before, /device:TPU:64 now
where the time goes in v1:
time: 73.7 us; the launch traced here: 73.2 us
  starting transfers between devices  41.5 us (56%)
  Pallas kernels  12.6 us (17%)
  waiting for transfers between devices  11.8 us (16%)
  local copies, waits for them, and re-layouts  4.69 us (6%)
  blocking collectives  2.33 us (3%)
    all_to_all x2, starting transfers between devices, exchanged(): return lax.all_to_all(spread, axes, 0, 0, tiled=True)  24.7 us
    pallas_call x4, Pallas kernels, call(): pl.pallas_call(kernel, out_shape=outs, in_specs=[pl.BlockSpec(memory_spac...  12.6 us
    ppermute x1, starting transfers between devices, local(): odd_y_in = lax.ppermute(strips[1], GY, pairs(count_y, 1))  10.1 us
    ppermute x1, waiting for transfers between devices, local(): odd_y_in = lax.ppermute(strips[1], GY, pairs(count_y, 1))  6.24 us
    all_to_all x2, waiting for transfers between devices, exchanged(): return lax.all_to_all(spread, axes, 0, 0, tiled=True)  5.57 us
    ppermute x1, starting transfers between devices, local(): odd_in = lax.ppermute(odd_out, GX, pairs(count_x, 1))  4.22 us
    unnamed x14, local copies, waits for them, and re-layouts  3.43 us
    ppermute x1, starting transfers between devices, local(): even_in = lax.ppermute(strips[0], GY, pairs(count_y, 0))  2.52 us
  transfers between devices with their start and end apart: 5, of which 2 were waited for; matrix products, arithmetic and copies ran while one was open for 1% of the time, Pallas kernels for 12%

profile of v1, /device:TPU:64, one launch (start us, length us, event | category | flops | bytes accessed | tf_op | source)
XLA Modules:
  0.0 73.2 jit_solution(12779303853395745324)
XLA Ops:
  0.0 0.1 pad_add_fusion.place
  0.1 0.8 %copy-done.4 = f32[3,3,16,128]{3,2,1,0:T(8,128)S(1)} copy-done((f32[3,3,16,128]{3,2,1,0:T(8,128)S(1)}, f32[3,3,16,128]{3,2,1,0:T(8,128)}, u32[]{:S(2)}) %copy-start.4) | copy-done | bytes 73752
  0.9 1.0 %copy-done = f32[2,6,3,16,128]{4,3,2,1,0:T(8,128)S(1)} copy-done((f32[2,6,3,16,128]{4,3,2,1,0:T(8,128)S(1)}, f32[2,6,3,16,128]{4,3,2,1,0:T(8,128)}, u32[]{:S(2)}) %copy-start) | copy-done | bytes 294936
  1.8 0.9 %copy-done.2 = f32[6,3,16,128]{3,2,1,0:T(8,128)S(1)} copy-done((f32[6,3,16,128]{3,2,1,0:T(8,128)S(1)}, f32[6,3,16,128]{3,2,1,0:T(8,128)}, u32[]{:S(2)}) %copy-start.2) | copy-done | bytes 147480
  2.8 0.7 %copy-done.5 = s32[3,16,128]{2,1,0:T(8,128)S(1)} copy-done((s32[3,16,128]{2,1,0:T(8,128)S(1)}, s32[3,16,128]{2,1,0:T(8,128)}, u32[]{:S(2)}) %copy-start.5) | copy-done | bytes 24600
  3.5 0.7 first.1
  4.2 0.0 copy-start.1
  4.2 2.3 %all-gather = f32[134,8,128]{2,1,0:T(8,128)S(1)} all-gather(f32[67,8,128]{2,1,0:T(8,128)S(1)} %get-tuple-element.12), channel_id=2, replica_groups=mesh['zl'=6,'core'=2,'y'=8,'zh'=2,'x'=4] {'core'}, dimensions={0}, use_global_device_ids=true | all-gather | bytes 823296 | tf_op jit(solution)/shard_map/all_gather | solution.py:514
  6.6 0.6 broadcast_in_dim.4
  7.2 10.0 %all-to-all-start = ((f32[32,2,128]{2,1,0:T(2,128)}), f32[32,2,128]{2,1,0:T(2,128)S(1)}, u32[]{:S(2)}, u32[]{:S(2)}) async-start(f32[32,2,128]{2,1,0:T(2,128)} %broadcast_in_dim.4), calls=%async_computation | async-start | bytes 65536 | tf_op jit(solution)/shard_map/all_to_all | solution.py:493
  17.2 4.2 %collective-permute-start = (f32[66,8,128]{2,1,0:T(8,128)S(1)}, f32[66,8,128]{2,1,0:T(8,128)S(1)}, u32[]{:S(2)}, u32[]{:S(2)}) collective-permute-start(f32[66,8,128]{2,1,0:T(8,128)S(1)} %get-tuple-element.13), channel_id=1, source_target_pairs={{64,128},{128,64},{192,256},{256,192},{320,384},{384,320},{448,512... | collective-permute-start | bytes 811016 | tf_op jit(solution)/shard_map/ppermute | solution.py:515
  21.4 5.6 %all-to-all-done = f32[32,2,128]{2,1,0:T(2,128)S(1)} async-done(((f32[32,2,128]{2,1,0:T(2,128)}), f32[32,2,128]{2,1,0:T(2,128)S(1)}, u32[]{:S(2)}, u32[]{:S(2)}) %all-to-all-start) | async-done | bytes 32800 | tf_op jit(solution)/shard_map/all_to_all | solution.py:493
  27.1 0.6 broadcast_in_dim.5
  27.7 14.8 %all-to-all-start.1 = ((f32[12,2,128]{2,1,0:T(2,128)}), f32[12,2,128]{2,1,0:T(2,128)S(1)}, u32[]{:S(2)}, u32[]{:S(2)}) async-start(f32[12,2,128]{2,1,0:T(2,128)} %broadcast_in_dim.5), calls=%async_computation.1 | async-start | bytes 24576 | tf_op jit(solution)/shard_map/all_to_all | solution.py:493
  42.4 0.0 collective-permute-done.odd_in
  42.4 0.0 copy-done.1
  42.5 1.0 %second.1 = (f32[64,128]{1,0:T(8,128)S(1)}, f32[64,128]{1,0:T(8,128)S(1)}) custom-call(s32[2]{0:T(128)S(1)} %pad_add_fusion.place, f32[6,3,16,128]{3,2,1,0:T(8,128)S(1)} %copy-done.3, s32[3,16,128]{2,1,0:T(8,128)S(1)} %copy-done.6, f32[2,6,3,16,128]{4,3,2,1,0:T(8,128)S(1)} %copy-done.1, f32[3,3,16,128]{3,2,1,0:T(8,128)S(1)} %copy-done.4, ...), custom_call_target="tpu_custom_call" | custom-call | bytes 1000000 | tf_op jit(solution)/shard_map/second/pallas_call | solution.py:466
  43.4 2.5 %collective-permute-start.1 = (f32[64,128]{1,0:T(8,128)S(1)}, f32[64,128]{1,0:T(8,128)S(1)}, u32[]{:S(2)}, u32[]{:S(2)}) collective-permute-start(f32[64,128]{1,0:T(8,128)S(1)} %get-tuple-element.14), channel_id=1, source_target_pairs={{0,1},{1,0},{2,3},{3,2},{4,5},{5,4},{6,7},{7,6},{8,9},{9,8},{10,11... | collective-permute-start | bytes 98312 | tf_op jit(solution)/shard_map/ppermute | solution.py:524
  46.0 10.1 %collective-permute-start.2 = (f32[64,128]{1,0:T(8,128)S(1)}, f32[64,128]{1,0:T(8,128)S(1)}, u32[]{:S(2)}, u32[]{:S(2)}) collective-permute-start(f32[64,128]{1,0:T(8,128)S(1)} %get-tuple-element.15), channel_id=1, source_target_pairs={{1,2},{2,1},{3,4},{4,3},{5,6},{6,5},{7,8},{8,7},{9,10},{10,9},{11,... | collective-permute-start | bytes 98312 | tf_op jit(solution)/shard_map/ppermute | solution.py:525
  56.1 0.0 collective-permute-done.1.even_in
  56.1 6.2 %collective-permute-done.2.odd_y_in = f32[64,128]{1,0:T(8,128)S(1)} collective-permute-done((f32[64,128]{1,0:T(8,128)S(1)}, f32[64,128]{1,0:T(8,128)S(1)}, u32[]{:S(2)}, u32[]{:S(2)}) %collective-permute-start.2) | collective-permute-done | bytes 32800 | tf_op jit(solution)/shard_map/ppermute | solution.py:525
  62.3 8.1 %third.1 = (f32[2,21,32,128]{3,2,1,0:T(8,128)S(1)}, f32[2,9,32,128]{3,2,1,0:T(8,128)S(1)}, f32[2,18,32,128]{3,2,1,0:T(8,128)S(1)}) custom-call(s32[2]{0:T(128)S(1)} %pad_add_fusion.place, f32[6,3,16,128]{3,2,1,0:T(8,128)S(1)} %copy-done.3, s32[3,16,128]{2,1,0:T(8,128)S(1)} %copy-done.6, f32[2,6,3,16,128]{4,3,2,1,0:T(8,128)S(1)} %copy-done.1, ...), custom_call_target="tpu_custom_call" | custom-call | flops 10000000 | bytes 1000000 | tf_op jit(solution)/shard_map/third/pallas_call | solution.py:466
  70.5 0.0 all-to-all-done.1.totals
  70.5 2.8 %fourth.1 = f32[6,3,16,128]{3,2,1,0:T(8,128)} custom-call(f32[12,2,128]{2,1,0:T(2,128)S(1)} %all-to-all-done.1.totals, f32[2,21,32,128]{3,2,1,0:T(8,128)S(1)} %get-tuple-element.16.fields, f32[2,9,32,128]{3,2,1,0:T(8,128)S(1)} %get-tuple-element.17.force, f32[2,18,32,128]{3,2,1,0:T(8,128)S(1)} %get-tuple-element.18.tend, f32[2,6,3,16,128]{4,3,2,1,0:T(8,128)S(1)} %copy-done.1), custom_call_target="tpu_custom_call" | custom-call | flops 10000000 | bytes 1000000 | tf_op jit(solution)/shard_map/fourth/pallas_call | solution.py:466
  (15 shorter events, 0.1 us)
Async XLA Ops:
  0.0 0.9 %copy-start.4 = (f32[3,3,16,128]{3,2,1,0:T(8,128)S(1)}, f32[3,3,16,128]{3,2,1,0:T(8,128)}, u32[]{:S(2)}) copy-start(f32[3,3,16,128]{3,2,1,0:T(8,128)} %forcing.5) | copy-start | bytes 221188
  0.9 1.0 %copy-start = (f32[2,6,3,16,128]{4,3,2,1,0:T(8,128)S(1)}, f32[2,6,3,16,128]{4,3,2,1,0:T(8,128)}, u32[]{:S(2)}) copy-start(f32[2,6,3,16,128]{4,3,2,1,0:T(8,128)} %edges.7) | copy-start | bytes 884740
  1.8 0.9 %copy-start.2 = (f32[6,3,16,128]{3,2,1,0:T(8,128)S(1)}, f32[6,3,16,128]{3,2,1,0:T(8,128)}, u32[]{:S(2)}) copy-start(f32[6,3,16,128]{3,2,1,0:T(8,128)} %state.5) | copy-start | bytes 442372
  2.8 0.7 %copy-start.5 = (s32[3,16,128]{2,1,0:T(8,128)S(1)}, s32[3,16,128]{2,1,0:T(8,128)}, u32[]{:S(2)}) copy-start(s32[3,16,128]{2,1,0:T(8,128)} %switch.5) | copy-start | bytes 73732
  4.2 38.2 %copy-start.1 = (f32[2,6,3,16,128]{4,3,2,1,0:T(8,128)S(1)}, f32[2,6,3,16,128]{4,3,2,1,0:T(8,128)}, u32[]{:S(2)}) copy-start(f32[2,6,3,16,128]{4,3,2,1,0:T(8,128)} %edges.7) | copy-start | bytes 884740
  6.5 35.9 %copy-start.3 = (f32[6,3,16,128]{3,2,1,0:T(8,128)S(1)}, f32[6,3,16,128]{3,2,1,0:T(8,128)}, u32[]{:S(2)}) copy-start(f32[6,3,16,128]{3,2,1,0:T(8,128)} %state.5) | copy-start | bytes 442372
  7.2 19.8 %all-to-all-start = ((f32[32,2,128]{2,1,0:T(2,128)}), f32[32,2,128]{2,1,0:T(2,128)S(1)}, u32[]{:S(2)}, u32[]{:S(2)}) async-start(f32[32,2,128]{2,1,0:T(2,128)} %broadcast_in_dim.4), calls=%async_computation | async-start | bytes 65536 | tf_op jit(solution)/shard_map/all_to_all | solution.py:493
  17.2 25.3 %collective-permute-start = (f32[66,8,128]{2,1,0:T(8,128)S(1)}, f32[66,8,128]{2,1,0:T(8,128)S(1)}, u32[]{:S(2)}, u32[]{:S(2)}) collective-permute-start(f32[66,8,128]{2,1,0:T(8,128)S(1)} %get-tuple-element.13), channel_id=1, source_target_pairs={{64,128},{128,64},{192,256},{256,192},{320,384},{384,320},{448,512... | collective-permute-start | bytes 811016 | tf_op jit(solution)/shard_map/ppermute | solution.py:515
  27.0 15.4 %copy-start.6 = (s32[3,16,128]{2,1,0:T(8,128)S(1)}, s32[3,16,128]{2,1,0:T(8,128)}, u32[]{:S(2)}) copy-start(s32[3,16,128]{2,1,0:T(8,128)} %switch.5) | copy-start | bytes 73732
  27.7 42.8 %all-to-all-start.1 = ((f32[12,2,128]{2,1,0:T(2,128)}), f32[12,2,128]{2,1,0:T(2,128)S(1)}, u32[]{:S(2)}, u32[]{:S(2)}) async-start(f32[12,2,128]{2,1,0:T(2,128)} %broadcast_in_dim.5), calls=%async_computation.1 | async-start | bytes 24576 | tf_op jit(solution)/shard_map/all_to_all | solution.py:493
  43.4 12.6 %collective-permute-start.1 = (f32[64,128]{1,0:T(8,128)S(1)}, f32[64,128]{1,0:T(8,128)S(1)}, u32[]{:S(2)}, u32[]{:S(2)}) collective-permute-start(f32[64,128]{1,0:T(8,128)S(1)} %get-tuple-element.14), channel_id=1, source_target_pairs={{0,1},{1,0},{2,3},{3,2},{4,5},{5,4},{6,7},{7,6},{8,9},{9,8},{10,11... | collective-permute-start | bytes 98312 | tf_op jit(solution)/shard_map/ppermute | solution.py:524
  46.0 16.3 %collective-permute-start.2 = (f32[64,128]{1,0:T(8,128)S(1)}, f32[64,128]{1,0:T(8,128)S(1)}, u32[]{:S(2)}, u32[]{:S(2)}) collective-permute-start(f32[64,128]{1,0:T(8,128)S(1)} %get-tuple-element.15), channel_id=1, source_target_pairs={{1,2},{2,1},{3,4},{4,3},{5,6},{6,5},{7,8},{8,7},{9,10},{10,9},{11,... | collective-permute-start | bytes 98312 | tf_op jit(solution)/shard_map/ppermute | solution.py:525

commit v2 on v1

--- a/solution.py
+++ b/solution.py
@@ -47,11 +47,24 @@
     return lambda rows: forcing[index // 3, index % 3, rows, :]
 
 
-def first_kernel(place, state, switch, edges, forcing, pair_out, odd_out):
+def first_kernel(
+    place, state_in, switch_in, edges_in, forcing_in,
+    pair_out, odd_out, state, switch, edges, forcing, arrived,
+):
+    refs = (state, switch, edges, forcing)
+    copies = [
+        pltpu.make_async_copy(source, target, arrived.at[k])
+        for k, (source, target) in enumerate(
+            zip((state_in, switch_in, edges_in, forcing_in), refs, strict=True)
+        )
+    ]
+    for copy in copies:
+        copy.start()
     odd = place[0]
     near = pl.multiple_of(8 * (1 - odd), 8)
     far = pl.multiple_of(8 * odd, 8)
-    refs = (state, switch, edges, forcing)
+    for copy in copies:
+        copy.wait()
     peak = None
     total = None
     for plane in range(3):
@@ -73,6 +86,13 @@
         odd_out[index] = tile(pl.ds(far, 8))
     row = lax.broadcasted_iota(jnp.int32, (8, LANES), 0)
     pair_out[X_TILES] = jnp.where(row == 0, jnp.max(peak), jnp.sum(total))
+
+
+def spread_kernel(rows, after, out):
+    peak = jnp.max(rows[:, 0, :], axis=0, keepdims=True)
+    total = jnp.sum(rows[:, 1, :], axis=0, keepdims=True)
+    joined = jnp.concatenate([peak, total], axis=0)
+    out[...] = jnp.broadcast_to(joined[None], out.shape)
 
 
 def second_kernel(place, state, switch, edges, forcing, pair_in, odd_in, even_out, odd_out):
@@ -461,7 +481,7 @@
     return [pl.BlockSpec(memory_space=pltpu.VMEM)] * count
 
 
-def call(kernel, name, outs, scalars, arrays, scratch=(), flops=0):
+def call(kernel, name, outs, scalars, arrays, scratch=(), cost=0):
     single = not isinstance(outs, tuple)
     return pl.pallas_call(
         kernel,
@@ -470,7 +490,7 @@
         out_specs=vmem_specs(1)[0] if single else tuple(vmem_specs(len(outs))),
         scratch_shapes=list(scratch),
         compiler_params=pltpu.CompilerParams(vmem_limit_bytes=VMEM_LIMIT),
-        cost_estimate=pl.CostEstimate(flops=flops, bytes_accessed=1000000, transcendentals=0),
+        cost_estimate=pl.CostEstimate(flops=cost, bytes_accessed=cost, transcendentals=0),
         name=name,
     )(*scalars, *arrays)
 
@@ -483,13 +503,16 @@
     return table
 
 
-def join(rows):
-    return jnp.stack([jnp.max(rows[:, 0], axis=0), jnp.sum(rows[:, 1], axis=0)])
-
-
-def exchanged(row, axes):
+def exchanged(rows, after, axes):
     count = lax.axis_size(axes)
-    spread = jnp.broadcast_to(row[None], (count,) + row.shape)
+    spread = pl.pallas_call(
+        spread_kernel,
+        out_shape=shape(count, 2, LANES),
+        in_specs=[*vmem_specs(1), pl.BlockSpec(memory_space=pl.ANY)],
+        out_specs=vmem_specs(1)[0],
+        compiler_params=pltpu.CompilerParams(vmem_limit_bytes=VMEM_LIMIT),
+        name="spread",
+    )(rows, after)
     return lax.all_to_all(spread, axes, 0, 0, tiled=True)
 
 
@@ -502,28 +525,38 @@
     count_y = lax.axis_size(GY)
     cells = 3.0 * ROWS * LANES * count_x * count_y
     place = jnp.stack([lax.axis_index(GX) % 2, lax.axis_index(GY) % 2]).astype(jnp.int32)
-    arrays = (fluid_state, switch, z_edges, forcing)
     tile = (8, LANES)
-    pair_out, odd_out = call(
+    inputs = (fluid_state, switch, z_edges, forcing)
+    pair_out, odd_out, *arrays = pl.pallas_call(
         first_kernel,
-        "first",
-        (shape(X_TILES + 1, *tile), shape(X_TILES, *tile)),
-        (place,),
-        arrays,
-    )
+        out_shape=(
+            shape(X_TILES + 1, *tile),
+            shape(X_TILES, *tile),
+            *(jax.ShapeDtypeStruct(values.shape, values.dtype) for values in inputs),
+        ),
+        in_specs=[
+            pl.BlockSpec(memory_space=pltpu.SMEM),
+            *([pl.BlockSpec(memory_space=pltpu.HBM)] * 4),
+        ],
+        out_specs=tuple(vmem_specs(6)),
+        scratch_shapes=[pltpu.SemaphoreType.DMA((4,))],
+        compiler_params=pltpu.CompilerParams(vmem_limit_bytes=VMEM_LIMIT),
+        name="first",
+    )(place, *(pltpu.with_memory_space_constraint(values, pltpu.HBM) for values in inputs))
     pair_in = lax.all_gather(pair_out, "core")
     odd_in = lax.ppermute(odd_out, GX, pairs(count_x, 1))
-    totals = exchanged(join(pair_in[:, X_TILES, 0:2]), ("y", "x"))
+    totals = exchanged(pair_in[:, X_TILES, 0:2], place, ("y", "x"))
     strips = call(
         second_kernel,
         "second",
         (shape(EXT + 2 * ROWS, LANES), shape(EXT + 2 * ROWS, LANES)),
         (place,),
         (*arrays, pair_in, odd_in),
+        cost=4_000_000,
     )
     even_in = lax.ppermute(strips[0], GY, pairs(count_y, 0))
     odd_y_in = lax.ppermute(strips[1], GY, pairs(count_y, 1))
-    totals = exchanged(join(totals), ("zh", "zl"))
+    totals = exchanged(totals, even_in, ("zh", "zl"))
     extended = (EXT, LANES)
     work = [pltpu.VMEM((6, *extended), F32) for _ in range(3)]
     fields, force, tend = call(
@@ -533,16 +566,16 @@
         (place,),
         (*arrays, pair_in, odd_in, even_in, odd_y_in),
         [pltpu.VMEM((2, 6, 3, *extended), F32), pltpu.VMEM((2, 2, 6, 3, *extended), F32), *work],
-        flops=10_000_000,
+        cost=60_000_000,
     )
     return call(
         functools.partial(fourth_kernel, cells),
         "fourth",
         shape(6, 3, ROWS, LANES),
         (),
-        (totals, fields, force, tend, z_edges),
+        (totals, fields, force, tend, arrays[2]),
         [pltpu.VMEM((6, 3, *extended), F32), pltpu.VMEM((2, 6, 3, *extended), F32), *work],
-        flops=10_000_000,
+        cost=8_000_000,
     )
 
 

time: 73.7 us -> 61.4 us (0.83)
  the two profiles are of different devices: /device:TPU:64 before, /device:TPU:1 now
where the time goes in v2:
time: 61.4 us; the launch traced here: 61.1 us
  starting transfers between devices  35.1 us (57%)
  Pallas kernels  14.9 us (24%)
  blocking collectives  10.1 us (16%)
  waiting for transfers between devices  0.73 us (1%)
    ppermute x1, starting transfers between devices, local(): odd_y_in = lax.ppermute(strips[1], GY, pairs(count_y, 1))  13.5 us
    all_to_all x2, starting transfers between devices, exchanged(): return lax.all_to_all(spread, axes, 0, 0, tiled=True)  13.2 us
    pallas_call x3, Pallas kernels, call(): pl.pallas_call(kernel, out_shape=outs, in_specs=[pl.BlockSpec(memory_spac...  11.9 us
    all_gather x1, blocking collectives, local(): pair_in = lax.all_gather(pair_out, 'core')  10.1 us
    ppermute x1, starting transfers between devices, local(): odd_in = lax.ppermute(odd_out, GX, pairs(count_x, 1))  5.39 us
    ppermute x1, starting transfers between devices, local(): even_in = lax.ppermute(strips[0], GY, pairs(count_y, 0))  3.14 us
    pallas_call x1, Pallas kernels, local(): pl.pallas_call(first_kernel, out_shape=(shape(X_TILES + 1, *tile), shape(...  1.79 us
    pallas_call x2, Pallas kernels, exchanged(): pl.pallas_call(spread_kernel, out_shape=shape(count, 2, LANES), in_specs=...  1.27 us
  transfers between devices with their start and end apart: 5, of which 1 were waited for; matrix products, arithmetic and copies ran while one was open for 0% of the time, Pallas kernels for 17%

profile of v2, /device:TPU:1, one launch (start us, length us, event | category | flops | bytes accessed | tf_op | source)
XLA Modules:
  0.0 61.1 jit_solution(16235971454577474445)
XLA Ops:
  0.0 0.1 pad_add_fusion.place.after
  0.1 1.8 %first.1 = (f32[67,8,128]{2,1,0:T(8,128)S(1)}, f32[66,8,128]{2,1,0:T(8,128)S(1)}, f32[6,3,16,128]{3,2,1,0:T(8,128)S(1)}, s32[3,16,128]{2,1,0:T(8,128)S(1)}, f32[...) custom-call(s32[2]{0:T(128)S(1)} %pad_add_fusion.place.after, f32[6,3,16,128]{3,2,1,0:T(8,128)} %state_in.1, ...), custom_call_target="tpu_custom_call" | custom-call | tf_op jit(solution)/shard_map/first/pallas_call | solution.py:530
  1.9 5.4 %collective-permute-start = (f32[66,8,128]{2,1,0:T(8,128)S(1)}, f32[66,8,128]{2,1,0:T(8,128)S(1)}, u32[]{:S(2)}, u32[]{:S(2)}) collective-permute-start(f32[66,8,128]{2,1,0:T(8,128)S(1)} %get-tuple-element.21), channel_id=1, source_target_pairs={{64,128},{128,64},{192,256},{256,192},{320,384},{384,320},{448,512... | collective-permute-start | bytes 811016 | tf_op jit(solution)/shard_map/ppermute | solution.py:547
  7.3 10.1 %all-gather = f32[134,8,128]{2,1,0:T(8,128)S(1)} all-gather(f32[67,8,128]{2,1,0:T(8,128)S(1)} %get-tuple-element.16), channel_id=2, replica_groups=mesh['zl'=6,'core'=2,'y'=8,'zh'=2,'x'=4] {'core'}, dimensions={0}, use_global_device_ids=true | all-gather | bytes 823296 | tf_op jit(solution)/shard_map/all_gather | solution.py:546
  17.4 0.6 %spread.2 = f32[32,2,128]{2,1,0:T(2,128)} custom-call(f32[2,2,128]{2,1,0:T(2,128)S(1)} %slice_bitcast_fusion.rows, s32[2]{0:T(128)S(1)} %pad_add_fusion.place.after), custom_call_target="tpu_custom_call" | custom-call | tf_op jit(solution)/shard_map/spread/pallas_call | solution.py:508
  18.0 9.7 %all-to-all-start = ((f32[32,2,128]{2,1,0:T(2,128)}), f32[32,2,128]{2,1,0:T(2,128)S(1)}, u32[]{:S(2)}, u32[]{:S(2)}) async-start(f32[32,2,128]{2,1,0:T(2,128)} %spread.2), calls=%async_computation | async-start | bytes 65536 | tf_op jit(solution)/shard_map/all_to_all | solution.py:516
  27.7 0.0 collective-permute-done.odd_in
  27.7 1.0 %second.1 = (f32[64,128]{1,0:T(8,128)S(1)}, f32[64,128]{1,0:T(8,128)S(1)}) custom-call(s32[2]{0:T(128)S(1)} %pad_add_fusion.place.after, f32[6,3,16,128]{3,2,1,0:T(8,128)S(1)} %get-tuple-element.17.state, s32[3,16,128]{2,1,0:T(8,128)S(1)} %get-tuple-element.18.switch, f32[2,6,3,16,128]{4,3,2,1,0:T(8,128)S(1)} %get-tuple-element.19.edges, ...), custom_call_target="tpu_custom_call" | custom-call | flops 4000000 | bytes 4000000 | tf_op jit(solution)/shard_map/second/pallas_call | solution.py:486
  28.7 3.1 %collective-permute-start.1 = (f32[64,128]{1,0:T(8,128)S(1)}, f32[64,128]{1,0:T(8,128)S(1)}, u32[]{:S(2)}, u32[]{:S(2)}) collective-permute-start(f32[64,128]{1,0:T(8,128)S(1)} %get-tuple-element.22), channel_id=1, source_target_pairs={{0,1},{1,0},{2,3},{3,2},{4,5},{5,4},{6,7},{7,6},{8,9},{9,8},{10,11... | collective-permute-start | bytes 98312 | tf_op jit(solution)/shard_map/ppermute | solution.py:557
  31.8 13.5 %collective-permute-start.2 = (f32[64,128]{1,0:T(8,128)S(1)}, f32[64,128]{1,0:T(8,128)S(1)}, u32[]{:S(2)}, u32[]{:S(2)}) collective-permute-start(f32[64,128]{1,0:T(8,128)S(1)} %get-tuple-element.23), channel_id=1, source_target_pairs={{1,2},{2,1},{3,4},{4,3},{5,6},{6,5},{7,8},{8,7},{9,10},{10,9},{11,... | collective-permute-start | bytes 98312 | tf_op jit(solution)/shard_map/ppermute | solution.py:558
  45.3 0.0 all-to-all-done.rows
  45.3 0.0 collective-permute-done.1.after.even_in
  45.3 0.6 %spread.3 = f32[12,2,128]{2,1,0:T(2,128)} custom-call(f32[32,2,128]{2,1,0:T(2,128)S(1)} %all-to-all-done.rows, f32[64,128]{1,0:T(8,128)S(1)} %collective-permute-done.1.after.even_in), custom_call_target="tpu_custom_call" | custom-call | tf_op jit(solution)/shard_map/spread/pallas_call | solution.py:508
  45.9 3.5 %all-to-all-start.1 = ((f32[12,2,128]{2,1,0:T(2,128)}), f32[12,2,128]{2,1,0:T(2,128)S(1)}, u32[]{:S(2)}, u32[]{:S(2)}) async-start(f32[12,2,128]{2,1,0:T(2,128)} %spread.3), calls=%async_computation.1 | async-start | bytes 24576 | tf_op jit(solution)/shard_map/all_to_all | solution.py:516
  49.4 0.0 collective-permute-done.2.odd_y_in
  49.5 8.1 %third.1 = (f32[2,21,32,128]{3,2,1,0:T(8,128)S(1)}, f32[2,9,32,128]{3,2,1,0:T(8,128)S(1)}, f32[2,18,32,128]{3,2,1,0:T(8,128)S(1)}) custom-call(s32[2]{0:T(128)S(1)} %pad_add_fusion.place.after, f32[6,3,16,128]{3,2,1,0:T(8,128)S(1)} %get-tuple-element.17.state, s32[3,16,128]{2,1,0:T(8,128)S(1)} %get-tuple-element.18.switch, ...), custom_call_target="tpu_custom_call" | custom-call | flops 60000000 | bytes 60000000 | tf_op jit(solution)/shard_map/third/pallas_call | solution.py:486
  57.6 0.7 %all-to-all-done.1.totals = f32[12,2,128]{2,1,0:T(2,128)S(1)} async-done(((f32[12,2,128]{2,1,0:T(2,128)}), f32[12,2,128]{2,1,0:T(2,128)S(1)}, u32[]{:S(2)}, u32[]{:S(2)}) %all-to-all-start.1) | async-done | bytes 12320 | tf_op jit(solution)/shard_map/all_to_all | solution.py:516
  58.3 2.8 %fourth.1 = f32[6,3,16,128]{3,2,1,0:T(8,128)} custom-call(f32[12,2,128]{2,1,0:T(2,128)S(1)} %all-to-all-done.1.totals, f32[2,21,32,128]{3,2,1,0:T(8,128)S(1)} %get-tuple-element.24.fields, f32[2,9,32,128]{3,2,1,0:T(8,128)S(1)} %get-tuple-element.25.force, f32[2,18,32,128]{3,2,1,0:T(8,128)S(1)} %get-tuple-element.26.tend, ...), custom_call_target="tpu_custom_call" | custom-call | flops 8000000 | bytes 8000000 | tf_op jit(solution)/shard_map/fourth/pallas_call | solution.py:486
  (1 shorter events, 0.0 us)
Async XLA Ops:
  1.9 25.8 %collective-permute-start = (f32[66,8,128]{2,1,0:T(8,128)S(1)}, f32[66,8,128]{2,1,0:T(8,128)S(1)}, u32[]{:S(2)}, u32[]{:S(2)}) collective-permute-start(f32[66,8,128]{2,1,0:T(8,128)S(1)} %get-tuple-element.21), channel_id=1, source_target_pairs={{64,128},{128,64},{192,256},{256,192},{320,384},{384,320},{448,512... | collective-permute-start | bytes 811016 | tf_op jit(solution)/shard_map/ppermute | solution.py:547
  18.0 27.3 %all-to-all-start = ((f32[32,2,128]{2,1,0:T(2,128)}), f32[32,2,128]{2,1,0:T(2,128)S(1)}, u32[]{:S(2)}, u32[]{:S(2)}) async-start(f32[32,2,128]{2,1,0:T(2,128)} %spread.2), calls=%async_computation | async-start | bytes 65536 | tf_op jit(solution)/shard_map/all_to_all | solution.py:516
  28.7 16.6 %collective-permute-start.1 = (f32[64,128]{1,0:T(8,128)S(1)}, f32[64,128]{1,0:T(8,128)S(1)}, u32[]{:S(2)}, u32[]{:S(2)}) collective-permute-start(f32[64,128]{1,0:T(8,128)S(1)} %get-tuple-element.22), channel_id=1, source_target_pairs={{0,1},{1,0},{2,3},{3,2},{4,5},{5,4},{6,7},{7,6},{8,9},{9,8},{10,11... | collective-permute-start | bytes 98312 | tf_op jit(solution)/shard_map/ppermute | solution.py:557
  31.8 17.6 %collective-permute-start.2 = (f32[64,128]{1,0:T(8,128)S(1)}, f32[64,128]{1,0:T(8,128)S(1)}, u32[]{:S(2)}, u32[]{:S(2)}) collective-permute-start(f32[64,128]{1,0:T(8,128)S(1)} %get-tuple-element.23), channel_id=1, source_target_pairs={{1,2},{2,1},{3,4},{4,3},{5,6},{6,5},{7,8},{8,7},{9,10},{10,9},{11,... | collective-permute-start | bytes 98312 | tf_op jit(solution)/shard_map/ppermute | solution.py:558
  45.9 12.4 %all-to-all-start.1 = ((f32[12,2,128]{2,1,0:T(2,128)}), f32[12,2,128]{2,1,0:T(2,128)S(1)}, u32[]{:S(2)}, u32[]{:S(2)}) async-start(f32[12,2,128]{2,1,0:T(2,128)} %spread.3), calls=%async_computation.1 | async-start | bytes 24576 | tf_op jit(solution)/shard_map/all_to_all | solution.py:516

commit v3 on v2

v3 whole, which is shorter than its diff:
```python
import functools

import jax
import jax.numpy as jnp
from jax import lax
from jax.experimental import pallas as pl
from jax.experimental.pallas import tpu as pltpu
from jax.sharding import Mesh
from jax.sharding import PartitionSpec as P

ADIABATIC = 5.0 / 3.0
CFL_NUMBER = 0.4
INJECTION = 0.04
LANES = 128
ROWS = 16
EXT = 32
FIELDS = 21
EDGES = 36
FORCES = 9
X_TILES = FIELDS + EDGES + FORCES
VMEM_LIMIT = 16 * 1024 * 1024
F32 = jnp.float32


def lane_index(shape):
    return lax.broadcasted_iota(jnp.int32, shape, len(shape) - 1)


def roll(values, shift, axis):
    size = values.shape[axis]
    shift = shift % size
    return values if shift == 0 else pltpu.roll(values, shift, axis)


def each(count, body):
    def step(index, carry):
        body(index)
        return carry

    lax.fori_loop(0, count, step, 0)


def x_place(refs, index):
    state, switch, edges, forcing = refs
    if index < 18:
        return lambda rows: state[index, rows, :]
    index -= 18
    if index < 3:
        return lambda rows: switch[index, rows, :].astype(F32)
    index -= 3
    if index < EDGES:
        return lambda rows: edges[index, rows, :]
    index -= EDGES
    return lambda rows: forcing[index, rows, :]


def first_kernel(
    place, state_in, switch_in, edges_in, forcing_in,
    pair_out, odd_out, state, switch, edges, forcing, arrived,
):
    refs = (state, switch, edges, forcing)
    copies = [
        pltpu.make_async_copy(source, target, arrived.at[k])
        for k, (source, target) in enumerate(
            zip((state_in, switch_in, edges_in, forcing_in), refs, strict=True)
        )
    ]
    for copy in copies:
        copy.start()
    odd = place[0]
    near = pl.multiple_of(8 * (1 - odd), 8)
    far = pl.multiple_of(8 * odd, 8)
    for copy in copies:
        copy.wait()
    peak = None
    total = None
    for plane in range(3):
        fields = [state[3 * k + plane] for k in range(6)]
        density = fields[0]
        inverse = 1.0 / density
        kinetic = 0.5 * inverse * (fields[1] ** 2 + fields[2] ** 2 + fields[3] ** 2)
        heat = jnp.where(switch[plane] == 1, fields[5], fields[4] - kinetic)
        sound = jnp.sqrt(ADIABATIC * (ADIABATIC - 1.0) * heat * inverse)
        speed = (
            jnp.abs(fields[1]) + jnp.abs(fields[2]) + jnp.abs(fields[3])
        ) * inverse + 3.0 * sound
        drive = [forcing[3 * k + plane] for k in range(3)]
        power = density * (drive[0] ** 2 + drive[1] ** 2 + drive[2] ** 2)
        peak = speed if peak is None else jnp.maximum(peak, speed)
        total = power if total is None else total + power
    for index in range(X_TILES):
        tile = x_place(refs, index)
        pair_out[index] = tile(pl.ds(near, 8))
        odd_out[index] = tile(pl.ds(far, 8))
    row = lax.broadcasted_iota(jnp.int32, (8, LANES), 0)
    pair_out[X_TILES] = jnp.where(row == 0, jnp.max(peak), jnp.sum(total))


def spread_kernel(rows, after, out):
    peak = jnp.max(rows[:, 0, :], axis=0, keepdims=True)
    total = jnp.sum(rows[:, 1, :], axis=0, keepdims=True)
    joined = jnp.concatenate([peak, total], axis=0)
    out[...] = jnp.broadcast_to(joined[None], out.shape)


def rows_around(odd_x, pair_in, odd_in, index, block):
    from_pair = pair_in[1 - odd_x, index]
    from_odd = odd_in[index]
    below = jnp.where(odd_x == 0, from_odd, from_pair)
    above = jnp.where(odd_x == 0, from_pair, from_odd)
    return jnp.concatenate([below, block, above], axis=0)


def turned(values, shift):
    return pltpu.roll(values, lax.rem(shift + LANES, LANES), 1)


def second_kernel(place, state, switch, edges, forcing, pair_in, odd_in, even_out, odd_out):
    odd_x = place[0]
    odd_y = place[1]
    lane = lane_index((EXT, LANES))

    def columns(index, block, sums):
        column = rows_around(odd_x, pair_in, odd_in, index, block)
        mine = (lane >= 6 * index) & (lane < 6 * index + 6)
        return (
            jnp.where(mine, turned(column, 6 * index - 122), sums[0]),
            jnp.where(mine, turned(column, 6 * index), sums[1]),
        )

    def state_columns(field, sums):
        for plane in range(3):
            index = 3 * field + plane
            sums = columns(index, state[index], sums)
        return sums

    blank = jnp.zeros((EXT, LANES), F32)
    sums = lax.fori_loop(0, 6, state_columns, (blank, blank))
    for plane in range(3):
        sums = columns(18 + plane, switch[plane].astype(F32), sums)
    high, low = sums
    even_out[0:EXT] = jnp.where(odd_y == 0, high, low)
    odd_out[0:EXT] = jnp.where(odd_y == 0, low, high)

    lane = lane[0:ROWS]
    blank = blank[0:ROWS]
    for source, count, row in ((edges, EDGES, EXT), (forcing, FORCES, EXT + ROWS)):

        def three(step, sums, source=source):
            for k in range(3):
                index = 3 * step + k
                block = source[index]
                mine = (lane >= 3 * index) & (lane < 3 * index + 3)
                sums = (
                    jnp.where(mine, turned(block, 3 * index - 125), sums[0]),
                    jnp.where(mine, turned(block, 3 * index), sums[1]),
                )
            return sums

        high, low = lax.fori_loop(0, count // 3, three, (blank, blank))
        even_out[row : row + ROWS] = jnp.where(odd_y == 0, high, low)
        odd_out[row : row + ROWS] = jnp.where(odd_y == 0, low, high)


def face_above(before, here, after, beyond):
    value = (7.0 / 12.0) * (here + after) - (1.0 / 12.0) * (before + beyond)
    return jnp.minimum(
        jnp.maximum(value, jnp.minimum(here, after)), jnp.maximum(here, after)
    )


def limited(here, face_low, face_high):
    low_dev = face_low - here
    high_dev = face_high - here
    opposite = low_dev * high_dev < 0.0
    low_span = 2.0 * jnp.abs(low_dev)
    high_span = 2.0 * jnp.abs(high_dev)
    low_dev = jnp.minimum(jnp.maximum(low_dev, -high_span), high_span)
    high_dev = jnp.minimum(jnp.maximum(high_dev, -low_span), low_span)
    return jnp.where(opposite, here + low_dev, here), jnp.where(opposite, here + high_dev, here)


def face_flux(left, right, normal):
    left_u, right_u = left[1 + normal], right[1 + normal]
    left_sound = jnp.sqrt(ADIABATIC * left[4] / left[0])
    right_sound = jnp.sqrt(ADIABATIC * right[4] / right[0])
    slow = jnp.minimum(jnp.minimum(left_u - left_sound, right_u - right_sound), 0.0)
    fast = jnp.maximum(jnp.maximum(left_u + left_sound, right_u + right_sound), 0.0)
    share = 1.0 / (fast - slow)
    left_part = fast * share
    right_part = -slow * share
    left_rate = left_part * (left_u - slow)
    right_rate = right_part * (right_u - fast)
    left_mass = left_rate * left[0]
    right_mass = right_rate * right[0]
    left_square = left[1] * left[1] + left[2] * left[2] + left[3] * left[3]
    right_square = right[1] * right[1] + right[2] * right[2] + right[3] * right[3]
    flux = [left_mass + right_mass]
    for k in (1, 2, 3):
        flux.append(left_mass * left[k] + right_mass * right[k])
    left_push = left_part * left[4]
    right_push = right_part * right[4]
    flux[1 + normal] = flux[1 + normal] + (left_push + right_push)
    flux.append(
        0.5 * (left_mass * left_square + right_mass * right_square)
        + left[4] * (1.5 * left_rate)
        + right[4] * (1.5 * right_rate)
        + left_push * left_u
        + right_push * right_u
    )
    flux.append(left_mass * left[5] + right_mass * right[5])
    return flux


def z_fluxes(planes):
    lower, upper = [], []
    for k in range(6):
        column = [planes[j][k] for j in range(9)]
        faces = [face_above(*column[j : j + 4]) for j in range(6)]
        cells = [limited(column[j + 2], faces[j], faces[j + 1]) for j in range(5)]
        lower.append([cells[j][1] for j in range(4)])
        upper.append([cells[j + 1][0] for j in range(4)])
    return [
        face_flux([lower[k][j] for k in range(6)], [upper[k][j] for k in range(6)], 2)
        for j in range(4)
    ]


def edge_primitives(fields):
    density = fields[0]
    inverse = 1.0 / density
    kinetic = 0.5 * inverse * (fields[1] ** 2 + fields[2] ** 2 + fields[3] ** 2)
    return [
        density,
        fields[1] * inverse,
        fields[2] * inverse,
        fields[3] * inverse,
        (ADIABATIC - 1.0) * (fields[4] - kinetic),
        fields[5] * inverse,
    ]


def shift_pair(main, rim, step):
    lane = lane_index(main.shape)
    main_rolled = roll(main, -step, 1)
    rim_rolled = roll(rim, -step, 1)
    inside = lane < LANES - step if step > 0 else lane >= -step
    return (
        jnp.where(inside, main_rolled, rim_rolled),
        jnp.where(inside, rim_rolled, main_rolled),
    )


def y_differences(main, rim):
    lows, highs = ([], []), ([], [])
    spread = None
    for k in range(6):
        here = (main[k], rim[k])
        before = shift_pair(*here, -1)
        after = shift_pair(*here, 1)
        beyond = shift_pair(*here, 2)
        faces = [face_above(before[j], here[j], after[j], beyond[j]) for j in range(2)]
        below = shift_pair(*faces, -1)
        cells = [limited(here[j], below[j], faces[j]) for j in range(2)]
        nexts = shift_pair(cells[0][0], cells[1][0], 1)
        for j in range(2):
            lows[j].append(cells[j][1])
            highs[j].append(nexts[j])
        if k == 2:
            spread = [0.5 * (after[j] - before[j]) for j in range(2)]
    fluxes = [face_flux(lows[j], highs[j], 1) for j in range(2)]
    differences = ([], [])
    for k in range(6):
        below = shift_pair(fluxes[0][k], fluxes[1][k], -1)
        for j in range(2):
            differences[j].append(fluxes[j][k] - below[j])
    return differences, spread


CHUNKS = (4, 12, 20)


def x_sweep(prims, low_ref, high_ref, face_ref, flux_ref):
    for row in CHUNKS:
        for k in range(6):
            before, here, after, beyond = [
                prims[k, pl.ds(row + s, 8), :] for s in (-1, 0, 1, 2)
            ]
            if row == CHUNKS[0]:
                below = face_above(prims[k, pl.ds(row - 2, 8), :], before, here, after)
            above = face_above(before, here, after, beyond)
            face_ref[k, pl.ds(row, 8), :] = above
            if row != CHUNKS[0]:
                below = face_ref[k, pl.ds(row - 1, 8), :]
            low_ref[k, pl.ds(row, 8), :], high_ref[k, pl.ds(row, 8), :] = limited(
                here, below, above
            )
    for row in CHUNKS:
        left = [high_ref[k, pl.ds(row, 8), :] for k in range(6)]
        right = [low_ref[k, pl.ds(row + 1, 8), :] for k in range(6)]
        flux = face_flux(left, right, 0)
        for k in range(6):
            flux_ref[k, pl.ds(row, 8), :] = flux[k]


def clear_ends(low_ref, flux_ref):
    for k in range(6):
        low_ref[k, pl.ds(28, 4), :] = jnp.ones((4, LANES), F32)
        flux_ref[k, pl.ds(0, 4), :] = jnp.zeros((4, LANES), F32)


def third_kernel(
    place, state, switch, edges, forcing, pair_in, odd_in, even_in, odd_y_in,
    fields, force, tend, prims, planes, low_ref, high_ref, face_ref, flux_ref, strip_ref,
):
    odd_x = place[0]
    odd_y = place[1]
    strip_ref[0] = jnp.where(odd_y == 0, even_in[...], odd_y_in[...])
    strip_ref[1] = jnp.where(odd_y == 0, odd_y_in[...], even_in[...])
    clear_ends(low_ref, flux_ref)
    lane = lane_index((EXT, LANES))
    edge_lane = lane[0:ROWS]

    def field_tiles(index, block):
        fields[0, index] = rows_around(odd_x, pair_in, odd_in, index, block)
        fields[1, index] = jnp.where(
            lane < 64,
            turned(strip_ref[0, 0:EXT], -6 * index),
            turned(strip_ref[1, 0:EXT], 122 - 6 * index),
        )

    def rim_tile(row, index):
        return jnp.where(
            edge_lane < 64,
            turned(strip_ref[0, row : row + ROWS], -3 * index),
            turned(strip_ref[1, row : row + ROWS], 125 - 3 * index),
        )

    @functools.partial(each, 6)
    def _(field):
        for plane in range(3):
            index = 3 * field + plane
            field_tiles(index, state[index])

    for plane in range(3):
        field_tiles(18 + plane, switch[plane].astype(F32))

    @functools.partial(each, 3)
    def _(part):
        for k in range(3):
            index = 3 * part + k
            force[0, index] = rows_around(
                odd_x, pair_in, odd_in, FIELDS + EDGES + index, forcing[index]
            )
            force[1, index, 0:8] = jnp.zeros((8, LANES), F32)
            force[1, index, 8:24] = rim_tile(EXT + ROWS, index)
            force[1, index, 24:32] = jnp.zeros((8, LANES), F32)

    @functools.partial(each, 6)
    def _(step):
        tile, plane = step // 3, step % 3
        values = [fields[tile, 3 * k + plane] for k in range(7)]
        density = values[0]
        inverse = 1.0 / density
        kinetic = 0.5 * inverse * (values[1] ** 2 + values[2] ** 2 + values[3] ** 2)
        heat = jnp.where(values[6] == 1.0, values[5], values[4] - kinetic)
        prims[tile, plane, 0] = density
        for k in (1, 2, 3):
            prims[tile, plane, k] = values[k] * inverse
        prims[tile, plane, 4] = (ADIABATIC - 1.0) * heat
        prims[tile, plane, 5] = values[5] * inverse

    @functools.partial(each, 6)
    def _(step):
        first = 18 * (step // 3) + step % 3
        places = [first + 3 * k for k in range(6)]
        values = edge_primitives(
            [rows_around(odd_x, pair_in, odd_in, FIELDS + k, edges[k]) for k in places]
        )
        for k in range(6):
            planes[0, step, k] = values[k]
        values = edge_primitives([rim_tile(EXT, k) for k in places])
        for k in range(6):
            planes[1, step, k, 0:8] = jnp.ones((8, LANES), F32)
            planes[1, step, k, 8:24] = values[k]
            planes[1, step, k, 24:32] = jnp.ones((8, LANES), F32)

    @functools.partial(each, 3)
    def _(plane):
        for row in CHUNKS:
            rows = pl.ds(row, 8)
            both = [[prims[tile, plane, k, rows, :] for k in range(6)] for tile in range(2)]
            differences, spread = y_differences(*both)
            for tile in range(2):
                for k in range(5):
                    tend[tile, 3 * k + plane, rows, :] = -differences[tile][k]
                tend[tile, 15 + plane, rows, :] = (
                    -differences[tile][5] - both[tile][4] * spread[tile]
                )

    @functools.partial(each, 6)
    def _(step):
        tile, plane = step // 3, step % 3
        x_sweep(prims.at[tile, plane], low_ref, high_ref, face_ref, flux_ref)
        for row in CHUNKS:
            rows = pl.ds(row, 8)
            for k in range(6):
                difference = flux_ref[k, rows, :] - flux_ref[k, pl.ds(row - 1, 8), :]
                if k == 5:
                    before = prims[tile, plane, 1, pl.ds(row - 1, 8), :]
                    after = prims[tile, plane, 1, pl.ds(row + 1, 8), :]
                    spread = 0.5 * (after - before)
                    difference = difference + prims[tile, plane, 4, rows, :] * spread
                tend[tile, 3 * k + plane, rows, :] -= difference

    @functools.partial(each, 2)
    def _(tile):
        for row in CHUNKS:
            rows = pl.ds(row, 8)
            column = (
                [[planes[tile, p, k, rows, :] for k in range(6)] for p in range(3)]
                + [[prims[tile, p, k, rows, :] for k in range(6)] for p in range(3)]
                + [[planes[tile, 3 + p, k, rows, :] for k in range(6)] for p in range(3)]
            )
            flux = z_fluxes(column)
            for plane in range(3):
                for k in range(6):
                    difference = flux[plane + 1][k] - flux[plane][k]
                    if k == 5:
                        spread = 0.5 * (column[plane + 4][3] - column[plane + 2][3])
                        difference = difference + column[plane + 3][4] * spread
                    tend[tile, 3 * k + plane, rows, :] -= difference


def fourth_kernel(
    cells, totals, fields, force, tend, edges, updated,
    section, prims, low_ref, high_ref, face_ref, flux_ref,
):
    peak = jnp.max(totals[:, 0, :], axis=0, keepdims=True)
    power = jnp.sum(totals[:, 1, :], axis=0, keepdims=True)
    time_step = CFL_NUMBER / peak
    scale = jnp.sqrt(INJECTION / (0.5 * time_step * (power / cells + 1e-06)))
    clear_ends(low_ref, flux_ref)

    def forced(values, drive, tendency):
        result = list(tendency)
        for k in (1, 2, 3):
            result[k] = result[k] + scale * values[0] * drive[k - 1]
        result[4] = result[4] + scale * (
            values[1] * drive[0] + values[2] * drive[1] + values[3] * drive[2]
        )
        return result

    def settle(values, switch, inverse):
        kinetic = 0.5 * inverse * (values[1] ** 2 + values[2] ** 2 + values[3] ** 2)
        values[5] = jnp.where(switch == 0.0, values[4] - kinetic, values[5])

    @functools.partial(each, 6)
    def _(step):
        tile, plane = step // 3, step % 3
        for row in CHUNKS:
            rows = pl.ds(row, 8)
            values = [fields[tile, 3 * k + plane, rows, :] for k in range(7)]
            drive = [force[tile, 3 * k + plane, rows, :] for k in range(3)]
            rate = forced(values, drive, [tend[tile, 3 * k + plane, rows, :] for k in range(6)])
            stage = [values[k] + time_step * rate[k] for k in range(6)]
            inverse = 1.0 / stage[0]
            settle(stage, values[6], inverse)
            for k in range(6):
                section[tile, plane, k, rows, :] = stage[k]
            prims[tile, plane, 0, rows, :] = stage[0]
            for k in (1, 2, 3):
                prims[tile, plane, k, rows, :] = stage[k] * inverse
            prims[tile, plane, 4, rows, :] = (ADIABATIC - 1.0) * stage[5]
            prims[tile, plane, 5, rows, :] = stage[5] * inverse

    @functools.partial(each, 2)
    def _(step):
        inner = pl.ds(pl.multiple_of(8 * step, 8), 8)
        rows = pl.ds(pl.multiple_of(8 * step + 8, 8), 8)
        outer = [
            edge_primitives([edges[18 * side + 3 * k + plane, inner, :] for k in range(6)])
            for side in range(2)
            for plane in range(3)
        ]
        column = (
            outer[0:3] + [[prims[0, p, k, rows, :] for k in range(6)] for p in range(3)] + outer[3:6]
        )
        flux = z_fluxes(column)
        for plane in range(3):
            for k in range(6):
                difference = flux[plane + 1][k] - flux[plane][k]
                if k == 5:
                    spread = 0.5 * (column[plane + 4][3] - column[plane + 2][3])
                    difference = difference + column[plane + 3][4] * spread
                updated[k, plane, inner, :] = -difference

    @functools.partial(each, 3)
    def _(plane):
        x_sweep(prims.at[0, plane], low_ref, high_ref, face_ref, flux_ref)
        for row in (8, 16):
            rows = pl.ds(row, 8)
            inner = pl.ds(row - 8, 8)
            both = [[prims[tile, plane, k, rows, :] for k in range(6)] for tile in range(2)]
            differences, spread = y_differences(*both)
            before = prims[0, plane, 1, pl.ds(row - 1, 8), :]
            after = prims[0, plane, 1, pl.ds(row + 1, 8), :]
            spread = spread[0] + 0.5 * (after - before)
            rate = []
            for k in range(6):
                across = flux_ref[k, rows, :] - flux_ref[k, pl.ds(row - 1, 8), :]
                rate.append(updated[k, plane, inner, :] - differences[0][k] - across)
            rate[5] = rate[5] - both[0][4] * spread
            stage = [section[0, plane, k, rows, :] for k in range(6)]
            drive = [force[0, 3 * k + plane, rows, :] for k in range(3)]
            rate = forced(stage, drive, rate)
            values = [fields[0, 3 * k + plane, rows, :] for k in range(7)]
            result = [
                0.5 * values[k] + 0.5 * (stage[k] + time_step * rate[k]) for k in range(6)
            ]
            settle(result, values[6], 1.0 / result[0])
            for k in range(6):
                updated[k, plane, inner, :] = result[k]


def shape(*sizes):
    return jax.ShapeDtypeStruct(sizes, F32)


def vmem_specs(count):
    return [pl.BlockSpec(memory_space=pltpu.VMEM)] * count


def call(kernel, name, outs, scalars, arrays, scratch=(), cost=0):
    single = not isinstance(outs, tuple)
    return pl.pallas_call(
        kernel,
        out_shape=outs,
        in_specs=[pl.BlockSpec(memory_space=pltpu.SMEM)] * len(scalars) + vmem_specs(len(arrays)),
        out_specs=vmem_specs(1)[0] if single else tuple(vmem_specs(len(outs))),
        scratch_shapes=list(scratch),
        compiler_params=pltpu.CompilerParams(vmem_limit_bytes=VMEM_LIMIT),
        cost_estimate=pl.CostEstimate(flops=cost, bytes_accessed=cost, transcendentals=0),
        name=name,
    )(*scalars, *arrays)


def pairs(count, begin):
    table = []
    for first in range(begin, begin + count, 2):
        low, high = first % count, (first + 1) % count
        table += [(low, high), (high, low)]
    return table


def exchanged(rows, after, axes):
    count = lax.axis_size(axes)
    spread = pl.pallas_call(
        spread_kernel,
        out_shape=shape(count, 2, LANES),
        in_specs=[*vmem_specs(1), pl.BlockSpec(memory_space=pl.ANY)],
        out_specs=vmem_specs(1)[0],
        compiler_params=pltpu.CompilerParams(vmem_limit_bytes=VMEM_LIMIT),
        name="spread",
    )(rows, after)
    return lax.all_to_all(spread, axes, 0, 0, tiled=True)


GX = ("zl", "core")
GY = ("y", "zh", "x")


def local(fluid_state, switch, z_edges, forcing):
    count_x = lax.axis_size(GX)
    count_y = lax.axis_size(GY)
    cells = 3.0 * ROWS * LANES * count_x * count_y
    place = jnp.stack([lax.axis_index(GX) % 2, lax.axis_index(GY) % 2]).astype(jnp.int32)
    tile = (8, LANES)
    block = (ROWS, LANES)
    inputs = (
        fluid_state.reshape(18, *block),
        switch,
        z_edges.reshape(EDGES, *block),
        forcing.reshape(FORCES, *block),
    )
    pair_out, odd_out, *arrays = pl.pallas_call(
        first_kernel,
        out_shape=(
            shape(X_TILES + 1, *tile),
            shape(X_TILES, *tile),
            *(jax.ShapeDtypeStruct(values.shape, values.dtype) for values in inputs),
        ),
        in_specs=[
            pl.BlockSpec(memory_space=pltpu.SMEM),
            *([pl.BlockSpec(memory_space=pltpu.HBM)] * 4),
        ],
        out_specs=tuple(vmem_specs(6)),
        scratch_shapes=[pltpu.SemaphoreType.DMA((4,))],
        compiler_params=pltpu.CompilerParams(vmem_limit_bytes=VMEM_LIMIT),
        name="first",
    )(place, *(pltpu.with_memory_space_constraint(values, pltpu.HBM) for values in inputs))
    pair_in = lax.all_gather(pair_out, "core")
    odd_in = lax.ppermute(odd_out, GX, pairs(count_x, 1))
    totals = exchanged(pair_in[:, X_TILES, 0:2], place, ("y", "x"))
    strips = call(
        second_kernel,
        "second",
        (shape(EXT + 2 * ROWS, LANES), shape(EXT + 2 * ROWS, LANES)),
        (place,),
        (*arrays, pair_in, odd_in),
        cost=4_000_000,
    )
    even_in = lax.ppermute(strips[0], GY, pairs(count_y, 0))
    odd_y_in = lax.ppermute(strips[1], GY, pairs(count_y, 1))
    totals = exchanged(totals, even_in, ("zh", "zl"))
    extended = (EXT, LANES)
    work = [pltpu.VMEM((6, *extended), F32) for _ in range(4)]
    fields, force, tend = call(
        third_kernel,
        "third",
        (shape(2, FIELDS, *extended), shape(2, FORCES, *extended), shape(2, 18, *extended)),
        (place,),
        (*arrays, pair_in, odd_in, even_in, odd_y_in),
        [
            pltpu.VMEM((2, 3, 6, *extended), F32),
            pltpu.VMEM((2, 6, 6, *extended), F32),
            *work,
            pltpu.VMEM((2, EXT + 2 * ROWS, LANES), F32),
        ],
        cost=60_000_000,
    )
    return call(
        functools.partial(fourth_kernel, cells),
        "fourth",
        shape(6, 3, ROWS, LANES),
        (),
        (totals, fields, force, tend, arrays[2]),
        [
            pltpu.VMEM((2, 3, 6, *extended), F32),
            pltpu.VMEM((2, 3, 6, *extended), F32),
            *work,
        ],
        cost=8_000_000,
    )


def solution(mesh):
    count_x, count_y = mesh.devices.shape
    count_z = 2 if count_y % 8 == 0 else 1
    parts = (count_x // 2, 2, count_y // (4 * count_z), count_z, 4)
    split = Mesh(mesh.devices.reshape(parts), (*GX, *GY))
    return jax.shard_map(
        local,
        mesh=split,
        in_specs=(
            P(None, None, GX, GY),
            P(None, GX, GY),
            P(None, None, None, GX, GY),
            P(None, None, GX, GY),
        ),
        out_specs=P(None, None, GX, GY),
        check_vma=False,
    )
```

time: 61.4 us -> 62.7 us (1.021)
  waiting for transfers between devices: 0.73 us -> 3.46 us
  Pallas kernels: 14.9 us -> 13.5 us
    all_to_all x2, waiting for transfers between devices: 0.73 us -> 3.45 us  [exchanged(): return lax.all_to_all(spread, axes, 0, 0, tiled=True)]
    pallas_call x3, Pallas kernels: 11.9 us -> 10.4 us  [call(): pl.pallas_call(kernel, out_shape=outs, in_specs=[pl.BlockSpec(memory_spac...]
  transfers between devices with their start and end apart: 5 -> 5, of which waited for: 1 -> 1; matrix products, arithmetic and copies ran while one was open for 0% -> 0% of each run, Pallas kernels for 17% -> 15%
where the time goes in v3:
time: 62.7 us; the launch traced here: 62.3 us
  starting transfers between devices  35.1 us (56%)
  Pallas kernels  13.5 us (22%)
  blocking collectives  10.1 us (16%)
  waiting for transfers between devices  3.46 us (6%)
    ppermute x1, starting transfers between devices, local(): odd_y_in = lax.ppermute(strips[1], GY, pairs(count_y, 1))  13.5 us
    all_to_all x2, starting transfers between devices, exchanged(): return lax.all_to_all(spread, axes, 0, 0, tiled=True)  13.2 us
    pallas_call x3, Pallas kernels, call(): pl.pallas_call(kernel, out_shape=outs, in_specs=[pl.BlockSpec(memory_spac...  10.4 us
    all_gather x1, blocking collectives, local(): pair_in = lax.all_gather(pair_out, 'core')  10.1 us
    ppermute x1, starting transfers between devices, local(): odd_in = lax.ppermute(odd_out, GX, pairs(count_x, 1))  5.39 us
    all_to_all x2, waiting for transfers between devices, exchanged(): return lax.all_to_all(spread, axes, 0, 0, tiled=True)  3.45 us
    ppermute x1, starting transfers between devices, local(): even_in = lax.ppermute(strips[0], GY, pairs(count_y, 0))  3.14 us
    pallas_call x1, Pallas kernels, local(): pl.pallas_call(first_kernel, out_shape=(shape(X_TILES + 1, *tile), shape(...  1.79 us
  transfers between devices with their start and end apart: 5, of which 1 were waited for; matrix products, arithmetic and copies ran while one was open for 0% of the time, Pallas kernels for 15%

profile of v3, /device:TPU:1, one launch (start us, length us, event | category | flops | bytes accessed | tf_op | source)
XLA Modules:
  0.0 62.3 jit_solution(16139279023017021459)
XLA Ops:
  0.0 0.1 pad_add_fusion.place.after
  0.1 1.8 %first.1 = (f32[67,8,128]{2,1,0:T(8,128)S(1)}, f32[66,8,128]{2,1,0:T(8,128)S(1)}, f32[18,16,128]{2,1,0:T(8,128)S(1)}, s32[3,16,128]{2,1,0:T(8,128)S(1)}, f32[36,...) custom-call(s32[2]{0:T(128)S(1)} %pad_add_fusion.place.after, f32[18,16,128]{2,1,0:T(8,128)} %bitcast.12, ...), custom_call_target="tpu_custom_call" | custom-call | tf_op jit(solution)/shard_map/first/pallas_call | solution.py:586
  1.9 5.4 %collective-permute-start = (f32[66,8,128]{2,1,0:T(8,128)S(1)}, f32[66,8,128]{2,1,0:T(8,128)S(1)}, u32[]{:S(2)}, u32[]{:S(2)}) collective-permute-start(f32[66,8,128]{2,1,0:T(8,128)S(1)} %get-tuple-element.21), channel_id=1, source_target_pairs={{64,128},{128,64},{192,256},{256,192},{320,384},{384,320},{448,512... | collective-permute-start | bytes 811016 | tf_op jit(solution)/shard_map/ppermute | solution.py:603
  7.3 10.1 %all-gather = f32[134,8,128]{2,1,0:T(8,128)S(1)} all-gather(f32[67,8,128]{2,1,0:T(8,128)S(1)} %get-tuple-element.16), channel_id=2, replica_groups=mesh['zl'=6,'core'=2,'y'=8,'zh'=2,'x'=4] {'core'}, dimensions={0}, use_global_device_ids=true | all-gather | bytes 823296 | tf_op jit(solution)/shard_map/all_gather | solution.py:602
  17.4 0.6 %spread.2 = f32[32,2,128]{2,1,0:T(2,128)} custom-call(f32[2,2,128]{2,1,0:T(2,128)S(1)} %slice_bitcast_fusion.rows, s32[2]{0:T(128)S(1)} %pad_add_fusion.place.after), custom_call_target="tpu_custom_call" | custom-call | tf_op jit(solution)/shard_map/spread/pallas_call | solution.py:558
  18.0 9.7 %all-to-all-start = ((f32[32,2,128]{2,1,0:T(2,128)}), f32[32,2,128]{2,1,0:T(2,128)S(1)}, u32[]{:S(2)}, u32[]{:S(2)}) async-start(f32[32,2,128]{2,1,0:T(2,128)} %spread.2), calls=%async_computation | async-start | bytes 65536 | tf_op jit(solution)/shard_map/all_to_all | solution.py:566
  27.7 0.0 collective-permute-done.odd_in
  27.7 2.4 %second.1 = (f32[64,128]{1,0:T(8,128)S(1)}, f32[64,128]{1,0:T(8,128)S(1)}) custom-call(s32[2]{0:T(128)S(1)} %pad_add_fusion.place.after, f32[18,16,128]{2,1,0:T(8,128)S(1)} %get-tuple-element.17.state, s32[3,16,128]{2,1,0:T(8,128)S(1)} %get-tuple-element.18.switch, f32[36,16,128]{2,1,0:T(8,128)S(1)} %get-tuple-element.19.edges, ...), custom_call_target="tpu_custom_call" | custom-call | flops 4000000 | bytes 4000000 | tf_op jit(solution)/shard_map/second/pallas_call | solution.py:536
  30.1 3.1 %collective-permute-start.1 = (f32[64,128]{1,0:T(8,128)S(1)}, f32[64,128]{1,0:T(8,128)S(1)}, u32[]{:S(2)}, u32[]{:S(2)}) collective-permute-start(f32[64,128]{1,0:T(8,128)S(1)} %get-tuple-element.22), channel_id=1, source_target_pairs={{0,1},{1,0},{2,3},{3,2},{4,5},{5,4},{6,7},{7,6},{8,9},{9,8},{10,11... | collective-permute-start | bytes 98312 | tf_op jit(solution)/shard_map/ppermute | solution.py:613
  33.3 13.5 %collective-permute-start.2 = (f32[64,128]{1,0:T(8,128)S(1)}, f32[64,128]{1,0:T(8,128)S(1)}, u32[]{:S(2)}, u32[]{:S(2)}) collective-permute-start(f32[64,128]{1,0:T(8,128)S(1)} %get-tuple-element.23), channel_id=1, source_target_pairs={{1,2},{2,1},{3,4},{4,3},{5,6},{6,5},{7,8},{8,7},{9,10},{10,9},{11,... | collective-permute-start | bytes 98312 | tf_op jit(solution)/shard_map/ppermute | solution.py:614
  46.7 0.0 all-to-all-done.rows
  46.8 0.0 collective-permute-done.1.after.even_in
  46.8 0.6 %spread.3 = f32[12,2,128]{2,1,0:T(2,128)} custom-call(f32[32,2,128]{2,1,0:T(2,128)S(1)} %all-to-all-done.rows, f32[64,128]{1,0:T(8,128)S(1)} %collective-permute-done.1.after.even_in), custom_call_target="tpu_custom_call" | custom-call | tf_op jit(solution)/shard_map/spread/pallas_call | solution.py:558
  47.4 3.5 %all-to-all-start.1 = ((f32[12,2,128]{2,1,0:T(2,128)}), f32[12,2,128]{2,1,0:T(2,128)S(1)}, u32[]{:S(2)}, u32[]{:S(2)}) async-start(f32[12,2,128]{2,1,0:T(2,128)} %spread.3), calls=%async_computation.1 | async-start | bytes 24576 | tf_op jit(solution)/shard_map/all_to_all | solution.py:566
  50.9 0.0 collective-permute-done.2.odd_y_in
  50.9 5.4 %third.1 = (f32[2,21,32,128]{3,2,1,0:T(8,128)S(1)}, f32[2,9,32,128]{3,2,1,0:T(8,128)S(1)}, f32[2,18,32,128]{3,2,1,0:T(8,128)S(1)}) custom-call(s32[2]{0:T(128)S(1)} %pad_add_fusion.place.after, f32[18,16,128]{2,1,0:T(8,128)S(1)} %get-tuple-element.17.state, s32[3,16,128]{2,1,0:T(8,128)S(1)} %get-tuple-element.18.switch, ...), custom_call_target="tpu_custom_call" | custom-call | flops 60000000 | bytes 60000000 | tf_op jit(solution)/shard_map/third/pallas_call | solution.py:536
  56.3 3.4 %all-to-all-done.1.totals = f32[12,2,128]{2,1,0:T(2,128)S(1)} async-done(((f32[12,2,128]{2,1,0:T(2,128)}), f32[12,2,128]{2,1,0:T(2,128)S(1)}, u32[]{:S(2)}, u32[]{:S(2)}) %all-to-all-start.1) | async-done | bytes 12320 | tf_op jit(solution)/shard_map/all_to_all | solution.py:566
  59.8 2.6 %fourth.1 = f32[6,3,16,128]{3,2,1,0:T(8,128)} custom-call(f32[12,2,128]{2,1,0:T(2,128)S(1)} %all-to-all-done.1.totals, f32[2,21,32,128]{3,2,1,0:T(8,128)S(1)} %get-tuple-element.24.fields, f32[2,9,32,128]{3,2,1,0:T(8,128)S(1)} %get-tuple-element.25.force, f32[2,18,32,128]{3,2,1,0:T(8,128)S(1)} %get-tuple-element.26.tend, ...), custom_call_target="tpu_custom_call" | custom-call | flops 8000000 | bytes 8000000 | tf_op jit(solution)/shard_map/fourth/pallas_call | solution.py:536
  (1 shorter events, 0.0 us)
Async XLA Ops:
  1.9 25.8 %collective-permute-start = (f32[66,8,128]{2,1,0:T(8,128)S(1)}, f32[66,8,128]{2,1,0:T(8,128)S(1)}, u32[]{:S(2)}, u32[]{:S(2)}) collective-permute-start(f32[66,8,128]{2,1,0:T(8,128)S(1)} %get-tuple-element.21), channel_id=1, source_target_pairs={{64,128},{128,64},{192,256},{256,192},{320,384},{384,320},{448,512... | collective-permute-start | bytes 811016 | tf_op jit(solution)/shard_map/ppermute | solution.py:603
  18.0 28.7 %all-to-all-start = ((f32[32,2,128]{2,1,0:T(2,128)}), f32[32,2,128]{2,1,0:T(2,128)S(1)}, u32[]{:S(2)}, u32[]{:S(2)}) async-start(f32[32,2,128]{2,1,0:T(2,128)} %spread.2), calls=%async_computation | async-start | bytes 65536 | tf_op jit(solution)/shard_map/all_to_all | solution.py:566
  30.1 16.6 %collective-permute-start.1 = (f32[64,128]{1,0:T(8,128)S(1)}, f32[64,128]{1,0:T(8,128)S(1)}, u32[]{:S(2)}, u32[]{:S(2)}) collective-permute-start(f32[64,128]{1,0:T(8,128)S(1)} %get-tuple-element.22), channel_id=1, source_target_pairs={{0,1},{1,0},{2,3},{3,2},{4,5},{5,4},{6,7},{7,6},{8,9},{9,8},{10,11... | collective-permute-start | bytes 98312 | tf_op jit(solution)/shard_map/ppermute | solution.py:613
  33.3 17.6 %collective-permute-start.2 = (f32[64,128]{1,0:T(8,128)S(1)}, f32[64,128]{1,0:T(8,128)S(1)}, u32[]{:S(2)}, u32[]{:S(2)}) collective-permute-start(f32[64,128]{1,0:T(8,128)S(1)} %get-tuple-element.23), channel_id=1, source_target_pairs={{1,2},{2,1},{3,4},{4,3},{5,6},{6,5},{7,8},{8,7},{9,10},{10,9},{11,... | collective-permute-start | bytes 98312 | tf_op jit(solution)/shard_map/ppermute | solution.py:614
  47.4 12.4 %all-to-all-start.1 = ((f32[12,2,128]{2,1,0:T(2,128)}), f32[12,2,128]{2,1,0:T(2,128)S(1)}, u32[]{:S(2)}, u32[]{:S(2)}) async-start(f32[12,2,128]{2,1,0:T(2,128)} %spread.3), calls=%async_computation.1 | async-start | bytes 24576 | tf_op jit(solution)/shard_map/all_to_all | solution.py:566

commit v4 on v3

--- a/solution.py
+++ b/solution.py
@@ -70,8 +70,8 @@
     odd = place[0]
     near = pl.multiple_of(8 * (1 - odd), 8)
     far = pl.multiple_of(8 * odd, 8)
-    for copy in copies:
-        copy.wait()
+    for k in (0, 1, 3):
+        copies[k].wait()
     peak = None
     total = None
     for plane in range(3):
@@ -88,12 +88,13 @@
         power = density * (drive[0] ** 2 + drive[1] ** 2 + drive[2] ** 2)
         peak = speed if peak is None else jnp.maximum(peak, speed)
         total = power if total is None else total + power
+    row = lax.broadcasted_iota(jnp.int32, (8, LANES), 0)
+    pair_out[X_TILES] = jnp.where(row == 0, jnp.max(peak), jnp.sum(total))
+    copies[2].wait()
     for index in range(X_TILES):
         tile = x_place(refs, index)
         pair_out[index] = tile(pl.ds(near, 8))
         odd_out[index] = tile(pl.ds(far, 8))
-    row = lax.broadcasted_iota(jnp.int32, (8, LANES), 0)
-    pair_out[X_TILES] = jnp.where(row == 0, jnp.max(peak), jnp.sum(total))
 
 
 def spread_kernel(rows, after, out):
@@ -119,80 +120,62 @@
     odd_x = place[0]
     odd_y = place[1]
     lane = lane_index((EXT, LANES))
-
-    def columns(index, block, sums):
+    high = jnp.zeros((EXT, LANES), F32)
+    low = jnp.zeros((EXT, LANES), F32)
+    for index in range(FIELDS):
+        block = x_place((state, switch, edges, forcing), index)(slice(0, ROWS))
         column = rows_around(odd_x, pair_in, odd_in, index, block)
         mine = (lane >= 6 * index) & (lane < 6 * index + 6)
-        return (
-            jnp.where(mine, turned(column, 6 * index - 122), sums[0]),
-            jnp.where(mine, turned(column, 6 * index), sums[1]),
-        )
-
-    def state_columns(field, sums):
-        for plane in range(3):
-            index = 3 * field + plane
-            sums = columns(index, state[index], sums)
-        return sums
-
-    blank = jnp.zeros((EXT, LANES), F32)
-    sums = lax.fori_loop(0, 6, state_columns, (blank, blank))
-    for plane in range(3):
-        sums = columns(18 + plane, switch[plane].astype(F32), sums)
-    high, low = sums
+        high = jnp.where(mine, roll(column, 6 * index - 122, 1), high)
+        low = jnp.where(mine, roll(column, 6 * index, 1), low)
     even_out[0:EXT] = jnp.where(odd_y == 0, high, low)
     odd_out[0:EXT] = jnp.where(odd_y == 0, low, high)
-
     lane = lane[0:ROWS]
-    blank = blank[0:ROWS]
     for source, count, row in ((edges, EDGES, EXT), (forcing, FORCES, EXT + ROWS)):
-
-        def three(step, sums, source=source):
-            for k in range(3):
-                index = 3 * step + k
-                block = source[index]
-                mine = (lane >= 3 * index) & (lane < 3 * index + 3)
-                sums = (
-                    jnp.where(mine, turned(block, 3 * index - 125), sums[0]),
-                    jnp.where(mine, turned(block, 3 * index), sums[1]),
-                )
-            return sums
-
-        high, low = lax.fori_loop(0, count // 3, three, (blank, blank))
+        high = jnp.zeros((ROWS, LANES), F32)
+        low = jnp.zeros((ROWS, LANES), F32)
+        for index in range(count):
+            mine = (lane >= 3 * index) & (lane < 3 * index + 3)
+            high = jnp.where(mine, roll(source[index], 3 * index - 125, 1), high)
+            low = jnp.where(mine, roll(source[index], 3 * index, 1), low)
         even_out[row : row + ROWS] = jnp.where(odd_y == 0, high, low)
         odd_out[row : row + ROWS] = jnp.where(odd_y == 0, low, high)
 
 
+def median(one, two, three):
+    return jnp.maximum(jnp.minimum(one, two), jnp.minimum(jnp.maximum(one, two), three))
+
+
 def face_above(before, here, after, beyond):
     value = (7.0 / 12.0) * (here + after) - (1.0 / 12.0) * (before + beyond)
-    return jnp.minimum(
-        jnp.maximum(value, jnp.minimum(here, after)), jnp.maximum(here, after)
-    )
+    return median(here, after, value)
 
 
 def limited(here, face_low, face_high):
-    low_dev = face_low - here
-    high_dev = face_high - here
-    opposite = low_dev * high_dev < 0.0
-    low_span = 2.0 * jnp.abs(low_dev)
-    high_span = 2.0 * jnp.abs(high_dev)
-    low_dev = jnp.minimum(jnp.maximum(low_dev, -high_span), high_span)
-    high_dev = jnp.minimum(jnp.maximum(high_dev, -low_span), low_span)
-    return jnp.where(opposite, here + low_dev, here), jnp.where(opposite, here + high_dev, here)
+    thrice = 3.0 * here
+    return (
+        median(here, face_low, thrice - (face_high + face_high)),
+        median(here, face_high, thrice - (face_low + face_low)),
+    )
+
+
+def sound_of(state):
+    push = ADIABATIC * state[4]
+    return push * lax.rsqrt(push * state[0])
 
 
 def face_flux(left, right, normal):
     left_u, right_u = left[1 + normal], right[1 + normal]
-    left_sound = jnp.sqrt(ADIABATIC * left[4] / left[0])
-    right_sound = jnp.sqrt(ADIABATIC * right[4] / right[0])
+    left_sound, right_sound = sound_of(left), sound_of(right)
     slow = jnp.minimum(jnp.minimum(left_u - left_sound, right_u - right_sound), 0.0)
     fast = jnp.maximum(jnp.maximum(left_u + left_sound, right_u + right_sound), 0.0)
     share = 1.0 / (fast - slow)
     left_part = fast * share
     right_part = -slow * share
-    left_rate = left_part * (left_u - slow)
-    right_rate = right_part * (right_u - fast)
-    left_mass = left_rate * left[0]
-    right_mass = right_rate * right[0]
+    left_lead = left_u - slow
+    right_lead = right_u - fast
+    left_mass = left_part * left_lead * left[0]
+    right_mass = right_part * right_lead * right[0]
     left_square = left[1] * left[1] + left[2] * left[2] + left[3] * left[3]
     right_square = right[1] * right[1] + right[2] * right[2] + right[3] * right[3]
     flux = [left_mass + right_mass]
@@ -203,10 +186,8 @@
     flux[1 + normal] = flux[1 + normal] + (left_push + right_push)
     flux.append(
         0.5 * (left_mass * left_square + right_mass * right_square)
-        + left[4] * (1.5 * left_rate)
-        + right[4] * (1.5 * right_rate)
-        + left_push * left_u
-        + right_push * right_u
+        + left_push * (1.5 * left_lead + left_u)
+        + right_push * (1.5 * right_lead + right_u)
     )
     flux.append(left_mass * left[5] + right_mass * right[5])
     return flux
@@ -433,8 +414,8 @@
 
 
 def fourth_kernel(
-    cells, totals, fields, force, tend, edges, updated,
-    section, prims, low_ref, high_ref, face_ref, flux_ref,
+    cells, totals, fields, force, tend, edges, out,
+    updated, section, prims, low_ref, high_ref, face_ref, flux_ref, sent,
 ):
     peak = jnp.max(totals[:, 0, :], axis=0, keepdims=True)
     power = jnp.sum(totals[:, 1, :], axis=0, keepdims=True)
@@ -521,6 +502,10 @@
             settle(result, values[6], 1.0 / result[0])
             for k in range(6):
                 updated[k, plane, inner, :] = result[k]
+        pltpu.make_async_copy(updated.at[:, plane], out.at[:, plane], sent.at[plane]).start()
+
+    for plane in range(3):
+        pltpu.make_async_copy(updated.at[:, plane], out.at[:, plane], sent.at[plane]).wait()
 
 
 def shape(*sizes):
@@ -531,13 +516,14 @@
     return [pl.BlockSpec(memory_space=pltpu.VMEM)] * count
 
 
-def call(kernel, name, outs, scalars, arrays, scratch=(), cost=0):
+def call(kernel, name, outs, scalars, arrays, scratch=(), cost=0, out_space=pltpu.VMEM):
     single = not isinstance(outs, tuple)
+    out_spec = pl.BlockSpec(memory_space=out_space)
     return pl.pallas_call(
         kernel,
         out_shape=outs,
         in_specs=[pl.BlockSpec(memory_space=pltpu.SMEM)] * len(scalars) + vmem_specs(len(arrays)),
-        out_specs=vmem_specs(1)[0] if single else tuple(vmem_specs(len(outs))),
+        out_specs=out_spec if single else (out_spec,) * len(outs),
         scratch_shapes=list(scratch),
         compiler_params=pltpu.CompilerParams(vmem_limit_bytes=VMEM_LIMIT),
         cost_estimate=pl.CostEstimate(flops=cost, bytes_accessed=cost, transcendentals=0),
@@ -636,11 +622,14 @@
         (),
         (totals, fields, force, tend, arrays[2]),
         [
+            pltpu.VMEM((6, 3, ROWS, LANES), F32),
             pltpu.VMEM((2, 3, 6, *extended), F32),
             pltpu.VMEM((2, 3, 6, *extended), F32),
             *work,
+            pltpu.SemaphoreType.DMA((3,)),
         ],
         cost=8_000_000,
+        out_space=pltpu.HBM,
     )
 
 

time: 62.7 us -> 61.1 us (0.974)
  Pallas kernels: 13.5 us -> 11.7 us
    pallas_call x3, Pallas kernels: 10.4 us -> 8.59 us  [call(): pl.pallas_call(kernel, out_shape=outs, in_specs=[pl.BlockSpec(memory_spac...]
  transfers between devices with their start and end apart: 5 -> 5, of which waited for: 1 -> 1; matrix products, arithmetic and copies ran while one was open for 0% -> 0% of each run, Pallas kernels for 15% -> 12%
where the time goes in v4:
time: 61.1 us; the launch traced here: 60.8 us
  starting transfers between devices  35.1 us (57%)
  Pallas kernels  11.7 us (19%)
  blocking collectives  10.1 us (17%)
  waiting for transfers between devices  3.69 us (6%)
    ppermute x1, starting transfers between devices, local(): odd_y_in = lax.ppermute(strips[1], GY, pairs(count_y, 1))  13.5 us
    all_to_all x2, starting transfers between devices, exchanged(): return lax.all_to_all(spread, axes, 0, 0, tiled=True)  13.2 us
    all_gather x1, blocking collectives, local(): pair_in = lax.all_gather(pair_out, 'core')  10.1 us
    pallas_call x3, Pallas kernels, call(): pl.pallas_call(kernel, out_shape=outs, in_specs=[pl.BlockSpec(memory_spac...  8.59 us
    ppermute x1, starting transfers between devices, local(): odd_in = lax.ppermute(odd_out, GX, pairs(count_x, 1))  5.39 us
    all_to_all x2, waiting for transfers between devices, exchanged(): return lax.all_to_all(spread, axes, 0, 0, tiled=True)  3.68 us
    ppermute x1, starting transfers between devices, local(): even_in = lax.ppermute(strips[0], GY, pairs(count_y, 0))  3.14 us
    pallas_call x1, Pallas kernels, local(): pl.pallas_call(first_kernel, out_shape=(shape(X_TILES + 1, *tile), shape(...  1.83 us
  transfers between devices with their start and end apart: 5, of which 1 were waited for; matrix products, arithmetic and copies ran while one was open for 0% of the time, Pallas kernels for 12%

profile of v4, /device:TPU:1, one launch (start us, length us, event | category | flops | bytes accessed | tf_op | source)
XLA Modules:
  0.0 60.8 jit_solution(3898267488300019375)
XLA Ops:
  0.0 0.1 pad_add_fusion.place.after
  0.1 1.8 %first.1 = (f32[67,8,128]{2,1,0:T(8,128)S(1)}, f32[66,8,128]{2,1,0:T(8,128)S(1)}, f32[18,16,128]{2,1,0:T(8,128)S(1)}, s32[3,16,128]{2,1,0:T(8,128)S(1)}, f32[36,...) custom-call(s32[2]{0:T(128)S(1)} %pad_add_fusion.place.after, f32[18,16,128]{2,1,0:T(8,128)} %bitcast.12, ...), custom_call_target="tpu_custom_call" | custom-call | tf_op jit(solution)/shard_map/first/pallas_call | solution.py:572
  1.9 5.4 %collective-permute-start = (f32[66,8,128]{2,1,0:T(8,128)S(1)}, f32[66,8,128]{2,1,0:T(8,128)S(1)}, u32[]{:S(2)}, u32[]{:S(2)}) collective-permute-start(f32[66,8,128]{2,1,0:T(8,128)S(1)} %get-tuple-element.21), channel_id=1, source_target_pairs={{64,128},{128,64},{192,256},{256,192},{320,384},{384,320},{448,512... | collective-permute-start | bytes 811016 | tf_op jit(solution)/shard_map/ppermute | solution.py:589
  7.3 10.1 %all-gather = f32[134,8,128]{2,1,0:T(8,128)S(1)} all-gather(f32[67,8,128]{2,1,0:T(8,128)S(1)} %get-tuple-element.16), channel_id=2, replica_groups=mesh['zl'=6,'core'=2,'y'=8,'zh'=2,'x'=4] {'core'}, dimensions={0}, use_global_device_ids=true | all-gather | bytes 823296 | tf_op jit(solution)/shard_map/all_gather | solution.py:588
  17.4 0.6 %spread.2 = f32[32,2,128]{2,1,0:T(2,128)} custom-call(f32[2,2,128]{2,1,0:T(2,128)S(1)} %slice_bitcast_fusion.rows, s32[2]{0:T(128)S(1)} %pad_add_fusion.place.after), custom_call_target="tpu_custom_call" | custom-call | tf_op jit(solution)/shard_map/spread/pallas_call | solution.py:544
  18.1 9.7 %all-to-all-start = ((f32[32,2,128]{2,1,0:T(2,128)}), f32[32,2,128]{2,1,0:T(2,128)S(1)}, u32[]{:S(2)}, u32[]{:S(2)}) async-start(f32[32,2,128]{2,1,0:T(2,128)} %spread.2), calls=%async_computation | async-start | bytes 65536 | tf_op jit(solution)/shard_map/all_to_all | solution.py:552
  27.7 0.0 collective-permute-done.odd_in
  27.7 1.0 %second.1 = (f32[64,128]{1,0:T(8,128)S(1)}, f32[64,128]{1,0:T(8,128)S(1)}) custom-call(s32[2]{0:T(128)S(1)} %pad_add_fusion.place.after, f32[18,16,128]{2,1,0:T(8,128)S(1)} %get-tuple-element.17.state, s32[3,16,128]{2,1,0:T(8,128)S(1)} %get-tuple-element.18.switch, f32[36,16,128]{2,1,0:T(8,128)S(1)} %get-tuple-element.19.edges, ...), custom_call_target="tpu_custom_call" | custom-call | flops 4000000 | bytes 4000000 | tf_op jit(solution)/shard_map/second/pallas_call | solution.py:522
  28.7 3.1 %collective-permute-start.1 = (f32[64,128]{1,0:T(8,128)S(1)}, f32[64,128]{1,0:T(8,128)S(1)}, u32[]{:S(2)}, u32[]{:S(2)}) collective-permute-start(f32[64,128]{1,0:T(8,128)S(1)} %get-tuple-element.22), channel_id=1, source_target_pairs={{0,1},{1,0},{2,3},{3,2},{4,5},{5,4},{6,7},{7,6},{8,9},{9,8},{10,11... | collective-permute-start | bytes 98312 | tf_op jit(solution)/shard_map/ppermute | solution.py:599
  31.9 13.5 %collective-permute-start.2 = (f32[64,128]{1,0:T(8,128)S(1)}, f32[64,128]{1,0:T(8,128)S(1)}, u32[]{:S(2)}, u32[]{:S(2)}) collective-permute-start(f32[64,128]{1,0:T(8,128)S(1)} %get-tuple-element.23), channel_id=1, source_target_pairs={{1,2},{2,1},{3,4},{4,3},{5,6},{6,5},{7,8},{8,7},{9,10},{10,9},{11,... | collective-permute-start | bytes 98312 | tf_op jit(solution)/shard_map/ppermute | solution.py:600
  45.3 0.0 all-to-all-done.rows
  45.3 0.0 collective-permute-done.1.after.even_in
  45.4 0.6 %spread.3 = f32[12,2,128]{2,1,0:T(2,128)} custom-call(f32[32,2,128]{2,1,0:T(2,128)S(1)} %all-to-all-done.rows, f32[64,128]{1,0:T(8,128)S(1)} %collective-permute-done.1.after.even_in), custom_call_target="tpu_custom_call" | custom-call | tf_op jit(solution)/shard_map/spread/pallas_call | solution.py:544
  46.0 3.5 %all-to-all-start.1 = ((f32[12,2,128]{2,1,0:T(2,128)}), f32[12,2,128]{2,1,0:T(2,128)S(1)}, u32[]{:S(2)}, u32[]{:S(2)}) async-start(f32[12,2,128]{2,1,0:T(2,128)} %spread.3), calls=%async_computation.1 | async-start | bytes 24576 | tf_op jit(solution)/shard_map/all_to_all | solution.py:552
  49.5 0.0 collective-permute-done.2.odd_y_in
  49.5 5.2 %third.1 = (f32[2,21,32,128]{3,2,1,0:T(8,128)S(1)}, f32[2,9,32,128]{3,2,1,0:T(8,128)S(1)}, f32[2,18,32,128]{3,2,1,0:T(8,128)S(1)}) custom-call(s32[2]{0:T(128)S(1)} %pad_add_fusion.place.after, f32[18,16,128]{2,1,0:T(8,128)S(1)} %get-tuple-element.17.state, s32[3,16,128]{2,1,0:T(8,128)S(1)} %get-tuple-element.18.switch, ...), custom_call_target="tpu_custom_call" | custom-call | flops 60000000 | bytes 60000000 | tf_op jit(solution)/shard_map/third/pallas_call | solution.py:522
  54.7 3.7 %all-to-all-done.1.totals = f32[12,2,128]{2,1,0:T(2,128)S(1)} async-done(((f32[12,2,128]{2,1,0:T(2,128)}), f32[12,2,128]{2,1,0:T(2,128)S(1)}, u32[]{:S(2)}, u32[]{:S(2)}) %all-to-all-start.1) | async-done | bytes 12320 | tf_op jit(solution)/shard_map/all_to_all | solution.py:552
  58.4 2.4 %fourth.1 = f32[6,3,16,128]{3,2,1,0:T(8,128)} custom-call(f32[12,2,128]{2,1,0:T(2,128)S(1)} %all-to-all-done.1.totals, f32[2,21,32,128]{3,2,1,0:T(8,128)S(1)} %get-tuple-element.24.fields, f32[2,9,32,128]{3,2,1,0:T(8,128)S(1)} %get-tuple-element.25.force, f32[2,18,32,128]{3,2,1,0:T(8,128)S(1)} %get-tuple-element.26.tend, ...), custom_call_target="tpu_custom_call" | custom-call | flops 8000000 | bytes 8000000 | tf_op jit(solution)/shard_map/fourth/pallas_call | solution.py:522
  (1 shorter events, 0.0 us)
Async XLA Ops:
  1.9 25.8 %collective-permute-start = (f32[66,8,128]{2,1,0:T(8,128)S(1)}, f32[66,8,128]{2,1,0:T(8,128)S(1)}, u32[]{:S(2)}, u32[]{:S(2)}) collective-permute-start(f32[66,8,128]{2,1,0:T(8,128)S(1)} %get-tuple-element.21), channel_id=1, source_target_pairs={{64,128},{128,64},{192,256},{256,192},{320,384},{384,320},{448,512... | collective-permute-start | bytes 811016 | tf_op jit(solution)/shard_map/ppermute | solution.py:589
  18.1 27.3 %all-to-all-start = ((f32[32,2,128]{2,1,0:T(2,128)}), f32[32,2,128]{2,1,0:T(2,128)S(1)}, u32[]{:S(2)}, u32[]{:S(2)}) async-start(f32[32,2,128]{2,1,0:T(2,128)} %spread.2), calls=%async_computation | async-start | bytes 65536 | tf_op jit(solution)/shard_map/all_to_all | solution.py:552
  28.7 16.6 %collective-permute-start.1 = (f32[64,128]{1,0:T(8,128)S(1)}, f32[64,128]{1,0:T(8,128)S(1)}, u32[]{:S(2)}, u32[]{:S(2)}) collective-permute-start(f32[64,128]{1,0:T(8,128)S(1)} %get-tuple-element.22), channel_id=1, source_target_pairs={{0,1},{1,0},{2,3},{3,2},{4,5},{5,4},{6,7},{7,6},{8,9},{9,8},{10,11... | collective-permute-start | bytes 98312 | tf_op jit(solution)/shard_map/ppermute | solution.py:599
  31.9 17.6 %collective-permute-start.2 = (f32[64,128]{1,0:T(8,128)S(1)}, f32[64,128]{1,0:T(8,128)S(1)}, u32[]{:S(2)}, u32[]{:S(2)}) collective-permute-start(f32[64,128]{1,0:T(8,128)S(1)} %get-tuple-element.23), channel_id=1, source_target_pairs={{1,2},{2,1},{3,4},{4,3},{5,6},{6,5},{7,8},{8,7},{9,10},{10,9},{11,... | collective-permute-start | bytes 98312 | tf_op jit(solution)/shard_map/ppermute | solution.py:600
  46.0 12.4 %all-to-all-start.1 = ((f32[12,2,128]{2,1,0:T(2,128)}), f32[12,2,128]{2,1,0:T(2,128)S(1)}, u32[]{:S(2)}, u32[]{:S(2)}) async-start(f32[12,2,128]{2,1,0:T(2,128)} %spread.3), calls=%async_computation.1 | async-start | bytes 24576 | tf_op jit(solution)/shard_map/all_to_all | solution.py:552

commit v5 on v4

--- a/solution.py
+++ b/solution.py
@@ -586,6 +586,7 @@
         name="first",
     )(place, *(pltpu.with_memory_space_constraint(values, pltpu.HBM) for values in inputs))
     pair_in = lax.all_gather(pair_out, "core")
+    odd_out, pair_in = lax.optimization_barrier((odd_out, pair_in))
     odd_in = lax.ppermute(odd_out, GX, pairs(count_x, 1))
     totals = exchanged(pair_in[:, X_TILES, 0:2], place, ("y", "x"))
     strips = call(

time: 61.1 us -> 60.7 us (level)
  the two profiles are of different devices: /device:TPU:1 before, /device:TPU:64 now
where the time goes in v5:
time: 60.7 us; the launch traced here: 60.4 us
  starting transfers between devices  42.5 us (70%)
  Pallas kernels  11.7 us (19%)
  waiting for transfers between devices  3.9 us (6%)
  blocking collectives  2.2 us (4%)
    ppermute x1, starting transfers between devices, local(): odd_y_in = lax.ppermute(strips[1], GY, pairs(count_y, 1))  15.8 us
    all_to_all x2, starting transfers between devices, exchanged(): return lax.all_to_all(spread, axes, 0, 0, tiled=True)  13.2 us
    ppermute x1, starting transfers between devices, local(): odd_in = lax.ppermute(odd_out, GX, pairs(count_x, 1))  10.3 us
    pallas_call x3, Pallas kernels, call(): pl.pallas_call(kernel, out_shape=outs, in_specs=[pl.BlockSpec(memory_spac...  8.58 us
    all_to_all x2, waiting for transfers between devices, exchanged(): return lax.all_to_all(spread, axes, 0, 0, tiled=True)  3.53 us
    ppermute x1, starting transfers between devices, local(): even_in = lax.ppermute(strips[0], GY, pairs(count_y, 0))  3.23 us
    all_gather x1, blocking collectives, local(): pair_in = lax.all_gather(pair_out, 'core')  2.2 us
    pallas_call x1, Pallas kernels, local(): pl.pallas_call(first_kernel, out_shape=(shape(X_TILES + 1, *tile), shape(...  1.83 us
  transfers between devices with their start and end apart: 5, of which 2 were waited for; matrix products, arithmetic and copies ran while one was open for 0% of the time, Pallas kernels for 12%

profile of v5, /device:TPU:64, one launch (start us, length us, event | category | flops | bytes accessed | tf_op | source)
XLA Modules:
  0.0 60.4 jit_solution(14293545606033112200)
XLA Ops:
  0.0 0.1 pad_add_fusion.place.after
  0.1 1.8 %first.1 = (f32[67,8,128]{2,1,0:T(8,128)S(1)}, f32[66,8,128]{2,1,0:T(8,128)S(1)}, f32[18,16,128]{2,1,0:T(8,128)S(1)}, s32[3,16,128]{2,1,0:T(8,128)S(1)}, f32[36,...) custom-call(s32[2]{0:T(128)S(1)} %pad_add_fusion.place.after, f32[18,16,128]{2,1,0:T(8,128)} %bitcast.12, ...), custom_call_target="tpu_custom_call" | custom-call | tf_op jit(solution)/shard_map/first/pallas_call | solution.py:572
  1.9 2.2 %all-gather = f32[134,8,128]{2,1,0:T(8,128)S(1)} all-gather(f32[67,8,128]{2,1,0:T(8,128)S(1)} %get-tuple-element.19), channel_id=2, replica_groups=mesh['zl'=6,'core'=2,'y'=8,'zh'=2,'x'=4] {'core'}, dimensions={0}, use_global_device_ids=true | all-gather | bytes 823296 | tf_op jit(solution)/shard_map/all_gather | solution.py:588
  4.1 10.3 %collective-permute-start = (f32[66,8,128]{2,1,0:T(8,128)S(1)}, f32[66,8,128]{2,1,0:T(8,128)S(1)}, u32[]{:S(2)}, u32[]{:S(2)}) collective-permute-start(f32[66,8,128]{2,1,0:T(8,128)S(1)} %get-tuple-element.25), channel_id=1, source_target_pairs={{64,128},{128,64},{192,256},{256,192},{320,384},{384,320},{448,512... | collective-permute-start | bytes 811016 | tf_op jit(solution)/shard_map/ppermute | solution.py:590
  14.4 0.6 %spread.2 = f32[32,2,128]{2,1,0:T(2,128)} custom-call(f32[2,2,128]{2,1,0:T(2,128)S(1)} %slice_bitcast_fusion.rows, s32[2]{0:T(128)S(1)} %pad_add_fusion.place.after), custom_call_target="tpu_custom_call" | custom-call | tf_op jit(solution)/shard_map/spread/pallas_call | solution.py:544
  15.1 3.9 %all-to-all-start = ((f32[32,2,128]{2,1,0:T(2,128)}), f32[32,2,128]{2,1,0:T(2,128)S(1)}, u32[]{:S(2)}, u32[]{:S(2)}) async-start(f32[32,2,128]{2,1,0:T(2,128)} %spread.2), calls=%async_computation | async-start | bytes 65536 | tf_op jit(solution)/shard_map/all_to_all | solution.py:552
  18.9 0.4 collective-permute-done.odd_in
  19.3 1.0 %second.1 = (f32[64,128]{1,0:T(8,128)S(1)}, f32[64,128]{1,0:T(8,128)S(1)}) custom-call(s32[2]{0:T(128)S(1)} %pad_add_fusion.place.after, f32[18,16,128]{2,1,0:T(8,128)S(1)} %get-tuple-element.21.state, s32[3,16,128]{2,1,0:T(8,128)S(1)} %get-tuple-element.22.switch, f32[36,16,128]{2,1,0:T(8,128)S(1)} %get-tuple-element.23.edges, ...), custom_call_target="tpu_custom_call" | custom-call | flops 4000000 | bytes 4000000 | tf_op jit(solution)/shard_map/second/pallas_call | solution.py:522
  20.3 3.2 %collective-permute-start.1 = (f32[64,128]{1,0:T(8,128)S(1)}, f32[64,128]{1,0:T(8,128)S(1)}, u32[]{:S(2)}, u32[]{:S(2)}) collective-permute-start(f32[64,128]{1,0:T(8,128)S(1)} %get-tuple-element.26), channel_id=1, source_target_pairs={{0,1},{1,0},{2,3},{3,2},{4,5},{5,4},{6,7},{7,6},{8,9},{9,8},{10,11... | collective-permute-start | bytes 98312 | tf_op jit(solution)/shard_map/ppermute | solution.py:600
  23.5 15.8 %collective-permute-start.2 = (f32[64,128]{1,0:T(8,128)S(1)}, f32[64,128]{1,0:T(8,128)S(1)}, u32[]{:S(2)}, u32[]{:S(2)}) collective-permute-start(f32[64,128]{1,0:T(8,128)S(1)} %get-tuple-element.27), channel_id=1, source_target_pairs={{1,2},{2,1},{3,4},{4,3},{5,6},{6,5},{7,8},{8,7},{9,10},{10,9},{11,... | collective-permute-start | bytes 98312 | tf_op jit(solution)/shard_map/ppermute | solution.py:601
  39.3 0.0 all-to-all-done.rows
  39.3 0.0 collective-permute-done.1.after.even_in
  39.3 0.6 %spread.3 = f32[12,2,128]{2,1,0:T(2,128)} custom-call(f32[32,2,128]{2,1,0:T(2,128)S(1)} %all-to-all-done.rows, f32[64,128]{1,0:T(8,128)S(1)} %collective-permute-done.1.after.even_in), custom_call_target="tpu_custom_call" | custom-call | tf_op jit(solution)/shard_map/spread/pallas_call | solution.py:544
  39.9 9.3 %all-to-all-start.1 = ((f32[12,2,128]{2,1,0:T(2,128)}), f32[12,2,128]{2,1,0:T(2,128)S(1)}, u32[]{:S(2)}, u32[]{:S(2)}) async-start(f32[12,2,128]{2,1,0:T(2,128)} %spread.3), calls=%async_computation.1 | async-start | bytes 24576 | tf_op jit(solution)/shard_map/all_to_all | solution.py:552
  49.3 0.0 collective-permute-done.2.odd_y_in
  49.3 5.2 %third.1 = (f32[2,21,32,128]{3,2,1,0:T(8,128)S(1)}, f32[2,9,32,128]{3,2,1,0:T(8,128)S(1)}, f32[2,18,32,128]{3,2,1,0:T(8,128)S(1)}) custom-call(s32[2]{0:T(128)S(1)} %pad_add_fusion.place.after, f32[18,16,128]{2,1,0:T(8,128)S(1)} %get-tuple-element.21.state, s32[3,16,128]{2,1,0:T(8,128)S(1)} %get-tuple-element.22.switch, ...), custom_call_target="tpu_custom_call" | custom-call | flops 60000000 | bytes 60000000 | tf_op jit(solution)/shard_map/third/pallas_call | solution.py:522
  54.5 3.5 %all-to-all-done.1.totals = f32[12,2,128]{2,1,0:T(2,128)S(1)} async-done(((f32[12,2,128]{2,1,0:T(2,128)}), f32[12,2,128]{2,1,0:T(2,128)S(1)}, u32[]{:S(2)}, u32[]{:S(2)}) %all-to-all-start.1) | async-done | bytes 12320 | tf_op jit(solution)/shard_map/all_to_all | solution.py:552
  58.0 2.4 %fourth.1 = f32[6,3,16,128]{3,2,1,0:T(8,128)} custom-call(f32[12,2,128]{2,1,0:T(2,128)S(1)} %all-to-all-done.1.totals, f32[2,21,32,128]{3,2,1,0:T(8,128)S(1)} %get-tuple-element.28.fields, f32[2,9,32,128]{3,2,1,0:T(8,128)S(1)} %get-tuple-element.29.force, f32[2,18,32,128]{3,2,1,0:T(8,128)S(1)} %get-tuple-element.30.tend, ...), custom_call_target="tpu_custom_call" | custom-call | flops 8000000 | bytes 8000000 | tf_op jit(solution)/shard_map/fourth/pallas_call | solution.py:522
  (1 shorter events, 0.0 us)
Async XLA Ops:
  4.1 15.2 %collective-permute-start = (f32[66,8,128]{2,1,0:T(8,128)S(1)}, f32[66,8,128]{2,1,0:T(8,128)S(1)}, u32[]{:S(2)}, u32[]{:S(2)}) collective-permute-start(f32[66,8,128]{2,1,0:T(8,128)S(1)} %get-tuple-element.25), channel_id=1, source_target_pairs={{64,128},{128,64},{192,256},{256,192},{320,384},{384,320},{448,512... | collective-permute-start | bytes 811016 | tf_op jit(solution)/shard_map/ppermute | solution.py:590
  15.1 24.2 %all-to-all-start = ((f32[32,2,128]{2,1,0:T(2,128)}), f32[32,2,128]{2,1,0:T(2,128)S(1)}, u32[]{:S(2)}, u32[]{:S(2)}) async-start(f32[32,2,128]{2,1,0:T(2,128)} %spread.2), calls=%async_computation | async-start | bytes 65536 | tf_op jit(solution)/shard_map/all_to_all | solution.py:552
  20.3 19.0 %collective-permute-start.1 = (f32[64,128]{1,0:T(8,128)S(1)}, f32[64,128]{1,0:T(8,128)S(1)}, u32[]{:S(2)}, u32[]{:S(2)}) collective-permute-start(f32[64,128]{1,0:T(8,128)S(1)} %get-tuple-element.26), channel_id=1, source_target_pairs={{0,1},{1,0},{2,3},{3,2},{4,5},{5,4},{6,7},{7,6},{8,9},{9,8},{10,11... | collective-permute-start | bytes 98312 | tf_op jit(solution)/shard_map/ppermute | solution.py:600
  23.5 25.8 %collective-permute-start.2 = (f32[64,128]{1,0:T(8,128)S(1)}, f32[64,128]{1,0:T(8,128)S(1)}, u32[]{:S(2)}, u32[]{:S(2)}) collective-permute-start(f32[64,128]{1,0:T(8,128)S(1)} %get-tuple-element.27), channel_id=1, source_target_pairs={{1,2},{2,1},{3,4},{4,3},{5,6},{6,5},{7,8},{8,7},{9,10},{10,9},{11,... | collective-permute-start | bytes 98312 | tf_op jit(solution)/shard_map/ppermute | solution.py:601
  39.9 18.1 %all-to-all-start.1 = ((f32[12,2,128]{2,1,0:T(2,128)}), f32[12,2,128]{2,1,0:T(2,128)S(1)}, u32[]{:S(2)}, u32[]{:S(2)}) async-start(f32[12,2,128]{2,1,0:T(2,128)} %spread.3), calls=%async_computation.1 | async-start | bytes 24576 | tf_op jit(solution)/shard_map/all_to_all | solution.py:552

commit v6 on v5

--- a/solution.py
+++ b/solution.py
@@ -32,6 +32,10 @@
     return values if shift == 0 else pltpu.roll(values, shift, axis)
 
 
+def parities():
+    return lax.axis_index("core"), lax.rem(lax.axis_index("x"), 2)
+
+
 def each(count, body):
     def step(index, carry):
         body(index)
@@ -55,7 +59,7 @@
 
 
 def first_kernel(
-    place, state_in, switch_in, edges_in, forcing_in,
+    state_in, switch_in, edges_in, forcing_in,
     pair_out, odd_out, state, switch, edges, forcing, arrived,
 ):
     refs = (state, switch, edges, forcing)
@@ -67,7 +71,7 @@
     ]
     for copy in copies:
         copy.start()
-    odd = place[0]
+    odd, _ = parities()
     near = pl.multiple_of(8 * (1 - odd), 8)
     far = pl.multiple_of(8 * odd, 8)
     for k in (0, 1, 3):
@@ -116,9 +120,8 @@
     return pltpu.roll(values, lax.rem(shift + LANES, LANES), 1)
 
 
-def second_kernel(place, state, switch, edges, forcing, pair_in, odd_in, even_out, odd_out):
-    odd_x = place[0]
-    odd_y = place[1]
+def second_kernel(state, switch, edges, forcing, pair_in, odd_in, even_out, odd_out):
+    odd_x, odd_y = parities()
     lane = lane_index((EXT, LANES))
     high = jnp.zeros((EXT, LANES), F32)
     low = jnp.zeros((EXT, LANES), F32)
@@ -291,11 +294,10 @@
 
 
 def third_kernel(
-    place, state, switch, edges, forcing, pair_in, odd_in, even_in, odd_y_in,
-    fields, force, tend, prims, planes, low_ref, high_ref, face_ref, flux_ref, strip_ref,
+    state, switch, edges, forcing, pair_in, odd_in, even_in, odd_y_in,
+    fields, force, tend, outer, prims, planes, low_ref, high_ref, face_ref, flux_ref, strip_ref,
 ):
-    odd_x = place[0]
-    odd_y = place[1]
+    odd_x, odd_y = parities()
     strip_ref[0] = jnp.where(odd_y == 0, even_in[...], odd_y_in[...])
     strip_ref[1] = jnp.where(odd_y == 0, odd_y_in[...], even_in[...])
     clear_ends(low_ref, flux_ref)
@@ -360,6 +362,7 @@
         )
         for k in range(6):
             planes[0, step, k] = values[k]
+            outer[step, k] = values[k][8:24]
         values = edge_primitives([rim_tile(EXT, k) for k in places])
         for k in range(6):
             planes[1, step, k, 0:8] = jnp.ones((8, LANES), F32)
@@ -414,7 +417,7 @@
 
 
 def fourth_kernel(
-    cells, totals, fields, force, tend, edges, out,
+    cells, totals, fields, force, tend, outer_prims, out,
     updated, section, prims, low_ref, high_ref, face_ref, flux_ref, sent,
 ):
     peak = jnp.max(totals[:, 0, :], axis=0, keepdims=True)
@@ -459,11 +462,7 @@
     def _(step):
         inner = pl.ds(pl.multiple_of(8 * step, 8), 8)
         rows = pl.ds(pl.multiple_of(8 * step + 8, 8), 8)
-        outer = [
-            edge_primitives([edges[18 * side + 3 * k + plane, inner, :] for k in range(6)])
-            for side in range(2)
-            for plane in range(3)
-        ]
+        outer = [[outer_prims[p, k, inner, :] for k in range(6)] for p in range(6)]
         column = (
             outer[0:3] + [[prims[0, p, k, rows, :] for k in range(6)] for p in range(3)] + outer[3:6]
         )
@@ -516,19 +515,19 @@
     return [pl.BlockSpec(memory_space=pltpu.VMEM)] * count
 
 
-def call(kernel, name, outs, scalars, arrays, scratch=(), cost=0, out_space=pltpu.VMEM):
+def call(kernel, name, outs, arrays, scratch=(), cost=0, out_space=pltpu.VMEM):
     single = not isinstance(outs, tuple)
     out_spec = pl.BlockSpec(memory_space=out_space)
     return pl.pallas_call(
         kernel,
         out_shape=outs,
-        in_specs=[pl.BlockSpec(memory_space=pltpu.SMEM)] * len(scalars) + vmem_specs(len(arrays)),
+        in_specs=vmem_specs(len(arrays)),
         out_specs=out_spec if single else (out_spec,) * len(outs),
         scratch_shapes=list(scratch),
         compiler_params=pltpu.CompilerParams(vmem_limit_bytes=VMEM_LIMIT),
         cost_estimate=pl.CostEstimate(flops=cost, bytes_accessed=cost, transcendentals=0),
         name=name,
-    )(*scalars, *arrays)
+    )(*arrays)
 
 
 def pairs(count, begin):
@@ -539,16 +538,18 @@
     return table
 
 
-def exchanged(rows, after, axes):
-    count = lax.axis_size(axes)
-    spread = pl.pallas_call(
+def spread_over(rows, after, axes):
+    return pl.pallas_call(
         spread_kernel,
-        out_shape=shape(count, 2, LANES),
+        out_shape=shape(lax.axis_size(axes), 2, LANES),
         in_specs=[*vmem_specs(1), pl.BlockSpec(memory_space=pl.ANY)],
         out_specs=vmem_specs(1)[0],
         compiler_params=pltpu.CompilerParams(vmem_limit_bytes=VMEM_LIMIT),
         name="spread",
     )(rows, after)
+
+
+def exchanged(spread, axes):
     return lax.all_to_all(spread, axes, 0, 0, tiled=True)
 
 
@@ -560,7 +561,6 @@
     count_x = lax.axis_size(GX)
     count_y = lax.axis_size(GY)
     cells = 3.0 * ROWS * LANES * count_x * count_y
-    place = jnp.stack([lax.axis_index(GX) % 2, lax.axis_index(GY) % 2]).astype(jnp.int32)
     tile = (8, LANES)
     block = (ROWS, LANES)
     inputs = (
@@ -577,36 +577,40 @@
             *(jax.ShapeDtypeStruct(values.shape, values.dtype) for values in inputs),
         ),
         in_specs=[
-            pl.BlockSpec(memory_space=pltpu.SMEM),
             *([pl.BlockSpec(memory_space=pltpu.HBM)] * 4),
         ],
         out_specs=tuple(vmem_specs(6)),
         scratch_shapes=[pltpu.SemaphoreType.DMA((4,))],
         compiler_params=pltpu.CompilerParams(vmem_limit_bytes=VMEM_LIMIT),
         name="first",
-    )(place, *(pltpu.with_memory_space_constraint(values, pltpu.HBM) for values in inputs))
+    )(*(pltpu.with_memory_space_constraint(values, pltpu.HBM) for values in inputs))
     pair_in = lax.all_gather(pair_out, "core")
     odd_out, pair_in = lax.optimization_barrier((odd_out, pair_in))
     odd_in = lax.ppermute(odd_out, GX, pairs(count_x, 1))
-    totals = exchanged(pair_in[:, X_TILES, 0:2], place, ("y", "x"))
+    rows = pair_in[:, X_TILES, 0:2]
+    spread = spread_over(rows, rows, ("y", "x"))
+    totals = exchanged(spread, ("y", "x"))
     strips = call(
         second_kernel,
         "second",
         (shape(EXT + 2 * ROWS, LANES), shape(EXT + 2 * ROWS, LANES)),
-        (place,),
         (*arrays, pair_in, odd_in),
         cost=4_000_000,
     )
     even_in = lax.ppermute(strips[0], GY, pairs(count_y, 0))
     odd_y_in = lax.ppermute(strips[1], GY, pairs(count_y, 1))
-    totals = exchanged(totals, even_in, ("zh", "zl"))
+    totals = exchanged(spread_over(totals, even_in, ("zh", "zl")), ("zh", "zl"))
     extended = (EXT, LANES)
     work = [pltpu.VMEM((6, *extended), F32) for _ in range(4)]
-    fields, force, tend = call(
+    fields, force, tend, outer = call(
         third_kernel,
         "third",
-        (shape(2, FIELDS, *extended), shape(2, FORCES, *extended), shape(2, 18, *extended)),
-        (place,),
+        (
+            shape(2, FIELDS, *extended),
+            shape(2, FORCES, *extended),
+            shape(2, 18, *extended),
+            shape(6, 6, ROWS, LANES),
+        ),
         (*arrays, pair_in, odd_in, even_in, odd_y_in),
         [
             pltpu.VMEM((2, 3, 6, *extended), F32),
@@ -620,8 +624,7 @@
         functools.partial(fourth_kernel, cells),
         "fourth",
         shape(6, 3, ROWS, LANES),
-        (),
-        (totals, fields, force, tend, arrays[2]),
+        (totals, fields, force, tend, outer),
         [
             pltpu.VMEM((6, 3, ROWS, LANES), F32),
             pltpu.VMEM((2, 3, 6, *extended), F32),

time: 60.7 us -> 59.6 us (0.982)
  Pallas kernels: 11.7 us -> 10.1 us
    pallas_call x5, Pallas kernels: 9.85 us -> 8.76 us  [the longest x3 7.5 us: call(): pl.pallas_call(kernel, out_shape=outs, in_specs=vmem_specs(len(arrays)),...]
  transfers between devices with their start and end apart: 5 -> 5, of which waited for: 2 -> 2; matrix products, arithmetic and copies ran while one was open for 0% -> 0% of each run, Pallas kernels for 12% -> 11%
where the time goes in v6:
time: 59.6 us; the launch traced here: 59.2 us
  starting transfers between devices  42.5 us (71%)
  Pallas kernels  10.1 us (17%)
  waiting for transfers between devices  4.43 us (7%)
  blocking collectives  2.2 us (4%)
    ppermute x1, starting transfers between devices, local(): odd_y_in = lax.ppermute(strips[1], GY, pairs(count_y, 1))  15.8 us
    all_to_all x2, starting transfers between devices, exchanged(): return lax.all_to_all(spread, axes, 0, 0, tiled=True)  13.2 us
    ppermute x1, starting transfers between devices, local(): odd_in = lax.ppermute(odd_out, GX, pairs(count_x, 1))  10.3 us
    pallas_call x3, Pallas kernels, call(): pl.pallas_call(kernel, out_shape=outs, in_specs=vmem_specs(len(arrays)),...  7.5 us
    all_to_all x2, waiting for transfers between devices, exchanged(): return lax.all_to_all(spread, axes, 0, 0, tiled=True)  4.06 us
    ppermute x1, starting transfers between devices, local(): even_in = lax.ppermute(strips[0], GY, pairs(count_y, 0))  3.23 us
    all_gather x1, blocking collectives, local(): pair_in = lax.all_gather(pair_out, 'core')  2.2 us
    pallas_call x1, Pallas kernels, local(): pl.pallas_call(first_kernel, out_shape=(shape(X_TILES + 1, *tile), shape(...  1.29 us
  transfers between devices with their start and end apart: 5, of which 2 were waited for; matrix products, arithmetic and copies ran while one was open for 0% of the time, Pallas kernels for 11%

profile of v6, /device:TPU:64, one launch (start us, length us, event | category | flops | bytes accessed | tf_op | source)
XLA Modules:
  0.0 59.2 jit_solution(8982911439893288896)
XLA Ops:
  0.0 1.3 %first.1 = (f32[67,8,128]{2,1,0:T(8,128)S(1)}, f32[66,8,128]{2,1,0:T(8,128)S(1)}, f32[18,16,128]{2,1,0:T(8,128)S(1)}, s32[3,16,128]{2,1,0:T(8,128)S(1)}, f32[36,...) custom-call(f32[18,16,128]{2,1,0:T(8,128)} %bitcast.10, s32[3,16,128]{2,1,0:T(8,128)} %switch_in.1, ...), custom_call_target="tpu_custom_call" | custom-call | tf_op jit(solution)/shard_map/first/pallas_call | solution.py:572
  1.3 2.2 %all-gather = f32[134,8,128]{2,1,0:T(8,128)S(1)} all-gather(f32[67,8,128]{2,1,0:T(8,128)S(1)} %get-tuple-element.20), channel_id=2, replica_groups=mesh['zl'=6,'core'=2,'y'=8,'zh'=2,'x'=4] {'core'}, dimensions={0}, use_global_device_ids=true | all-gather | bytes 823296 | tf_op jit(solution)/shard_map/all_gather | solution.py:587
  3.5 10.3 %collective-permute-start = (f32[66,8,128]{2,1,0:T(8,128)S(1)}, f32[66,8,128]{2,1,0:T(8,128)S(1)}, u32[]{:S(2)}, u32[]{:S(2)}) collective-permute-start(f32[66,8,128]{2,1,0:T(8,128)S(1)} %get-tuple-element.26), channel_id=1, source_target_pairs={{64,128},{128,64},{192,256},{256,192},{320,384},{384,320},{448,512... | collective-permute-start | bytes 811016 | tf_op jit(solution)/shard_map/ppermute | solution.py:589
  13.8 0.6 %spread.2 = f32[32,2,128]{2,1,0:T(2,128)} custom-call(f32[2,2,128]{2,1,0:T(2,128)S(1)} %slice_bitcast_fusion.rows.after, f32[2,2,128]{2,1,0:T(2,128)S(1)} %slice_bitcast_fusion.rows.after), custom_call_target="tpu_custom_call" | custom-call | tf_op jit(solution)/shard_map/spread/pallas_call | solution.py:542
  14.5 3.9 %all-to-all-start = ((f32[32,2,128]{2,1,0:T(2,128)}), f32[32,2,128]{2,1,0:T(2,128)S(1)}, u32[]{:S(2)}, u32[]{:S(2)}) async-start(f32[32,2,128]{2,1,0:T(2,128)} %spread.2), calls=%async_computation | async-start | bytes 65536 | tf_op jit(solution)/shard_map/all_to_all | solution.py:553
  18.3 0.4 collective-permute-done.odd_in
  18.7 0.4 second.1
  19.1 3.2 %collective-permute-start.1 = (f32[64,128]{1,0:T(8,128)S(1)}, f32[64,128]{1,0:T(8,128)S(1)}, u32[]{:S(2)}, u32[]{:S(2)}) collective-permute-start(f32[64,128]{1,0:T(8,128)S(1)} %get-tuple-element.27), channel_id=1, source_target_pairs={{0,1},{1,0},{2,3},{3,2},{4,5},{5,4},{6,7},{7,6},{8,9},{9,8},{10,11... | collective-permute-start | bytes 98312 | tf_op jit(solution)/shard_map/ppermute | solution.py:600
  22.4 15.8 %collective-permute-start.2 = (f32[64,128]{1,0:T(8,128)S(1)}, f32[64,128]{1,0:T(8,128)S(1)}, u32[]{:S(2)}, u32[]{:S(2)}) collective-permute-start(f32[64,128]{1,0:T(8,128)S(1)} %get-tuple-element.28), channel_id=1, source_target_pairs={{1,2},{2,1},{3,4},{4,3},{5,6},{6,5},{7,8},{8,7},{9,10},{10,9},{11,... | collective-permute-start | bytes 98312 | tf_op jit(solution)/shard_map/ppermute | solution.py:601
  38.1 0.0 all-to-all-done.rows
  38.1 0.0 collective-permute-done.1.after.even_in
  38.1 0.6 %spread.3 = f32[12,2,128]{2,1,0:T(2,128)} custom-call(f32[32,2,128]{2,1,0:T(2,128)S(1)} %all-to-all-done.rows, f32[64,128]{1,0:T(8,128)S(1)} %collective-permute-done.1.after.even_in), custom_call_target="tpu_custom_call" | custom-call | tf_op jit(solution)/shard_map/spread/pallas_call | solution.py:542
  38.8 9.3 %all-to-all-start.1 = ((f32[12,2,128]{2,1,0:T(2,128)}), f32[12,2,128]{2,1,0:T(2,128)S(1)}, u32[]{:S(2)}, u32[]{:S(2)}) async-start(f32[12,2,128]{2,1,0:T(2,128)} %spread.3), calls=%async_computation.1 | async-start | bytes 24576 | tf_op jit(solution)/shard_map/all_to_all | solution.py:553
  48.1 0.0 collective-permute-done.2.odd_y_in
  48.1 4.7 %third.1 = (f32[2,21,32,128]{3,2,1,0:T(8,128)S(1)}, f32[2,9,32,128]{3,2,1,0:T(8,128)S(1)}, f32[2,18,32,128]{3,2,1,0:T(8,128)S(1)}, f32[6,6,16,128]{3,2,1,0:T(8,128)S(1)}) custom-call(f32[18,16,128]{2,1,0:T(8,128)S(1)} %get-tuple-element.22.state, s32[3,16,128]{2,1,0:T(8,128)S(1)} %get-tuple-element.23.switch, f32[36,16,128]{2,1,0:T(8,128)S(1)} %get-tuple-element.24.edges, ...), custom_call_target="tpu_custom_call" | custom-call | flops 60000000 | bytes 60000000 | tf_op jit(solution)/shard_map/third/pallas_call | solution.py:521
  52.8 4.1 %all-to-all-done.1.totals = f32[12,2,128]{2,1,0:T(2,128)S(1)} async-done(((f32[12,2,128]{2,1,0:T(2,128)}), f32[12,2,128]{2,1,0:T(2,128)S(1)}, u32[]{:S(2)}, u32[]{:S(2)}) %all-to-all-start.1) | async-done | bytes 12320 | tf_op jit(solution)/shard_map/all_to_all | solution.py:553
  56.8 2.4 %fourth.1 = f32[6,3,16,128]{3,2,1,0:T(8,128)} custom-call(f32[12,2,128]{2,1,0:T(2,128)S(1)} %all-to-all-done.1.totals, f32[2,21,32,128]{3,2,1,0:T(8,128)S(1)} %get-tuple-element.29.fields, f32[2,9,32,128]{3,2,1,0:T(8,128)S(1)} %get-tuple-element.30.force, f32[2,18,32,128]{3,2,1,0:T(8,128)S(1)} %get-tuple-element.31.tend, ...), custom_call_target="tpu_custom_call" | custom-call | flops 8000000 | bytes 8000000 | tf_op jit(solution)/shard_map/fourth/pallas_call | solution.py:521
  (1 shorter events, 0.0 us)
Async XLA Ops:
  3.5 15.2 %collective-permute-start = (f32[66,8,128]{2,1,0:T(8,128)S(1)}, f32[66,8,128]{2,1,0:T(8,128)S(1)}, u32[]{:S(2)}, u32[]{:S(2)}) collective-permute-start(f32[66,8,128]{2,1,0:T(8,128)S(1)} %get-tuple-element.26), channel_id=1, source_target_pairs={{64,128},{128,64},{192,256},{256,192},{320,384},{384,320},{448,512... | collective-permute-start | bytes 811016 | tf_op jit(solution)/shard_map/ppermute | solution.py:589
  14.5 23.7 %all-to-all-start = ((f32[32,2,128]{2,1,0:T(2,128)}), f32[32,2,128]{2,1,0:T(2,128)S(1)}, u32[]{:S(2)}, u32[]{:S(2)}) async-start(f32[32,2,128]{2,1,0:T(2,128)} %spread.2), calls=%async_computation | async-start | bytes 65536 | tf_op jit(solution)/shard_map/all_to_all | solution.py:553
  19.1 19.0 %collective-permute-start.1 = (f32[64,128]{1,0:T(8,128)S(1)}, f32[64,128]{1,0:T(8,128)S(1)}, u32[]{:S(2)}, u32[]{:S(2)}) collective-permute-start(f32[64,128]{1,0:T(8,128)S(1)} %get-tuple-element.27), channel_id=1, source_target_pairs={{0,1},{1,0},{2,3},{3,2},{4,5},{5,4},{6,7},{7,6},{8,9},{9,8},{10,11... | collective-permute-start | bytes 98312 | tf_op jit(solution)/shard_map/ppermute | solution.py:600
  22.4 25.8 %collective-permute-start.2 = (f32[64,128]{1,0:T(8,128)S(1)}, f32[64,128]{1,0:T(8,128)S(1)}, u32[]{:S(2)}, u32[]{:S(2)}) collective-permute-start(f32[64,128]{1,0:T(8,128)S(1)} %get-tuple-element.28), channel_id=1, source_target_pairs={{1,2},{2,1},{3,4},{4,3},{5,6},{6,5},{7,8},{8,7},{9,10},{10,9},{11,... | collective-permute-start | bytes 98312 | tf_op jit(solution)/shard_map/ppermute | solution.py:601
  38.8 18.1 %all-to-all-start.1 = ((f32[12,2,128]{2,1,0:T(2,128)}), f32[12,2,128]{2,1,0:T(2,128)S(1)}, u32[]{:S(2)}, u32[]{:S(2)}) async-start(f32[12,2,128]{2,1,0:T(2,128)} %spread.3), calls=%async_computation.1 | async-start | bytes 24576 | tf_op jit(solution)/shard_map/all_to_all | solution.py:553

commit v7 on v6

--- a/solution.py
+++ b/solution.py
@@ -585,10 +585,10 @@
         name="first",
     )(*(pltpu.with_memory_space_constraint(values, pltpu.HBM) for values in inputs))
     pair_in = lax.all_gather(pair_out, "core")
-    odd_out, pair_in = lax.optimization_barrier((odd_out, pair_in))
-    odd_in = lax.ppermute(odd_out, GX, pairs(count_x, 1))
     rows = pair_in[:, X_TILES, 0:2]
     spread = spread_over(rows, rows, ("y", "x"))
+    odd_out, spread = lax.optimization_barrier((odd_out, spread))
+    odd_in = lax.ppermute(odd_out, GX, pairs(count_x, 1))
     totals = exchanged(spread, ("y", "x"))
     strips = call(
         second_kernel,

time: 59.6 us -> 59.6 us (level)
  waiting for transfers between devices: 4.43 us -> 5.06 us
  starting transfers between devices: 42.5 us -> 41.9 us
    ppermute x1, starting transfers between devices: 3.23 us -> 2.6 us  [local(): even_in = lax.ppermute(strips[0], GY, pairs(count_y, 0))]
    ppermute x1, waiting for transfers between devices: 0.36 us -> 1 us  [local(): odd_in = lax.ppermute(odd_out, GX, pairs(count_x, 1))]
  transfers between devices with their start and end apart: 5 -> 5, of which waited for: 2 -> 2; matrix products, arithmetic and copies ran while one was open for 0% -> 0% of each run, Pallas kernels for 11% -> 10%
where the time goes in v7:
time: 59.6 us; the launch traced here: 59.2 us
  starting transfers between devices  41.9 us (70%)
  Pallas kernels  10.1 us (17%)
  waiting for transfers between devices  5.06 us (8%)
  blocking collectives  2.2 us (4%)
    ppermute x1, starting transfers between devices, local(): odd_y_in = lax.ppermute(strips[1], GY, pairs(count_y, 1))  15.8 us
    all_to_all x2, starting transfers between devices, exchanged(): return lax.all_to_all(spread, axes, 0, 0, tiled=True)  13.2 us
    ppermute x1, starting transfers between devices, local(): odd_in = lax.ppermute(odd_out, GX, pairs(count_x, 1))  10.3 us
    pallas_call x3, Pallas kernels, call(): pl.pallas_call(kernel, out_shape=outs, in_specs=vmem_specs(len(arrays)),...  7.5 us
    all_to_all x2, waiting for transfers between devices, exchanged(): return lax.all_to_all(spread, axes, 0, 0, tiled=True)  4.06 us
    ppermute x1, starting transfers between devices, local(): even_in = lax.ppermute(strips[0], GY, pairs(count_y, 0))  2.6 us
    all_gather x1, blocking collectives, local(): pair_in = lax.all_gather(pair_out, 'core')  2.2 us
    pallas_call x1, Pallas kernels, local(): pl.pallas_call(first_kernel, out_shape=(shape(X_TILES + 1, *tile), shape(...  1.29 us
  transfers between devices with their start and end apart: 5, of which 2 were waited for; matrix products, arithmetic and copies ran while one was open for 0% of the time, Pallas kernels for 10%

profile of v7, /device:TPU:64, one launch (start us, length us, event | category | flops | bytes accessed | tf_op | source)
XLA Modules:
  0.0 59.2 jit_solution(17650859519110274416)
XLA Ops:
  0.0 1.3 %first.1 = (f32[67,8,128]{2,1,0:T(8,128)S(1)}, f32[66,8,128]{2,1,0:T(8,128)S(1)}, f32[18,16,128]{2,1,0:T(8,128)S(1)}, s32[3,16,128]{2,1,0:T(8,128)S(1)}, f32[36,...) custom-call(f32[18,16,128]{2,1,0:T(8,128)} %bitcast.10, s32[3,16,128]{2,1,0:T(8,128)} %switch_in.1, ...), custom_call_target="tpu_custom_call" | custom-call | tf_op jit(solution)/shard_map/first/pallas_call | solution.py:572
  1.3 2.2 %all-gather = f32[134,8,128]{2,1,0:T(8,128)S(1)} all-gather(f32[67,8,128]{2,1,0:T(8,128)S(1)} %get-tuple-element.20), channel_id=2, replica_groups=mesh['zl'=6,'core'=2,'y'=8,'zh'=2,'x'=4] {'core'}, dimensions={0}, use_global_device_ids=true | all-gather | bytes 823296 | tf_op jit(solution)/shard_map/all_gather | solution.py:587
  3.5 0.6 %spread.2 = f32[32,2,128]{2,1,0:T(2,128)} custom-call(f32[2,2,128]{2,1,0:T(2,128)S(1)} %slice_bitcast_fusion.rows.after, f32[2,2,128]{2,1,0:T(2,128)S(1)} %slice_bitcast_fusion.rows.after), custom_call_target="tpu_custom_call" | custom-call | tf_op jit(solution)/shard_map/spread/pallas_call | solution.py:542
  4.1 10.3 %collective-permute-start = (f32[66,8,128]{2,1,0:T(8,128)S(1)}, f32[66,8,128]{2,1,0:T(8,128)S(1)}, u32[]{:S(2)}, u32[]{:S(2)}) collective-permute-start(f32[66,8,128]{2,1,0:T(8,128)S(1)} %get-tuple-element.26), channel_id=1, source_target_pairs={{64,128},{128,64},{192,256},{256,192},{320,384},{384,320},{448,512... | collective-permute-start | bytes 811016 | tf_op jit(solution)/shard_map/ppermute | solution.py:591
  14.4 3.9 %all-to-all-start = ((f32[32,2,128]{2,1,0:T(2,128)}), f32[32,2,128]{2,1,0:T(2,128)S(1)}, u32[]{:S(2)}, u32[]{:S(2)}) async-start(f32[32,2,128]{2,1,0:T(2,128)} %spread.2), calls=%async_computation | async-start | bytes 65536 | tf_op jit(solution)/shard_map/all_to_all | solution.py:553
  18.3 1.0 %collective-permute-done.odd_in = f32[66,8,128]{2,1,0:T(8,128)S(1)} collective-permute-done((f32[66,8,128]{2,1,0:T(8,128)S(1)}, f32[66,8,128]{2,1,0:T(8,128)S(1)}, u32[]{:S(2)}, u32[]{:S(2)}) %collective-permute-start) | collective-permute-done | bytes 270368 | tf_op jit(solution)/shard_map/ppermute | solution.py:591
  19.3 0.4 second.1
  19.8 2.6 %collective-permute-start.1 = (f32[64,128]{1,0:T(8,128)S(1)}, f32[64,128]{1,0:T(8,128)S(1)}, u32[]{:S(2)}, u32[]{:S(2)}) collective-permute-start(f32[64,128]{1,0:T(8,128)S(1)} %get-tuple-element.27), channel_id=1, source_target_pairs={{0,1},{1,0},{2,3},{3,2},{4,5},{5,4},{6,7},{7,6},{8,9},{9,8},{10,11... | collective-permute-start | bytes 98312 | tf_op jit(solution)/shard_map/ppermute | solution.py:600
  22.4 15.8 %collective-permute-start.2 = (f32[64,128]{1,0:T(8,128)S(1)}, f32[64,128]{1,0:T(8,128)S(1)}, u32[]{:S(2)}, u32[]{:S(2)}) collective-permute-start(f32[64,128]{1,0:T(8,128)S(1)} %get-tuple-element.28), channel_id=1, source_target_pairs={{1,2},{2,1},{3,4},{4,3},{5,6},{6,5},{7,8},{8,7},{9,10},{10,9},{11,... | collective-permute-start | bytes 98312 | tf_op jit(solution)/shard_map/ppermute | solution.py:601
  38.1 0.0 all-to-all-done.rows
  38.1 0.0 collective-permute-done.1.after.even_in
  38.1 0.6 %spread.3 = f32[12,2,128]{2,1,0:T(2,128)} custom-call(f32[32,2,128]{2,1,0:T(2,128)S(1)} %all-to-all-done.rows, f32[64,128]{1,0:T(8,128)S(1)} %collective-permute-done.1.after.even_in), custom_call_target="tpu_custom_call" | custom-call | tf_op jit(solution)/shard_map/spread/pallas_call | solution.py:542
  38.8 9.3 %all-to-all-start.1 = ((f32[12,2,128]{2,1,0:T(2,128)}), f32[12,2,128]{2,1,0:T(2,128)S(1)}, u32[]{:S(2)}, u32[]{:S(2)}) async-start(f32[12,2,128]{2,1,0:T(2,128)} %spread.3), calls=%async_computation.1 | async-start | bytes 24576 | tf_op jit(solution)/shard_map/all_to_all | solution.py:553
  48.1 0.0 collective-permute-done.2.odd_y_in
  48.1 4.7 %third.1 = (f32[2,21,32,128]{3,2,1,0:T(8,128)S(1)}, f32[2,9,32,128]{3,2,1,0:T(8,128)S(1)}, f32[2,18,32,128]{3,2,1,0:T(8,128)S(1)}, f32[6,6,16,128]{3,2,1,0:T(8,128)S(1)}) custom-call(f32[18,16,128]{2,1,0:T(8,128)S(1)} %get-tuple-element.22.state, s32[3,16,128]{2,1,0:T(8,128)S(1)} %get-tuple-element.23.switch, f32[36,16,128]{2,1,0:T(8,128)S(1)} %get-tuple-element.24.edges, ...), custom_call_target="tpu_custom_call" | custom-call | flops 60000000 | bytes 60000000 | tf_op jit(solution)/shard_map/third/pallas_call | solution.py:521
  52.8 4.1 %all-to-all-done.1.totals = f32[12,2,128]{2,1,0:T(2,128)S(1)} async-done(((f32[12,2,128]{2,1,0:T(2,128)}), f32[12,2,128]{2,1,0:T(2,128)S(1)}, u32[]{:S(2)}, u32[]{:S(2)}) %all-to-all-start.1) | async-done | bytes 12320 | tf_op jit(solution)/shard_map/all_to_all | solution.py:553
  56.8 2.4 %fourth.1 = f32[6,3,16,128]{3,2,1,0:T(8,128)} custom-call(f32[12,2,128]{2,1,0:T(2,128)S(1)} %all-to-all-done.1.totals, f32[2,21,32,128]{3,2,1,0:T(8,128)S(1)} %get-tuple-element.29.fields, f32[2,9,32,128]{3,2,1,0:T(8,128)S(1)} %get-tuple-element.30.force, f32[2,18,32,128]{3,2,1,0:T(8,128)S(1)} %get-tuple-element.31.tend, ...), custom_call_target="tpu_custom_call" | custom-call | flops 8000000 | bytes 8000000 | tf_op jit(solution)/shard_map/fourth/pallas_call | solution.py:521
  (1 shorter events, 0.0 us)
Async XLA Ops:
  4.1 15.2 %collective-permute-start = (f32[66,8,128]{2,1,0:T(8,128)S(1)}, f32[66,8,128]{2,1,0:T(8,128)S(1)}, u32[]{:S(2)}, u32[]{:S(2)}) collective-permute-start(f32[66,8,128]{2,1,0:T(8,128)S(1)} %get-tuple-element.26), channel_id=1, source_target_pairs={{64,128},{128,64},{192,256},{256,192},{320,384},{384,320},{448,512... | collective-permute-start | bytes 811016 | tf_op jit(solution)/shard_map/ppermute | solution.py:591
  14.4 23.7 %all-to-all-start = ((f32[32,2,128]{2,1,0:T(2,128)}), f32[32,2,128]{2,1,0:T(2,128)S(1)}, u32[]{:S(2)}, u32[]{:S(2)}) async-start(f32[32,2,128]{2,1,0:T(2,128)} %spread.2), calls=%async_computation | async-start | bytes 65536 | tf_op jit(solution)/shard_map/all_to_all | solution.py:553
  19.8 18.4 %collective-permute-start.1 = (f32[64,128]{1,0:T(8,128)S(1)}, f32[64,128]{1,0:T(8,128)S(1)}, u32[]{:S(2)}, u32[]{:S(2)}) collective-permute-start(f32[64,128]{1,0:T(8,128)S(1)} %get-tuple-element.27), channel_id=1, source_target_pairs={{0,1},{1,0},{2,3},{3,2},{4,5},{5,4},{6,7},{7,6},{8,9},{9,8},{10,11... | collective-permute-start | bytes 98312 | tf_op jit(solution)/shard_map/ppermute | solution.py:600
  22.4 25.8 %collective-permute-start.2 = (f32[64,128]{1,0:T(8,128)S(1)}, f32[64,128]{1,0:T(8,128)S(1)}, u32[]{:S(2)}, u32[]{:S(2)}) collective-permute-start(f32[64,128]{1,0:T(8,128)S(1)} %get-tuple-element.28), channel_id=1, source_target_pairs={{1,2},{2,1},{3,4},{4,3},{5,6},{6,5},{7,8},{8,7},{9,10},{10,9},{11,... | collective-permute-start | bytes 98312 | tf_op jit(solution)/shard_map/ppermute | solution.py:601
  38.8 18.1 %all-to-all-start.1 = ((f32[12,2,128]{2,1,0:T(2,128)}), f32[12,2,128]{2,1,0:T(2,128)S(1)}, u32[]{:S(2)}, u32[]{:S(2)}) async-start(f32[12,2,128]{2,1,0:T(2,128)} %spread.3), calls=%async_computation.1 | async-start | bytes 24576 | tf_op jit(solution)/shard_map/all_to_all | solution.py:553

commit v8 on v7

--- a/solution.py
+++ b/solution.py
@@ -69,8 +69,8 @@
             zip((state_in, switch_in, edges_in, forcing_in), refs, strict=True)
         )
     ]
-    for copy in copies:
-        copy.start()
+    for k in (2, 0, 3, 1):
+        copies[k].start()
     odd, _ = parities()
     near = pl.multiple_of(8 * (1 - odd), 8)
     far = pl.multiple_of(8 * odd, 8)
@@ -439,10 +439,8 @@
         kinetic = 0.5 * inverse * (values[1] ** 2 + values[2] ** 2 + values[3] ** 2)
         values[5] = jnp.where(switch == 0.0, values[4] - kinetic, values[5])
 
-    @functools.partial(each, 6)
-    def _(step):
-        tile, plane = step // 3, step % 3
-        for row in CHUNKS:
+    def advance(tile, plane, chunks):
+        for row in chunks:
             rows = pl.ds(row, 8)
             values = [fields[tile, 3 * k + plane, rows, :] for k in range(7)]
             drive = [force[tile, 3 * k + plane, rows, :] for k in range(3)]
@@ -450,13 +448,19 @@
             stage = [values[k] + time_step * rate[k] for k in range(6)]
             inverse = 1.0 / stage[0]
             settle(stage, values[6], inverse)
-            for k in range(6):
-                section[tile, plane, k, rows, :] = stage[k]
+            if tile == 0:
+                for k in range(6):
+                    section[plane, k, rows, :] = stage[k]
             prims[tile, plane, 0, rows, :] = stage[0]
             for k in (1, 2, 3):
                 prims[tile, plane, k, rows, :] = stage[k] * inverse
             prims[tile, plane, 4, rows, :] = (ADIABATIC - 1.0) * stage[5]
             prims[tile, plane, 5, rows, :] = stage[5] * inverse
+
+    @functools.partial(each, 3)
+    def _(plane):
+        advance(0, plane, CHUNKS)
+        advance(1, plane, (8, 16))
 
     @functools.partial(each, 2)
     def _(step):
@@ -491,7 +495,7 @@
                 across = flux_ref[k, rows, :] - flux_ref[k, pl.ds(row - 1, 8), :]
                 rate.append(updated[k, plane, inner, :] - differences[0][k] - across)
             rate[5] = rate[5] - both[0][4] * spread
-            stage = [section[0, plane, k, rows, :] for k in range(6)]
+            stage = [section[plane, k, rows, :] for k in range(6)]
             drive = [force[0, 3 * k + plane, rows, :] for k in range(3)]
             rate = forced(stage, drive, rate)
             values = [fields[0, 3 * k + plane, rows, :] for k in range(7)]
@@ -627,7 +631,7 @@
         (totals, fields, force, tend, outer),
         [
             pltpu.VMEM((6, 3, ROWS, LANES), F32),
-            pltpu.VMEM((2, 3, 6, *extended), F32),
+            pltpu.VMEM((3, 6, *extended), F32),
             pltpu.VMEM((2, 3, 6, *extended), F32),
             *work,
             pltpu.SemaphoreType.DMA((3,)),

time: 59.6 us -> 59.4 us (level)
  no operation moved by 1% of the time
where the time goes in v8:
time: 59.4 us; the launch traced here: 59.1 us
  starting transfers between devices  41.9 us (71%)
  Pallas kernels  9.93 us (17%)
  waiting for transfers between devices  5.06 us (9%)
  blocking collectives  2.2 us (4%)
    ppermute x1, starting transfers between devices, local(): odd_y_in = lax.ppermute(strips[1], GY, pairs(count_y, 1))  15.8 us
    all_to_all x2, starting transfers between devices, exchanged(): return lax.all_to_all(spread, axes, 0, 0, tiled=True)  13.2 us
    ppermute x1, starting transfers between devices, local(): odd_in = lax.ppermute(odd_out, GX, pairs(count_x, 1))  10.3 us
    pallas_call x3, Pallas kernels, call(): pl.pallas_call(kernel, out_shape=outs, in_specs=vmem_specs(len(arrays)),...  7.4 us
    all_to_all x2, waiting for transfers between devices, exchanged(): return lax.all_to_all(spread, axes, 0, 0, tiled=True)  4.06 us
    ppermute x1, starting transfers between devices, local(): even_in = lax.ppermute(strips[0], GY, pairs(count_y, 0))  2.6 us
    all_gather x1, blocking collectives, local(): pair_in = lax.all_gather(pair_out, 'core')  2.2 us
    pallas_call x2, Pallas kernels, spread_over(): pl.pallas_call(spread_kernel, out_shape=shape(lax.axis_size(axes), 2, LAN...  1.27 us
  transfers between devices with their start and end apart: 5, of which 2 were waited for; matrix products, arithmetic and copies ran while one was open for 0% of the time, Pallas kernels for 10%

profile of v8, /device:TPU:64, one launch (start us, length us, event | category | flops | bytes accessed | tf_op | source)
XLA Modules:
  0.0 59.1 jit_solution(17824905610878875140)
XLA Ops:
  0.0 1.3 %first.1 = (f32[67,8,128]{2,1,0:T(8,128)S(1)}, f32[66,8,128]{2,1,0:T(8,128)S(1)}, f32[18,16,128]{2,1,0:T(8,128)S(1)}, s32[3,16,128]{2,1,0:T(8,128)S(1)}, f32[36,...) custom-call(f32[18,16,128]{2,1,0:T(8,128)} %bitcast.10, s32[3,16,128]{2,1,0:T(8,128)} %switch_in.1, ...), custom_call_target="tpu_custom_call" | custom-call | tf_op jit(solution)/shard_map/first/pallas_call | solution.py:576
  1.3 2.2 %all-gather = f32[134,8,128]{2,1,0:T(8,128)S(1)} all-gather(f32[67,8,128]{2,1,0:T(8,128)S(1)} %get-tuple-element.20), channel_id=2, replica_groups=mesh['zl'=6,'core'=2,'y'=8,'zh'=2,'x'=4] {'core'}, dimensions={0}, use_global_device_ids=true | all-gather | bytes 823296 | tf_op jit(solution)/shard_map/all_gather | solution.py:591
  3.5 0.6 %spread.2 = f32[32,2,128]{2,1,0:T(2,128)} custom-call(f32[2,2,128]{2,1,0:T(2,128)S(1)} %slice_bitcast_fusion.rows.after, f32[2,2,128]{2,1,0:T(2,128)S(1)} %slice_bitcast_fusion.rows.after), custom_call_target="tpu_custom_call" | custom-call | tf_op jit(solution)/shard_map/spread/pallas_call | solution.py:546
  4.1 10.3 %collective-permute-start = (f32[66,8,128]{2,1,0:T(8,128)S(1)}, f32[66,8,128]{2,1,0:T(8,128)S(1)}, u32[]{:S(2)}, u32[]{:S(2)}) collective-permute-start(f32[66,8,128]{2,1,0:T(8,128)S(1)} %get-tuple-element.26), channel_id=1, source_target_pairs={{64,128},{128,64},{192,256},{256,192},{320,384},{384,320},{448,512... | collective-permute-start | bytes 811016 | tf_op jit(solution)/shard_map/ppermute | solution.py:595
  14.4 3.9 %all-to-all-start = ((f32[32,2,128]{2,1,0:T(2,128)}), f32[32,2,128]{2,1,0:T(2,128)S(1)}, u32[]{:S(2)}, u32[]{:S(2)}) async-start(f32[32,2,128]{2,1,0:T(2,128)} %spread.2), calls=%async_computation | async-start | bytes 65536 | tf_op jit(solution)/shard_map/all_to_all | solution.py:557
  18.3 1.0 %collective-permute-done.odd_in = f32[66,8,128]{2,1,0:T(8,128)S(1)} collective-permute-done((f32[66,8,128]{2,1,0:T(8,128)S(1)}, f32[66,8,128]{2,1,0:T(8,128)S(1)}, u32[]{:S(2)}, u32[]{:S(2)}) %collective-permute-start) | collective-permute-done | bytes 270368 | tf_op jit(solution)/shard_map/ppermute | solution.py:595
  19.3 0.4 second.1
  19.7 2.6 %collective-permute-start.1 = (f32[64,128]{1,0:T(8,128)S(1)}, f32[64,128]{1,0:T(8,128)S(1)}, u32[]{:S(2)}, u32[]{:S(2)}) collective-permute-start(f32[64,128]{1,0:T(8,128)S(1)} %get-tuple-element.27), channel_id=1, source_target_pairs={{0,1},{1,0},{2,3},{3,2},{4,5},{5,4},{6,7},{7,6},{8,9},{9,8},{10,11... | collective-permute-start | bytes 98312 | tf_op jit(solution)/shard_map/ppermute | solution.py:604
  22.3 15.8 %collective-permute-start.2 = (f32[64,128]{1,0:T(8,128)S(1)}, f32[64,128]{1,0:T(8,128)S(1)}, u32[]{:S(2)}, u32[]{:S(2)}) collective-permute-start(f32[64,128]{1,0:T(8,128)S(1)} %get-tuple-element.28), channel_id=1, source_target_pairs={{1,2},{2,1},{3,4},{4,3},{5,6},{6,5},{7,8},{8,7},{9,10},{10,9},{11,... | collective-permute-start | bytes 98312 | tf_op jit(solution)/shard_map/ppermute | solution.py:605
  38.1 0.0 all-to-all-done.rows
  38.1 0.0 collective-permute-done.1.after.even_in
  38.1 0.6 %spread.3 = f32[12,2,128]{2,1,0:T(2,128)} custom-call(f32[32,2,128]{2,1,0:T(2,128)S(1)} %all-to-all-done.rows, f32[64,128]{1,0:T(8,128)S(1)} %collective-permute-done.1.after.even_in), custom_call_target="tpu_custom_call" | custom-call | tf_op jit(solution)/shard_map/spread/pallas_call | solution.py:546
  38.8 9.3 %all-to-all-start.1 = ((f32[12,2,128]{2,1,0:T(2,128)}), f32[12,2,128]{2,1,0:T(2,128)S(1)}, u32[]{:S(2)}, u32[]{:S(2)}) async-start(f32[12,2,128]{2,1,0:T(2,128)} %spread.3), calls=%async_computation.1 | async-start | bytes 24576 | tf_op jit(solution)/shard_map/all_to_all | solution.py:557
  48.1 0.0 collective-permute-done.2.odd_y_in
  48.1 4.7 %third.1 = (f32[2,21,32,128]{3,2,1,0:T(8,128)S(1)}, f32[2,9,32,128]{3,2,1,0:T(8,128)S(1)}, f32[2,18,32,128]{3,2,1,0:T(8,128)S(1)}, f32[6,6,16,128]{3,2,1,0:T(8,128)S(1)}) custom-call(f32[18,16,128]{2,1,0:T(8,128)S(1)} %get-tuple-element.22.state, s32[3,16,128]{2,1,0:T(8,128)S(1)} %get-tuple-element.23.switch, f32[36,16,128]{2,1,0:T(8,128)S(1)} %get-tuple-element.24.edges, ...), custom_call_target="tpu_custom_call" | custom-call | flops 60000000 | bytes 60000000 | tf_op jit(solution)/shard_map/third/pallas_call | solution.py:525
  52.8 4.1 %all-to-all-done.1.totals = f32[12,2,128]{2,1,0:T(2,128)S(1)} async-done(((f32[12,2,128]{2,1,0:T(2,128)}), f32[12,2,128]{2,1,0:T(2,128)S(1)}, u32[]{:S(2)}, u32[]{:S(2)}) %all-to-all-start.1) | async-done | bytes 12320 | tf_op jit(solution)/shard_map/all_to_all | solution.py:557
  56.8 2.3 %fourth.1 = f32[6,3,16,128]{3,2,1,0:T(8,128)} custom-call(f32[12,2,128]{2,1,0:T(2,128)S(1)} %all-to-all-done.1.totals, f32[2,21,32,128]{3,2,1,0:T(8,128)S(1)} %get-tuple-element.29.fields, f32[2,9,32,128]{3,2,1,0:T(8,128)S(1)} %get-tuple-element.30.force, f32[2,18,32,128]{3,2,1,0:T(8,128)S(1)} %get-tuple-element.31.tend, ...), custom_call_target="tpu_custom_call" | custom-call | flops 8000000 | bytes 8000000 | tf_op jit(solution)/shard_map/fourth/pallas_call | solution.py:525
  (1 shorter events, 0.0 us)
Async XLA Ops:
  4.1 15.2 %collective-permute-start = (f32[66,8,128]{2,1,0:T(8,128)S(1)}, f32[66,8,128]{2,1,0:T(8,128)S(1)}, u32[]{:S(2)}, u32[]{:S(2)}) collective-permute-start(f32[66,8,128]{2,1,0:T(8,128)S(1)} %get-tuple-element.26), channel_id=1, source_target_pairs={{64,128},{128,64},{192,256},{256,192},{320,384},{384,320},{448,512... | collective-permute-start | bytes 811016 | tf_op jit(solution)/shard_map/ppermute | solution.py:595
  14.4 23.7 %all-to-all-start = ((f32[32,2,128]{2,1,0:T(2,128)}), f32[32,2,128]{2,1,0:T(2,128)S(1)}, u32[]{:S(2)}, u32[]{:S(2)}) async-start(f32[32,2,128]{2,1,0:T(2,128)} %spread.2), calls=%async_computation | async-start | bytes 65536 | tf_op jit(solution)/shard_map/all_to_all | solution.py:557
  19.7 18.4 %collective-permute-start.1 = (f32[64,128]{1,0:T(8,128)S(1)}, f32[64,128]{1,0:T(8,128)S(1)}, u32[]{:S(2)}, u32[]{:S(2)}) collective-permute-start(f32[64,128]{1,0:T(8,128)S(1)} %get-tuple-element.27), channel_id=1, source_target_pairs={{0,1},{1,0},{2,3},{3,2},{4,5},{5,4},{6,7},{7,6},{8,9},{9,8},{10,11... | collective-permute-start | bytes 98312 | tf_op jit(solution)/shard_map/ppermute | solution.py:604
  22.3 25.8 %collective-permute-start.2 = (f32[64,128]{1,0:T(8,128)S(1)}, f32[64,128]{1,0:T(8,128)S(1)}, u32[]{:S(2)}, u32[]{:S(2)}) collective-permute-start(f32[64,128]{1,0:T(8,128)S(1)} %get-tuple-element.28), channel_id=1, source_target_pairs={{1,2},{2,1},{3,4},{4,3},{5,6},{6,5},{7,8},{8,7},{9,10},{10,9},{11,... | collective-permute-start | bytes 98312 | tf_op jit(solution)/shard_map/ppermute | solution.py:605
  38.8 18.1 %all-to-all-start.1 = ((f32[12,2,128]{2,1,0:T(2,128)}), f32[12,2,128]{2,1,0:T(2,128)S(1)}, u32[]{:S(2)}, u32[]{:S(2)}) async-start(f32[12,2,128]{2,1,0:T(2,128)} %spread.3), calls=%async_computation.1 | async-start | bytes 24576 | tf_op jit(solution)/shard_map/all_to_all | solution.py:557

commit v9 on v8

--- a/solution.py
+++ b/solution.py
@@ -17,7 +17,8 @@
 FIELDS = 21
 EDGES = 36
 FORCES = 9
-X_TILES = FIELDS + EDGES + FORCES
+HALVES = 23
+PAYLOAD = FIELDS + HALVES
 VMEM_LIMIT = 16 * 1024 * 1024
 F32 = jnp.float32
 
@@ -93,12 +94,20 @@
         peak = speed if peak is None else jnp.maximum(peak, speed)
         total = power if total is None else total + power
     row = lax.broadcasted_iota(jnp.int32, (8, LANES), 0)
-    pair_out[X_TILES] = jnp.where(row == 0, jnp.max(peak), jnp.sum(total))
+    pair_out[PAYLOAD] = jnp.where(row == 0, jnp.max(peak), jnp.sum(total))
     copies[2].wait()
-    for index in range(X_TILES):
-        tile = x_place(refs, index)
-        pair_out[index] = tile(pl.ds(near, 8))
-        odd_out[index] = tile(pl.ds(far, 8))
+    upper = lax.broadcasted_iota(jnp.int32, (8, LANES), 0) // 4
+    for out, start, keep in (
+        (pair_out, near, upper == 1 - odd),
+        (odd_out, far, upper == odd),
+    ):
+        rows = pl.ds(start, 8)
+        for index in range(PAYLOAD):
+            tile = x_place(refs, index)(rows)
+            if index >= FIELDS and index + HALVES < FIELDS + EDGES + FORCES:
+                other = x_place(refs, index + HALVES)(rows)
+                tile = jnp.where(keep, tile, roll(other, 4, 0))
+            out[index] = tile
 
 
 def spread_kernel(rows, after, out):
@@ -114,6 +123,21 @@
     below = jnp.where(odd_x == 0, from_odd, from_pair)
     above = jnp.where(odd_x == 0, from_pair, from_odd)
     return jnp.concatenate([below, block, above], axis=0)
+
+
+def rows_around_half(odd_x, pair_in, odd_in, index, block):
+    second = index >= HALVES
+    slot = FIELDS + jnp.where(second, index - HALVES, index)
+    column = rows_around(odd_x, pair_in, odd_in, slot, block)
+    below, above = column[0:8], column[ROWS + 8 :]
+    return jnp.concatenate(
+        [
+            jnp.where(second, roll(below, 4, 0), below),
+            block,
+            jnp.where(second, roll(above, 4, 0), above),
+        ],
+        axis=0,
+    )
 
 
 def turned(values, shift):
@@ -332,8 +356,8 @@
     def _(part):
         for k in range(3):
             index = 3 * part + k
-            force[0, index] = rows_around(
-                odd_x, pair_in, odd_in, FIELDS + EDGES + index, forcing[index]
+            force[0, index] = rows_around_half(
+                odd_x, pair_in, odd_in, EDGES + index, forcing[index]
             )
             force[1, index, 0:8] = jnp.zeros((8, LANES), F32)
             force[1, index, 8:24] = rim_tile(EXT + ROWS, index)
@@ -358,7 +382,7 @@
         first = 18 * (step // 3) + step % 3
         places = [first + 3 * k for k in range(6)]
         values = edge_primitives(
-            [rows_around(odd_x, pair_in, odd_in, FIELDS + k, edges[k]) for k in places]
+            [rows_around_half(odd_x, pair_in, odd_in, k, edges[k]) for k in places]
         )
         for k in range(6):
             planes[0, step, k] = values[k]
@@ -576,8 +600,8 @@
     pair_out, odd_out, *arrays = pl.pallas_call(
         first_kernel,
         out_shape=(
-            shape(X_TILES + 1, *tile),
-            shape(X_TILES, *tile),
+            shape(PAYLOAD + 1, *tile),
+            shape(PAYLOAD, *tile),
             *(jax.ShapeDtypeStruct(values.shape, values.dtype) for values in inputs),
         ),
         in_specs=[
@@ -589,7 +613,7 @@
         name="first",
     )(*(pltpu.with_memory_space_constraint(values, pltpu.HBM) for values in inputs))
     pair_in = lax.all_gather(pair_out, "core")
-    rows = pair_in[:, X_TILES, 0:2]
+    rows = pair_in[:, PAYLOAD, 0:2]
     spread = spread_over(rows, rows, ("y", "x"))
     odd_out, spread = lax.optimization_barrier((odd_out, spread))
     odd_in = lax.ppermute(odd_out, GX, pairs(count_x, 1))

time: 59.4 us -> 59.3 us (level)
  waiting for transfers between devices: 5.06 us -> 3.99 us
  starting transfers between devices: 41.9 us -> 42.8 us
    ppermute x1, waiting for transfers between devices: 1 us -> 0.01 us  [local(): odd_in = lax.ppermute(odd_out, GX, pairs(count_x, 1))]
    ppermute x1, starting transfers between devices: 2.6 us -> 3.59 us  [local(): even_in = lax.ppermute(strips[0], GY, pairs(count_y, 0))]
  transfers between devices with their start and end apart: 5 -> 5, of which waited for: 2 -> 1; matrix products, arithmetic and copies ran while one was open for 0% -> 0% of each run, Pallas kernels for 10% -> 10%
where the time goes in v9:
time: 59.3 us; the launch traced here: 59 us
  starting transfers between devices  42.8 us (72%)
  Pallas kernels  10 us (17%)
  waiting for transfers between devices  3.99 us (7%)
  blocking collectives  2.07 us (3%)
    ppermute x1, starting transfers between devices, local(): odd_y_in = lax.ppermute(strips[1], GY, pairs(count_y, 1))  15.8 us
    all_to_all x2, starting transfers between devices, exchanged(): return lax.all_to_all(spread, axes, 0, 0, tiled=True)  13.2 us
    ppermute x1, starting transfers between devices, local(): odd_in = lax.ppermute(odd_out, GX, pairs(count_x, 1))  10.3 us
    pallas_call x3, Pallas kernels, call(): pl.pallas_call(kernel, out_shape=outs, in_specs=vmem_specs(len(arrays)),...  7.48 us
    all_to_all x2, waiting for transfers between devices, exchanged(): return lax.all_to_all(spread, axes, 0, 0, tiled=True)  3.98 us
    ppermute x1, starting transfers between devices, local(): even_in = lax.ppermute(strips[0], GY, pairs(count_y, 0))  3.59 us
    all_gather x1, blocking collectives, local(): pair_in = lax.all_gather(pair_out, 'core')  2.07 us
    pallas_call x1, Pallas kernels, local(): pl.pallas_call(first_kernel, out_shape=(shape(PAYLOAD + 1, *tile), shape(...  1.27 us
  transfers between devices with their start and end apart: 5, of which 1 were waited for; matrix products, arithmetic and copies ran while one was open for 0% of the time, Pallas kernels for 10%

profile of v9, /device:TPU:64, one launch (start us, length us, event | category | flops | bytes accessed | tf_op | source)
XLA Modules:
  0.0 59.0 jit_solution(1035042371250895785)
XLA Ops:
  0.0 1.3 %first.1 = (f32[45,8,128]{2,1,0:T(8,128)S(1)}, f32[44,8,128]{2,1,0:T(8,128)S(1)}, f32[18,16,128]{2,1,0:T(8,128)S(1)}, s32[3,16,128]{2,1,0:T(8,128)S(1)}, f32[36,...) custom-call(f32[18,16,128]{2,1,0:T(8,128)} %bitcast.10, s32[3,16,128]{2,1,0:T(8,128)} %switch_in.1, ...), custom_call_target="tpu_custom_call" | custom-call | tf_op jit(solution)/shard_map/first/pallas_call | solution.py:600
  1.3 2.1 %all-gather = f32[90,8,128]{2,1,0:T(8,128)S(1)} all-gather(f32[45,8,128]{2,1,0:T(8,128)S(1)} %get-tuple-element.20), channel_id=2, replica_groups=mesh['zl'=6,'core'=2,'y'=8,'zh'=2,'x'=4] {'core'}, dimensions={0}, use_global_device_ids=true | all-gather | bytes 552960 | tf_op jit(solution)/shard_map/all_gather | solution.py:615
  3.4 0.6 %spread.2 = f32[32,2,128]{2,1,0:T(2,128)} custom-call(f32[2,2,128]{2,1,0:T(2,128)S(1)} %slice_bitcast_fusion.rows.after, f32[2,2,128]{2,1,0:T(2,128)S(1)} %slice_bitcast_fusion.rows.after), custom_call_target="tpu_custom_call" | custom-call | tf_op jit(solution)/shard_map/spread/pallas_call | solution.py:570
  4.0 10.3 %collective-permute-start = (f32[44,8,128]{2,1,0:T(8,128)S(1)}, f32[44,8,128]{2,1,0:T(8,128)S(1)}, u32[]{:S(2)}, u32[]{:S(2)}) collective-permute-start(f32[44,8,128]{2,1,0:T(8,128)S(1)} %get-tuple-element.26), channel_id=1, source_target_pairs={{64,128},{128,64},{192,256},{256,192},{320,384},{384,320},{448,512... | collective-permute-start | bytes 540680 | tf_op jit(solution)/shard_map/ppermute | solution.py:619
  14.3 3.9 %all-to-all-start = ((f32[32,2,128]{2,1,0:T(2,128)}), f32[32,2,128]{2,1,0:T(2,128)S(1)}, u32[]{:S(2)}, u32[]{:S(2)}) async-start(f32[32,2,128]{2,1,0:T(2,128)} %spread.2), calls=%async_computation | async-start | bytes 65536 | tf_op jit(solution)/shard_map/all_to_all | solution.py:581
  18.2 0.0 collective-permute-done.odd_in
  18.2 0.4 second.1
  18.6 3.6 %collective-permute-start.1 = (f32[64,128]{1,0:T(8,128)S(1)}, f32[64,128]{1,0:T(8,128)S(1)}, u32[]{:S(2)}, u32[]{:S(2)}) collective-permute-start(f32[64,128]{1,0:T(8,128)S(1)} %get-tuple-element.27), channel_id=1, source_target_pairs={{0,1},{1,0},{2,3},{3,2},{4,5},{5,4},{6,7},{7,6},{8,9},{9,8},{10,11... | collective-permute-start | bytes 98312 | tf_op jit(solution)/shard_map/ppermute | solution.py:628
  22.2 15.8 %collective-permute-start.2 = (f32[64,128]{1,0:T(8,128)S(1)}, f32[64,128]{1,0:T(8,128)S(1)}, u32[]{:S(2)}, u32[]{:S(2)}) collective-permute-start(f32[64,128]{1,0:T(8,128)S(1)} %get-tuple-element.28), channel_id=1, source_target_pairs={{1,2},{2,1},{3,4},{4,3},{5,6},{6,5},{7,8},{8,7},{9,10},{10,9},{11,... | collective-permute-start | bytes 98312 | tf_op jit(solution)/shard_map/ppermute | solution.py:629
  38.0 0.0 all-to-all-done.rows
  38.0 0.0 collective-permute-done.1.after.even_in
  38.0 0.6 %spread.3 = f32[12,2,128]{2,1,0:T(2,128)} custom-call(f32[32,2,128]{2,1,0:T(2,128)S(1)} %all-to-all-done.rows, f32[64,128]{1,0:T(8,128)S(1)} %collective-permute-done.1.after.even_in), custom_call_target="tpu_custom_call" | custom-call | tf_op jit(solution)/shard_map/spread/pallas_call | solution.py:570
  38.6 9.3 %all-to-all-start.1 = ((f32[12,2,128]{2,1,0:T(2,128)}), f32[12,2,128]{2,1,0:T(2,128)S(1)}, u32[]{:S(2)}, u32[]{:S(2)}) async-start(f32[12,2,128]{2,1,0:T(2,128)} %spread.3), calls=%async_computation.1 | async-start | bytes 24576 | tf_op jit(solution)/shard_map/all_to_all | solution.py:581
  48.0 0.0 collective-permute-done.2.odd_y_in
  48.0 4.7 %third.1 = (f32[2,21,32,128]{3,2,1,0:T(8,128)S(1)}, f32[2,9,32,128]{3,2,1,0:T(8,128)S(1)}, f32[2,18,32,128]{3,2,1,0:T(8,128)S(1)}, f32[6,6,16,128]{3,2,1,0:T(8,128)S(1)}) custom-call(f32[18,16,128]{2,1,0:T(8,128)S(1)} %get-tuple-element.22.state, s32[3,16,128]{2,1,0:T(8,128)S(1)} %get-tuple-element.23.switch, f32[36,16,128]{2,1,0:T(8,128)S(1)} %get-tuple-element.24.edges, ...), custom_call_target="tpu_custom_call" | custom-call | flops 60000000 | bytes 60000000 | tf_op jit(solution)/shard_map/third/pallas_call | solution.py:549
  52.7 4.0 %all-to-all-done.1.totals = f32[12,2,128]{2,1,0:T(2,128)S(1)} async-done(((f32[12,2,128]{2,1,0:T(2,128)}), f32[12,2,128]{2,1,0:T(2,128)S(1)}, u32[]{:S(2)}, u32[]{:S(2)}) %all-to-all-start.1) | async-done | bytes 12320 | tf_op jit(solution)/shard_map/all_to_all | solution.py:581
  56.7 2.3 %fourth.1 = f32[6,3,16,128]{3,2,1,0:T(8,128)} custom-call(f32[12,2,128]{2,1,0:T(2,128)S(1)} %all-to-all-done.1.totals, f32[2,21,32,128]{3,2,1,0:T(8,128)S(1)} %get-tuple-element.29.fields, f32[2,9,32,128]{3,2,1,0:T(8,128)S(1)} %get-tuple-element.30.force, f32[2,18,32,128]{3,2,1,0:T(8,128)S(1)} %get-tuple-element.31.tend, ...), custom_call_target="tpu_custom_call" | custom-call | flops 8000000 | bytes 8000000 | tf_op jit(solution)/shard_map/fourth/pallas_call | solution.py:549
  (1 shorter events, 0.0 us)
Async XLA Ops:
  4.0 14.2 %collective-permute-start = (f32[44,8,128]{2,1,0:T(8,128)S(1)}, f32[44,8,128]{2,1,0:T(8,128)S(1)}, u32[]{:S(2)}, u32[]{:S(2)}) collective-permute-start(f32[44,8,128]{2,1,0:T(8,128)S(1)} %get-tuple-element.26), channel_id=1, source_target_pairs={{64,128},{128,64},{192,256},{256,192},{320,384},{384,320},{448,512... | collective-permute-start | bytes 540680 | tf_op jit(solution)/shard_map/ppermute | solution.py:619
  14.3 23.7 %all-to-all-start = ((f32[32,2,128]{2,1,0:T(2,128)}), f32[32,2,128]{2,1,0:T(2,128)S(1)}, u32[]{:S(2)}, u32[]{:S(2)}) async-start(f32[32,2,128]{2,1,0:T(2,128)} %spread.2), calls=%async_computation | async-start | bytes 65536 | tf_op jit(solution)/shard_map/all_to_all | solution.py:581
  18.6 19.4 %collective-permute-start.1 = (f32[64,128]{1,0:T(8,128)S(1)}, f32[64,128]{1,0:T(8,128)S(1)}, u32[]{:S(2)}, u32[]{:S(2)}) collective-permute-start(f32[64,128]{1,0:T(8,128)S(1)} %get-tuple-element.27), channel_id=1, source_target_pairs={{0,1},{1,0},{2,3},{3,2},{4,5},{5,4},{6,7},{7,6},{8,9},{9,8},{10,11... | collective-permute-start | bytes 98312 | tf_op jit(solution)/shard_map/ppermute | solution.py:628
  22.2 25.8 %collective-permute-start.2 = (f32[64,128]{1,0:T(8,128)S(1)}, f32[64,128]{1,0:T(8,128)S(1)}, u32[]{:S(2)}, u32[]{:S(2)}) collective-permute-start(f32[64,128]{1,0:T(8,128)S(1)} %get-tuple-element.28), channel_id=1, source_target_pairs={{1,2},{2,1},{3,4},{4,3},{5,6},{6,5},{7,8},{8,7},{9,10},{10,9},{11,... | collective-permute-start | bytes 98312 | tf_op jit(solution)/shard_map/ppermute | solution.py:629
  38.6 18.1 %all-to-all-start.1 = ((f32[12,2,128]{2,1,0:T(2,128)}), f32[12,2,128]{2,1,0:T(2,128)S(1)}, u32[]{:S(2)}, u32[]{:S(2)}) async-start(f32[12,2,128]{2,1,0:T(2,128)} %spread.3), calls=%async_computation.1 | async-start | bytes 24576 | tf_op jit(solution)/shard_map/all_to_all | solution.py:581

commit v10 on v8

--- a/solution.py
+++ b/solution.py
@@ -295,7 +295,7 @@
 
 def third_kernel(
     state, switch, edges, forcing, pair_in, odd_in, even_in, odd_y_in,
-    fields, force, tend, outer, prims, planes, low_ref, high_ref, face_ref, flux_ref, strip_ref,
+    fields, force, push, tend, outer, prims, planes, low_ref, high_ref, face_ref, flux_ref, strip_ref,
 ):
     odd_x, odd_y = parities()
     strip_ref[0] = jnp.where(odd_y == 0, even_in[...], odd_y_in[...])
@@ -350,6 +350,12 @@
         prims[tile, plane, 0] = density
         for k in (1, 2, 3):
             prims[tile, plane, k] = values[k] * inverse
+        drive = [force[tile, 3 * k + plane] for k in range(3)]
+        for k in range(3):
+            push[tile, 3 * k + plane] = density * drive[k]
+        push[tile, 9 + plane] = (
+            values[1] * drive[0] + values[2] * drive[1] + values[3] * drive[2]
+        )
         prims[tile, plane, 4] = (ADIABATIC - 1.0) * heat
         prims[tile, plane, 5] = values[5] * inverse
 
@@ -417,7 +423,7 @@
 
 
 def fourth_kernel(
-    cells, totals, fields, force, tend, outer_prims, out,
+    cells, totals, fields, force, push, tend, outer_prims, out,
     updated, section, prims, low_ref, high_ref, face_ref, flux_ref, sent,
 ):
     peak = jnp.max(totals[:, 0, :], axis=0, keepdims=True)
@@ -443,8 +449,9 @@
         for row in chunks:
             rows = pl.ds(row, 8)
             values = [fields[tile, 3 * k + plane, rows, :] for k in range(7)]
-            drive = [force[tile, 3 * k + plane, rows, :] for k in range(3)]
-            rate = forced(values, drive, [tend[tile, 3 * k + plane, rows, :] for k in range(6)])
+            rate = [tend[tile, 3 * k + plane, rows, :] for k in range(6)]
+            for k in range(4):
+                rate[1 + k] = rate[1 + k] + scale * push[tile, 3 * k + plane, rows, :]
             stage = [values[k] + time_step * rate[k] for k in range(6)]
             inverse = 1.0 / stage[0]
             settle(stage, values[6], inverse)
@@ -606,12 +613,13 @@
     totals = exchanged(spread_over(totals, even_in, ("zh", "zl")), ("zh", "zl"))
     extended = (EXT, LANES)
     work = [pltpu.VMEM((6, *extended), F32) for _ in range(4)]
-    fields, force, tend, outer = call(
+    fields, force, push, tend, outer = call(
         third_kernel,
         "third",
         (
             shape(2, FIELDS, *extended),
             shape(2, FORCES, *extended),
+            shape(2, 12, *extended),
             shape(2, 18, *extended),
             shape(6, 6, ROWS, LANES),
         ),
@@ -628,7 +636,7 @@
         functools.partial(fourth_kernel, cells),
         "fourth",
         shape(6, 3, ROWS, LANES),
-        (totals, fields, force, tend, outer),
+        (totals, fields, force, push, tend, outer),
         [
             pltpu.VMEM((6, 3, ROWS, LANES), F32),
             pltpu.VMEM((3, 6, *extended), F32),

time: 59.4 us -> 61.1 us (1.029)
  local copies, waits for them, and re-layouts: 0.01 us -> 2.98 us
  waiting for transfers between devices: 5.06 us -> 2.18 us
  Pallas kernels: 9.93 us -> 10.6 us
    unnamed x0 -> x12, local copies, waits for them, and re-layouts: none -> 2.98 us
    all_to_all x2, waiting for transfers between devices: 4.06 us -> 1.16 us  [exchanged(): return lax.all_to_all(spread, axes, 0, 0, tiled=True)]
    pallas_call x3, Pallas kernels: 7.4 us -> 8.11 us  [call(): pl.pallas_call(kernel, out_shape=outs, in_specs=vmem_specs(len(arrays)),...]
  transfers between devices with their start and end apart: 5 -> 5, of which waited for: 2 -> 2; matrix products, arithmetic and copies ran while one was open for 0% -> 0% of each run, Pallas kernels for 10% -> 9%
where the time goes in v10:
time: 61.1 us; the launch traced here: 60.5 us
  starting transfers between devices  42.4 us (69%)
  Pallas kernels  10.6 us (17%)
  local copies, waits for them, and re-layouts  2.98 us (5%)
  blocking collectives  2.2 us (4%)
  waiting for transfers between devices  2.18 us (4%)
    ppermute x1, starting transfers between devices, local(): odd_y_in = lax.ppermute(strips[1], GY, pairs(count_y, 1))  15.8 us
    all_to_all x2, starting transfers between devices, exchanged(): return lax.all_to_all(spread, axes, 0, 0, tiled=True)  13.8 us
    ppermute x1, starting transfers between devices, local(): odd_in = lax.ppermute(odd_out, GX, pairs(count_x, 1))  10.3 us
    pallas_call x3, Pallas kernels, call(): pl.pallas_call(kernel, out_shape=outs, in_specs=vmem_specs(len(arrays)),...  8.11 us
    unnamed x12, local copies, waits for them, and re-layouts  2.98 us
    ppermute x1, starting transfers between devices, local(): even_in = lax.ppermute(strips[0], GY, pairs(count_y, 0))  2.6 us
    all_gather x1, blocking collectives, local(): pair_in = lax.all_gather(pair_out, 'core')  2.2 us
    pallas_call x1, Pallas kernels, local(): pl.pallas_call(first_kernel, out_shape=(shape(X_TILES + 1, *tile), shape(...  1.27 us
  transfers between devices with their start and end apart: 5, of which 2 were waited for; matrix products, arithmetic and copies ran while one was open for 0% of the time, Pallas kernels for 9%

profile of v10, /device:TPU:64, one launch (start us, length us, event | category | flops | bytes accessed | tf_op | source)
XLA Modules:
  0.0 60.5 jit_solution(7031480023845655038)
XLA Ops:
  0.0 1.3 %first.1 = (f32[67,8,128]{2,1,0:T(8,128)S(1)}, f32[66,8,128]{2,1,0:T(8,128)S(1)}, f32[18,16,128]{2,1,0:T(8,128)S(1)}, s32[3,16,128]{2,1,0:T(8,128)S(1)}, f32[36,...) custom-call(f32[18,16,128]{2,1,0:T(8,128)} %bitcast.10, s32[3,16,128]{2,1,0:T(8,128)} %switch_in.1, ...), custom_call_target="tpu_custom_call" | custom-call | tf_op jit(solution)/shard_map/first/pallas_call | solution.py:583
  1.3 0.0 copy-start
  1.3 0.0 copy-start.2
  1.3 2.2 %all-gather = f32[134,8,128]{2,1,0:T(8,128)S(1)} all-gather(f32[67,8,128]{2,1,0:T(8,128)S(1)} %get-tuple-element.21), channel_id=2, replica_groups=mesh['zl'=6,'core'=2,'y'=8,'zh'=2,'x'=4] {'core'}, dimensions={0}, use_global_device_ids=true | all-gather | bytes 823296 | tf_op jit(solution)/shard_map/all_gather | solution.py:598
  3.5 0.6 %spread.2 = f32[32,2,128]{2,1,0:T(2,128)} custom-call(f32[2,2,128]{2,1,0:T(2,128)S(1)} %slice_bitcast_fusion.rows.after, f32[2,2,128]{2,1,0:T(2,128)S(1)} %slice_bitcast_fusion.rows.after), custom_call_target="tpu_custom_call" | custom-call | tf_op jit(solution)/shard_map/spread/pallas_call | solution.py:553
  4.1 10.3 %collective-permute-start = (f32[66,8,128]{2,1,0:T(8,128)S(1)}, f32[66,8,128]{2,1,0:T(8,128)S(1)}, u32[]{:S(2)}, u32[]{:S(2)}) collective-permute-start(f32[66,8,128]{2,1,0:T(8,128)S(1)} %get-tuple-element.27), channel_id=1, source_target_pairs={{64,128},{128,64},{192,256},{256,192},{320,384},{384,320},{448,512... | collective-permute-start | bytes 811016 | tf_op jit(solution)/shard_map/ppermute | solution.py:602
  14.4 3.8 %all-to-all-start = ((f32[32,2,128]{2,1,0:T(2,128)}), f32[32,2,128]{2,1,0:T(2,128)S(1)}, u32[]{:S(2)}, u32[]{:S(2)}) async-start(f32[32,2,128]{2,1,0:T(2,128)} %spread.2), calls=%async_computation | async-start | bytes 65536 | tf_op jit(solution)/shard_map/all_to_all | solution.py:564
  18.3 1.0 %collective-permute-done.odd_in = f32[66,8,128]{2,1,0:T(8,128)S(1)} collective-permute-done((f32[66,8,128]{2,1,0:T(8,128)S(1)}, f32[66,8,128]{2,1,0:T(8,128)S(1)}, u32[]{:S(2)}, u32[]{:S(2)}) %collective-permute-start) | collective-permute-done | bytes 270368 | tf_op jit(solution)/shard_map/ppermute | solution.py:602
  19.3 0.0 copy-done
  19.3 0.4 second.1
  19.7 2.6 %collective-permute-start.1 = (f32[64,128]{1,0:T(8,128)S(1)}, f32[64,128]{1,0:T(8,128)S(1)}, u32[]{:S(2)}, u32[]{:S(2)}) collective-permute-start(f32[64,128]{1,0:T(8,128)S(1)} %get-tuple-element.28), channel_id=1, source_target_pairs={{0,1},{1,0},{2,3},{3,2},{4,5},{5,4},{6,7},{7,6},{8,9},{9,8},{10,11... | collective-permute-start | bytes 98312 | tf_op jit(solution)/shard_map/ppermute | solution.py:611
  22.4 15.8 %collective-permute-start.2 = (f32[64,128]{1,0:T(8,128)S(1)}, f32[64,128]{1,0:T(8,128)S(1)}, u32[]{:S(2)}, u32[]{:S(2)}) collective-permute-start(f32[64,128]{1,0:T(8,128)S(1)} %get-tuple-element.29), channel_id=1, source_target_pairs={{1,2},{2,1},{3,4},{4,3},{5,6},{6,5},{7,8},{8,7},{9,10},{10,9},{11,... | collective-permute-start | bytes 98312 | tf_op jit(solution)/shard_map/ppermute | solution.py:612
  38.1 0.0 all-to-all-done.rows
  38.1 0.0 collective-permute-done.1.after.even_in
  38.2 0.6 %spread.3 = f32[12,2,128]{2,1,0:T(2,128)} custom-call(f32[32,2,128]{2,1,0:T(2,128)S(1)} %all-to-all-done.rows, f32[64,128]{1,0:T(8,128)S(1)} %collective-permute-done.1.after.even_in), custom_call_target="tpu_custom_call" | custom-call | tf_op jit(solution)/shard_map/spread/pallas_call | solution.py:553
  38.8 9.9 %all-to-all-start.1 = ((f32[12,2,128]{2,1,0:T(2,128)}), f32[12,2,128]{2,1,0:T(2,128)}, u32[]{:S(2)}, u32[]{:S(2)}) async-start(f32[12,2,128]{2,1,0:T(2,128)} %spread.3), calls=%async_computation.1 | async-start | bytes 24576 | tf_op jit(solution)/shard_map/all_to_all | solution.py:564
  48.7 0.0 collective-permute-done.2.odd_y_in
  48.7 0.6 copy-done.4
  49.3 0.9 %copy-done.1 = f32[9,16,128]{2,1,0:T(8,128)S(1)} copy-done((f32[9,16,128]{2,1,0:T(8,128)S(1)}, f32[9,16,128]{2,1,0:T(8,128)}, u32[]{:S(2)}) %copy-start.1) | copy-done | bytes 73752
  50.2 0.7 %copy-done.3 = s32[3,16,128]{2,1,0:T(8,128)S(1)} copy-done((s32[3,16,128]{2,1,0:T(8,128)S(1)}, s32[3,16,128]{2,1,0:T(8,128)}, u32[]{:S(2)}) %copy-start.3) | copy-done | bytes 24600
  50.9 0.8 %copy-done.5 = f32[64,128]{1,0:T(8,128)S(1)} copy-done((f32[64,128]{1,0:T(8,128)S(1)}, f32[64,128]{1,0:T(8,128)}, u32[]{:S(2)}) %copy-start.5) | copy-done | bytes 32792
  51.7 4.7 %third.1 = (f32[2,21,32,128]{3,2,1,0:T(8,128)S(1)}, f32[2,9,32,128]{3,2,1,0:T(8,128)S(1)}, f32[2,12,32,128]{3,2,1,0:T(8,128)S(1)}, f32[2,18,32,128]{3,2,1,0:T(8,128)S(1)}, f32[6,6,16,128]{3,2,1,0:T(8,128)S(1)}) custom-call(f32[18,16,128]{2,1,0:T(8,128)S(1)} %get-tuple-element.23.state, s32[3,16,128]{2,1,0:T(8,128)S(1)} %copy-done.3, ...), custom_call_target="tpu_custom_call" | custom-call | flops 60000000 | bytes 60000000 | tf_op jit(solution)/shard_map/third/pallas_call | solution.py:532
  56.4 1.2 %all-to-all-done.1.totals = f32[12,2,128]{2,1,0:T(2,128)} async-done(((f32[12,2,128]{2,1,0:T(2,128)}), f32[12,2,128]{2,1,0:T(2,128)}, u32[]{:S(2)}, u32[]{:S(2)}) %all-to-all-start.1) | async-done | bytes 12320 | tf_op jit(solution)/shard_map/all_to_all | solution.py:564
  57.5 3.0 %fourth.1 = f32[6,3,16,128]{3,2,1,0:T(8,128)} custom-call(f32[12,2,128]{2,1,0:T(2,128)} %all-to-all-done.1.totals, f32[2,21,32,128]{3,2,1,0:T(8,128)S(1)} %get-tuple-element.30.fields, f32[2,9,32,128]{3,2,1,0:T(8,128)S(1)} %get-tuple-element.31.force, f32[2,12,32,128]{3,2,1,0:T(8,128)S(1)} %get-tuple-element.32.push, ...), custom_call_target="tpu_custom_call" | custom-call | flops 8000000 | bytes 8000000 | tf_op jit(solution)/shard_map/fourth/pallas_call | solution.py:532
  (6 shorter events, 0.0 us)
Async XLA Ops:
  1.3 18.0 %copy-start = (f32[9,16,128]{2,1,0:T(8,128)}, f32[9,16,128]{2,1,0:T(8,128)S(1)}, u32[]{:S(2)}) copy-start(f32[9,16,128]{2,1,0:T(8,128)S(1)} %get-tuple-element.26.forcing) | copy-start | bytes 221188
  1.3 18.0 %copy-start.2 = (s32[3,16,128]{2,1,0:T(8,128)}, s32[3,16,128]{2,1,0:T(8,128)S(1)}, u32[]{:S(2)}) copy-start(s32[3,16,128]{2,1,0:T(8,128)S(1)} %get-tuple-element.24.switch) | copy-start | bytes 73732
  4.1 15.2 %collective-permute-start = (f32[66,8,128]{2,1,0:T(8,128)S(1)}, f32[66,8,128]{2,1,0:T(8,128)S(1)}, u32[]{:S(2)}, u32[]{:S(2)}) collective-permute-start(f32[66,8,128]{2,1,0:T(8,128)S(1)} %get-tuple-element.27), channel_id=1, source_target_pairs={{64,128},{128,64},{192,256},{256,192},{320,384},{384,320},{448,512... | collective-permute-start | bytes 811016 | tf_op jit(solution)/shard_map/ppermute | solution.py:602
  14.4 23.7 %all-to-all-start = ((f32[32,2,128]{2,1,0:T(2,128)}), f32[32,2,128]{2,1,0:T(2,128)S(1)}, u32[]{:S(2)}, u32[]{:S(2)}) async-start(f32[32,2,128]{2,1,0:T(2,128)} %spread.2), calls=%async_computation | async-start | bytes 65536 | tf_op jit(solution)/shard_map/all_to_all | solution.py:564
  19.7 18.4 %collective-permute-start.1 = (f32[64,128]{1,0:T(8,128)S(1)}, f32[64,128]{1,0:T(8,128)S(1)}, u32[]{:S(2)}, u32[]{:S(2)}) collective-permute-start(f32[64,128]{1,0:T(8,128)S(1)} %get-tuple-element.28), channel_id=1, source_target_pairs={{0,1},{1,0},{2,3},{3,2},{4,5},{5,4},{6,7},{7,6},{8,9},{9,8},{10,11... | collective-permute-start | bytes 98312 | tf_op jit(solution)/shard_map/ppermute | solution.py:611
  22.4 26.4 %collective-permute-start.2 = (f32[64,128]{1,0:T(8,128)S(1)}, f32[64,128]{1,0:T(8,128)S(1)}, u32[]{:S(2)}, u32[]{:S(2)}) collective-permute-start(f32[64,128]{1,0:T(8,128)S(1)} %get-tuple-element.29), channel_id=1, source_target_pairs={{1,2},{2,1},{3,4},{4,3},{5,6},{6,5},{7,8},{8,7},{9,10},{10,9},{11,... | collective-permute-start | bytes 98312 | tf_op jit(solution)/shard_map/ppermute | solution.py:612
  38.8 18.8 %all-to-all-start.1 = ((f32[12,2,128]{2,1,0:T(2,128)}), f32[12,2,128]{2,1,0:T(2,128)}, u32[]{:S(2)}, u32[]{:S(2)}) async-start(f32[12,2,128]{2,1,0:T(2,128)} %spread.3), calls=%async_computation.1 | async-start | bytes 24576 | tf_op jit(solution)/shard_map/all_to_all | solution.py:564
  48.7 0.6 copy-start.4
  49.3 0.9 %copy-start.1 = (f32[9,16,128]{2,1,0:T(8,128)S(1)}, f32[9,16,128]{2,1,0:T(8,128)}, u32[]{:S(2)}) copy-start(f32[9,16,128]{2,1,0:T(8,128)} %copy-done) | copy-start | bytes 221188
  50.2 0.7 %copy-start.3 = (s32[3,16,128]{2,1,0:T(8,128)S(1)}, s32[3,16,128]{2,1,0:T(8,128)}, u32[]{:S(2)}) copy-start(s32[3,16,128]{2,1,0:T(8,128)} %copy-done.2) | copy-start | bytes 73732
  50.9 0.8 %copy-start.5 = (f32[64,128]{1,0:T(8,128)S(1)}, f32[64,128]{1,0:T(8,128)}, u32[]{:S(2)}) copy-start(f32[64,128]{1,0:T(8,128)} %copy-done.4) | copy-start | bytes 98308

commit v11 on v8

--- a/solution.py
+++ b/solution.py
@@ -589,10 +589,10 @@
         name="first",
     )(*(pltpu.with_memory_space_constraint(values, pltpu.HBM) for values in inputs))
     pair_in = lax.all_gather(pair_out, "core")
+    odd_out, pair_in = lax.optimization_barrier((odd_out, pair_in))
+    odd_in = lax.ppermute(odd_out, GX, pairs(count_x, 1))
     rows = pair_in[:, X_TILES, 0:2]
     spread = spread_over(rows, rows, ("y", "x"))
-    odd_out, spread = lax.optimization_barrier((odd_out, spread))
-    odd_in = lax.ppermute(odd_out, GX, pairs(count_x, 1))
     totals = exchanged(spread, ("y", "x"))
     strips = call(
         second_kernel,

time: 59.4 us -> 59.4 us (level)
  waiting for transfers between devices: 5.06 us -> 4.43 us
  starting transfers between devices: 41.9 us -> 42.5 us
    ppermute x1, waiting for transfers between devices: 1 us -> 0.36 us  [local(): odd_in = lax.ppermute(odd_out, GX, pairs(count_x, 1))]
    ppermute x1, starting transfers between devices: 2.6 us -> 3.23 us  [local(): even_in = lax.ppermute(strips[0], GY, pairs(count_y, 0))]
  transfers between devices with their start and end apart: 5 -> 5, of which waited for: 2 -> 2; matrix products, arithmetic and copies ran while one was open for 0% -> 0% of each run, Pallas kernels for 10% -> 11%
where the time goes in v11:
time: 59.4 us; the launch traced here: 59.1 us
  starting transfers between devices  42.5 us (72%)
  Pallas kernels  9.93 us (17%)
  waiting for transfers between devices  4.43 us (7%)
  blocking collectives  2.2 us (4%)
    ppermute x1, starting transfers between devices, local(): odd_y_in = lax.ppermute(strips[1], GY, pairs(count_y, 1))  15.8 us
    all_to_all x2, starting transfers between devices, exchanged(): return lax.all_to_all(spread, axes, 0, 0, tiled=True)  13.2 us
    ppermute x1, starting transfers between devices, local(): odd_in = lax.ppermute(odd_out, GX, pairs(count_x, 1))  10.3 us
    pallas_call x3, Pallas kernels, call(): pl.pallas_call(kernel, out_shape=outs, in_specs=vmem_specs(len(arrays)),...  7.4 us
    all_to_all x2, waiting for transfers between devices, exchanged(): return lax.all_to_all(spread, axes, 0, 0, tiled=True)  4.06 us
    ppermute x1, starting transfers between devices, local(): even_in = lax.ppermute(strips[0], GY, pairs(count_y, 0))  3.23 us
    all_gather x1, blocking collectives, local(): pair_in = lax.all_gather(pair_out, 'core')  2.2 us
    pallas_call x1, Pallas kernels, local(): pl.pallas_call(first_kernel, out_shape=(shape(X_TILES + 1, *tile), shape(...  1.27 us
  transfers between devices with their start and end apart: 5, of which 2 were waited for; matrix products, arithmetic and copies ran while one was open for 0% of the time, Pallas kernels for 11%

profile of v11, /device:TPU:64, one launch (start us, length us, event | category | flops | bytes accessed | tf_op | source)
XLA Modules:
  0.0 59.1 jit_solution(10992734510481181840)
XLA Ops:
  0.0 1.3 %first.1 = (f32[67,8,128]{2,1,0:T(8,128)S(1)}, f32[66,8,128]{2,1,0:T(8,128)S(1)}, f32[18,16,128]{2,1,0:T(8,128)S(1)}, s32[3,16,128]{2,1,0:T(8,128)S(1)}, f32[36,...) custom-call(f32[18,16,128]{2,1,0:T(8,128)} %bitcast.10, s32[3,16,128]{2,1,0:T(8,128)} %switch_in.1, ...), custom_call_target="tpu_custom_call" | custom-call | tf_op jit(solution)/shard_map/first/pallas_call | solution.py:576
  1.3 2.2 %all-gather = f32[134,8,128]{2,1,0:T(8,128)S(1)} all-gather(f32[67,8,128]{2,1,0:T(8,128)S(1)} %get-tuple-element.20), channel_id=2, replica_groups=mesh['zl'=6,'core'=2,'y'=8,'zh'=2,'x'=4] {'core'}, dimensions={0}, use_global_device_ids=true | all-gather | bytes 823296 | tf_op jit(solution)/shard_map/all_gather | solution.py:591
  3.5 10.3 %collective-permute-start = (f32[66,8,128]{2,1,0:T(8,128)S(1)}, f32[66,8,128]{2,1,0:T(8,128)S(1)}, u32[]{:S(2)}, u32[]{:S(2)}) collective-permute-start(f32[66,8,128]{2,1,0:T(8,128)S(1)} %get-tuple-element.26), channel_id=1, source_target_pairs={{64,128},{128,64},{192,256},{256,192},{320,384},{384,320},{448,512... | collective-permute-start | bytes 811016 | tf_op jit(solution)/shard_map/ppermute | solution.py:593
  13.8 0.6 %spread.2 = f32[32,2,128]{2,1,0:T(2,128)} custom-call(f32[2,2,128]{2,1,0:T(2,128)S(1)} %slice_bitcast_fusion.rows.after, f32[2,2,128]{2,1,0:T(2,128)S(1)} %slice_bitcast_fusion.rows.after), custom_call_target="tpu_custom_call" | custom-call | tf_op jit(solution)/shard_map/spread/pallas_call | solution.py:546
  14.4 3.9 %all-to-all-start = ((f32[32,2,128]{2,1,0:T(2,128)}), f32[32,2,128]{2,1,0:T(2,128)S(1)}, u32[]{:S(2)}, u32[]{:S(2)}) async-start(f32[32,2,128]{2,1,0:T(2,128)} %spread.2), calls=%async_computation | async-start | bytes 65536 | tf_op jit(solution)/shard_map/all_to_all | solution.py:557
  18.3 0.4 collective-permute-done.odd_in
  18.7 0.4 second.1
  19.1 3.2 %collective-permute-start.1 = (f32[64,128]{1,0:T(8,128)S(1)}, f32[64,128]{1,0:T(8,128)S(1)}, u32[]{:S(2)}, u32[]{:S(2)}) collective-permute-start(f32[64,128]{1,0:T(8,128)S(1)} %get-tuple-element.27), channel_id=1, source_target_pairs={{0,1},{1,0},{2,3},{3,2},{4,5},{5,4},{6,7},{7,6},{8,9},{9,8},{10,11... | collective-permute-start | bytes 98312 | tf_op jit(solution)/shard_map/ppermute | solution.py:604
  22.3 15.8 %collective-permute-start.2 = (f32[64,128]{1,0:T(8,128)S(1)}, f32[64,128]{1,0:T(8,128)S(1)}, u32[]{:S(2)}, u32[]{:S(2)}) collective-permute-start(f32[64,128]{1,0:T(8,128)S(1)} %get-tuple-element.28), channel_id=1, source_target_pairs={{1,2},{2,1},{3,4},{4,3},{5,6},{6,5},{7,8},{8,7},{9,10},{10,9},{11,... | collective-permute-start | bytes 98312 | tf_op jit(solution)/shard_map/ppermute | solution.py:605
  38.1 0.0 all-to-all-done.rows
  38.1 0.0 collective-permute-done.1.after.even_in
  38.1 0.6 %spread.3 = f32[12,2,128]{2,1,0:T(2,128)} custom-call(f32[32,2,128]{2,1,0:T(2,128)S(1)} %all-to-all-done.rows, f32[64,128]{1,0:T(8,128)S(1)} %collective-permute-done.1.after.even_in), custom_call_target="tpu_custom_call" | custom-call | tf_op jit(solution)/shard_map/spread/pallas_call | solution.py:546
  38.8 9.3 %all-to-all-start.1 = ((f32[12,2,128]{2,1,0:T(2,128)}), f32[12,2,128]{2,1,0:T(2,128)S(1)}, u32[]{:S(2)}, u32[]{:S(2)}) async-start(f32[12,2,128]{2,1,0:T(2,128)} %spread.3), calls=%async_computation.1 | async-start | bytes 24576 | tf_op jit(solution)/shard_map/all_to_all | solution.py:557
  48.1 0.0 collective-permute-done.2.odd_y_in
  48.1 4.7 %third.1 = (f32[2,21,32,128]{3,2,1,0:T(8,128)S(1)}, f32[2,9,32,128]{3,2,1,0:T(8,128)S(1)}, f32[2,18,32,128]{3,2,1,0:T(8,128)S(1)}, f32[6,6,16,128]{3,2,1,0:T(8,128)S(1)}) custom-call(f32[18,16,128]{2,1,0:T(8,128)S(1)} %get-tuple-element.22.state, s32[3,16,128]{2,1,0:T(8,128)S(1)} %get-tuple-element.23.switch, f32[36,16,128]{2,1,0:T(8,128)S(1)} %get-tuple-element.24.edges, ...), custom_call_target="tpu_custom_call" | custom-call | flops 60000000 | bytes 60000000 | tf_op jit(solution)/shard_map/third/pallas_call | solution.py:525
  52.8 4.1 %all-to-all-done.1.totals = f32[12,2,128]{2,1,0:T(2,128)S(1)} async-done(((f32[12,2,128]{2,1,0:T(2,128)}), f32[12,2,128]{2,1,0:T(2,128)S(1)}, u32[]{:S(2)}, u32[]{:S(2)}) %all-to-all-start.1) | async-done | bytes 12320 | tf_op jit(solution)/shard_map/all_to_all | solution.py:557
  56.8 2.3 %fourth.1 = f32[6,3,16,128]{3,2,1,0:T(8,128)} custom-call(f32[12,2,128]{2,1,0:T(2,128)S(1)} %all-to-all-done.1.totals, f32[2,21,32,128]{3,2,1,0:T(8,128)S(1)} %get-tuple-element.29.fields, f32[2,9,32,128]{3,2,1,0:T(8,128)S(1)} %get-tuple-element.30.force, f32[2,18,32,128]{3,2,1,0:T(8,128)S(1)} %get-tuple-element.31.tend, ...), custom_call_target="tpu_custom_call" | custom-call | flops 8000000 | bytes 8000000 | tf_op jit(solution)/shard_map/fourth/pallas_call | solution.py:525
  (1 shorter events, 0.0 us)
Async XLA Ops:
  3.5 15.2 %collective-permute-start = (f32[66,8,128]{2,1,0:T(8,128)S(1)}, f32[66,8,128]{2,1,0:T(8,128)S(1)}, u32[]{:S(2)}, u32[]{:S(2)}) collective-permute-start(f32[66,8,128]{2,1,0:T(8,128)S(1)} %get-tuple-element.26), channel_id=1, source_target_pairs={{64,128},{128,64},{192,256},{256,192},{320,384},{384,320},{448,512... | collective-permute-start | bytes 811016 | tf_op jit(solution)/shard_map/ppermute | solution.py:593
  14.4 23.7 %all-to-all-start = ((f32[32,2,128]{2,1,0:T(2,128)}), f32[32,2,128]{2,1,0:T(2,128)S(1)}, u32[]{:S(2)}, u32[]{:S(2)}) async-start(f32[32,2,128]{2,1,0:T(2,128)} %spread.2), calls=%async_computation | async-start | bytes 65536 | tf_op jit(solution)/shard_map/all_to_all | solution.py:557
  19.1 19.0 %collective-permute-start.1 = (f32[64,128]{1,0:T(8,128)S(1)}, f32[64,128]{1,0:T(8,128)S(1)}, u32[]{:S(2)}, u32[]{:S(2)}) collective-permute-start(f32[64,128]{1,0:T(8,128)S(1)} %get-tuple-element.27), channel_id=1, source_target_pairs={{0,1},{1,0},{2,3},{3,2},{4,5},{5,4},{6,7},{7,6},{8,9},{9,8},{10,11... | collective-permute-start | bytes 98312 | tf_op jit(solution)/shard_map/ppermute | solution.py:604
  22.3 25.8 %collective-permute-start.2 = (f32[64,128]{1,0:T(8,128)S(1)}, f32[64,128]{1,0:T(8,128)S(1)}, u32[]{:S(2)}, u32[]{:S(2)}) collective-permute-start(f32[64,128]{1,0:T(8,128)S(1)} %get-tuple-element.28), channel_id=1, source_target_pairs={{1,2},{2,1},{3,4},{4,3},{5,6},{6,5},{7,8},{8,7},{9,10},{10,9},{11,... | collective-permute-start | bytes 98312 | tf_op jit(solution)/shard_map/ppermute | solution.py:605
  38.8 18.1 %all-to-all-start.1 = ((f32[12,2,128]{2,1,0:T(2,128)}), f32[12,2,128]{2,1,0:T(2,128)S(1)}, u32[]{:S(2)}, u32[]{:S(2)}) async-start(f32[12,2,128]{2,1,0:T(2,128)} %spread.3), calls=%async_computation.1 | async-start | bytes 24576 | tf_op jit(solution)/shard_map/all_to_all | solution.py:557
